TPU v7x, 32 devices: a whole 2x2x4 slice. The times are simulated.
32 devices in a mesh: group: 4 (over x, core), dp: 2 (over y), mp: 4 (over z).
Axes of the slice: x: 2, y: 2, z: 4, core: 2. Of those that a mesh axis runs over, the one named last changes fastest.
Arguments:
- patches: float32 [4, 96, 196, 768], P('group', 'dp', None, 'mp'), may hold values from -6 to 6
- labels: int32 [4, 96], P('group', 'dp'), may hold values from 0 to 999
- partner: int32 [4, 96], P('group', 'dp'), may hold values from 0 to 47
- class_weight: float32 [1000], replicated, may hold values from 0.3 to 3
- embedding: float32 [768, 384], P('mp'), may hold values from -0.21875 to 0.21875
- mixing: float32 [1, 196, 197], replicated, may hold values from -0.4375 to 0.4375
- expand: float32 [1, 385, 1536], P(None, None, 'mp'), may hold values from -0.3125 to 0.3125
- shrink: float32 [1, 1536, 384], P(None, 'mp'), may hold values from -0.15625 to 0.15625
- classifier: float32 [385, 1000], P(None, 'mp'), may hold values from -6 to 6
- scales: float32 [5, 384], P(None, 'mp'), may hold values from 0.5 to 1.5
- shifts: float32 [5, 384], P(None, 'mp'), may hold values from -2 to 2
- embedding_first: float32 [4, 768, 384], P('group', 'mp'), may hold values from -1 to 1, as said below
- mixing_first: float32 [4, 1, 196, 197], P('group'), may hold values from -1 to 1, as said below
- expand_first: float32 [4, 1, 385, 1536], P('group', None, None, 'mp'), may hold values from -1 to 1, as said below
- shrink_first: float32 [4, 1, 1536, 384], P('group', None, 'mp'), may hold values from -1 to 1, as said below
- classifier_first: float32 [4, 385, 1000], P('group', None, 'mp'), may hold values from -1 to 1, as said below
- scale_first_moments: float32 [4, 5, 384], P('group', None, 'mp'), may hold values from -1 to 1, as said below
- shifts_first: float32 [4, 5, 384], P('group', None, 'mp'), may hold values from -1 to 1, as said below
- embedding_second: float32 [4, 768, 384], P('group', 'mp'), may hold values from 0 to 1, as said below
- mixing_second: float32 [4, 1, 196, 197], P('group'), may hold values from 0 to 1, as said below
- expand_second: float32 [4, 1, 385, 1536], P('group', None, None, 'mp'), may hold values from 0 to 1, as said below
- shrink_second: float32 [4, 1, 1536, 384], P('group', None, 'mp'), may hold values from 0 to 1, as said below
- classifier_second: float32 [4, 385, 1000], P('group', None, 'mp'), may hold values from 0 to 1, as said below
- scales_second: float32 [4, 5, 384], P('group', None, 'mp'), may hold values from 0 to 1, as said below
- shifts_second: float32 [4, 5, 384], P('group', None, 'mp'), may hold values from 0 to 1, as said below
- embedding_outer: float32 [768, 384], P('mp'), may hold values from -0.12 to 0.12
- mixing_outer: float32 [1, 196, 197], replicated, may hold values from -0.12 to 0.12
- expand_outer: float32 [1, 385, 1536], P(None, None, 'mp'), may hold values from -0.12 to 0.12
- shrink_outer: float32 [1, 1536, 384], P(None, 'mp'), may hold values from -0.12 to 0.12
- classifier_outer: float32 [385, 1000], P(None, 'mp'), may hold values from -0.12 to 0.12
- scales_outer: float32 [5, 384], P(None, 'mp'), may hold values from -0.12 to 0.12
- shifts_outer: float32 [5, 384], P(None, 'mp'), may hold values from -0.12 to 0.12
Outputs:
- losses: float32 [4, 2], P('group')
- grad_norm: float32 [4], P('group')
- embedding_update: float32 [768, 384], P('mp')
- mixing_update: float32 [1, 196, 197], replicated
- expand_update: float32 [1, 385, 1536], P(None, None, 'mp')
- shrink_update: float32 [1, 1536, 384], P(None, 'mp')
- classifier_update: float32 [385, 1000], P(None, 'mp')
- scales_update: float32 [5, 384], P(None, 'mp')
- shifts_update: float32 [5, 384], P(None, 'mp')
- embedding_mean: float32 [4, 768, 384], P('group', 'mp')
- mixing_mean: float32 [4, 1, 196, 197], P('group')
- expand_mean: float32 [4, 1, 385, 1536], P('group', None, None, 'mp')
- shrink_mean: float32 [4, 1, 1536, 384], P('group', None, 'mp')
- classifier_mean: float32 [4, 385, 1000], P('group', None, 'mp')
- scales_mean: float32 [4, 5, 384], P('group', None, 'mp')
- shifts_mean: float32 [4, 5, 384], P('group', None, 'mp')
- embedding_square: float32 [4, 768, 384], P('group', 'mp')
- mixing_square: float32 [4, 1, 196, 197], P('group')
- expand_square: float32 [4, 1, 385, 1536], P('group', None, None, 'mp')
- shrink_square: float32 [4, 1, 1536, 384], P('group', None, 'mp')
- classifier_square: float32 [4, 385, 1000], P('group', None, 'mp')
- scales_square: float32 [4, 5, 384], P('group', None, 'mp')
- shifts_square: float32 [4, 5, 384], P('group', None, 'mp')
- embedding_velocity: float32 [768, 384], P('mp')
- mixing_velocity: float32 [1, 196, 197], replicated
- expand_velocity: float32 [1, 385, 1536], P(None, None, 'mp')
- shrink_velocity: float32 [1, 1536, 384], P(None, 'mp')
- classifier_velocity: float32 [385, 1000], P(None, 'mp')
- scales_velocity: float32 [5, 384], P(None, 'mp')
- shifts_velocity: float32 [5, 384], P(None, 'mp')
Inputs may be any that keep to these rules, and one draw needn't show every extreme that they name: partner names an image of the same aligned block of 48 images, by its place in that block. `embedding_first`: first moments of both signs. `mixing_first`: first moments of both signs. `expand_first`: first moments of both signs. `shrink_first`: first moments of both signs. `classifier_first`: first moments of both signs. `scale_first_moments`: first moments of both signs. `shifts_first`: first moments of both signs. `embedding_second`: positive. `mixing_second`: positive. `expand_second`: positive. `shrink_second`: positive. `classifier_second`: positive. `scales_second`: positive. `shifts_second`: positive.
All inputs are finite; a program needn't handle non-finite values.
Results may differ from a plain program's by a relative error of at most 0.0024.
The roundings to bfloat16 on the way count: a program that leaves them out, or rounds other values in their place, can miss the bound.
Values may be sent and summed in bfloat16 or wider, within the bound.
A program may use at most 256 MiB of HBM per device.

v0:
```python
import jax
import jax.numpy as jnp
from jax import lax
from jax.sharding import PartitionSpec as P

D = 384
PATCH_EDGE = 196
LAYERS = 1
STEP = 10


mix_share = 0.7
clip_limit = 0.01
beta_one = 0.9
beta_two = 0.999
adam_eps = 1e-08
weight_decay = 0.05
matrix_rate = 0.05
head_rate = 0.5
vector_rate = 0.4
outer_rate = 0.7
outer_momentum = 0.9


def product(first_operand, second_operand, left_dims, right_dims):
    return lax.dot_general(
        first_operand,
        second_operand,
        ((left_dims, right_dims), ((), ())),
        preferred_element_type=jnp.float32,
    )


def layer_forward(stream, mixing_layer, expand_layer, shrink_layer, gain_rows, shift_rows):
    width, row_count = stream.shape
    image_count = row_count // PATCH_EDGE
    mixing_block_input = (gain_rows[0][:, None] * stream + shift_rows[0][:, None]).astype(
        jnp.bfloat16
    )
    lookup_table = mixing_layer.astype(jnp.bfloat16)
    mixed_images = product(
        mixing_block_input.reshape(width, image_count, PATCH_EDGE),
        lookup_table[:, :PATCH_EDGE],
        (2,),
        (1,),
    )
    mixed_images = (
        mixed_images + lookup_table[:, PATCH_EDGE].astype(jnp.float32)[None, None, :]
    ).reshape(width, row_count)
    stream_mid = stream + gain_rows[1][:, None] * mixed_images
    ffn_input = (gain_rows[2][:, None] * stream_mid + shift_rows[1][:, None]).astype(jnp.bfloat16)
    ffn_whole = lax.all_gather(ffn_input, "mp", axis=0, tiled=True)
    up_table = expand_layer.astype(jnp.bfloat16)
    hidden = product(up_table[:D], ffn_whole, (0,), (0,)) + up_table[D].astype(jnp.float32)[:, None]
    active = jax.nn.gelu(hidden).astype(jnp.bfloat16)
    down_table = shrink_layer.astype(jnp.bfloat16)
    output = lax.psum_scatter(
        product(down_table, active, (0,), (0,)), "mp", scatter_dimension=0, tiled=True
    )
    stream_out = stream_mid + gain_rows[3][:, None] * (output + shift_rows[2][:, None])
    return (
        stream_out,
        (stream, mixing_block_input, mixed_images, stream_mid, ffn_whole, hidden, active, output),
    )


def layer_backward(
    d_stream, saved, mixing_layer, expand_layer, shrink_layer, gain_rows, shift_rows
):
    stream, mixing_block_input, mixed_images, stream_mid, ffn_whole, hidden, active, output = saved
    width, row_count = stream.shape
    image_count = row_count // PATCH_EDGE
    lookup_table = mixing_layer.astype(jnp.bfloat16)
    up_table = expand_layer.astype(jnp.bfloat16)
    down_table = shrink_layer.astype(jnp.bfloat16)
    d_output = gain_rows[3][:, None] * d_stream
    grad_scale_two = jnp.sum((output + shift_rows[2][:, None]) * d_stream, axis=1)
    grad_bias_two = jnp.sum(d_output, axis=1)
    d_output_low = d_output.astype(jnp.bfloat16)
    output_whole = lax.all_gather(d_output_low, "mp", axis=0, tiled=True)
    d_active = product(down_table, output_whole, (1,), (0,))
    grad_shrink = product(active, output_whole, (1,), (1,))
    unused, gelu_pull = jax.vjp(jax.nn.gelu, hidden)
    (d_hidden,) = gelu_pull(d_active)
    d_hidden = d_hidden.astype(jnp.bfloat16)
    grad_expand = jnp.concatenate(
        [
            product(ffn_whole, d_hidden, (1,), (1,)),
            jnp.sum(d_hidden.astype(jnp.float32), axis=1)[None, :],
        ],
        axis=0,
    )
    d_ffn = lax.psum_scatter(
        product(
            lax.slice_in_dim(up_table, 0, width * lax.axis_size("mp"), axis=0), d_hidden, (1,), (0,)
        ),
        "mp",
        scatter_dimension=0,
        tiled=True,
    )
    grad_aff_two = jnp.sum(d_ffn * stream_mid, axis=1)
    grad_shift_two = jnp.sum(d_ffn, axis=1)
    d_mid = d_stream + gain_rows[2][:, None] * d_ffn
    grad_scale_one = jnp.sum(mixed_images * d_mid, axis=1)
    d_mixed = (
        (gain_rows[1][:, None] * d_mid).astype(jnp.bfloat16).reshape(width, image_count, PATCH_EDGE)
    )
    mixer_blocks = mixing_block_input.reshape(width, image_count, PATCH_EDGE)
    grad_mixing = jnp.concatenate(
        [
            product(d_mixed, mixer_blocks, (0, 1), (0, 1)),
            jnp.sum(d_mixed.astype(jnp.float32), axis=(0, 1))[:, None],
        ],
        axis=1,
    )
    d_mixer = product(d_mixed, lookup_table[:, :PATCH_EDGE], (2,), (0,)).reshape(width, row_count)
    grad_aff_one = jnp.sum(d_mixer * stream, axis=1)
    grad_shift_one = jnp.sum(d_mixer, axis=1)
    d_below = d_mid + gain_rows[0][:, None] * d_mixer
    gain_grads = jnp.stack([grad_aff_one, grad_scale_one, grad_aff_two, grad_scale_two])
    shift_grads = jnp.stack([grad_shift_one, grad_shift_two, grad_bias_two])
    return (d_below, (grad_mixing, grad_expand, grad_shrink, gain_grads, shift_grads))


def adamw(weight, gradient, moment_one, moment_two, step_rate):
    mean_new = beta_one * moment_one + (1.0 - beta_one) * gradient
    square_new = beta_two * moment_two + (1.0 - beta_two) * gradient * gradient
    mean_hat = mean_new / (1.0 - beta_one**STEP)
    square_hat = square_new / (1.0 - beta_two**STEP)
    inner = weight - step_rate * (
        mean_hat / (jnp.sqrt(square_hat) + adam_eps) + weight_decay * weight
    )
    return (inner, mean_new, square_new)


def per_device(
    patches,
    labels,
    partner,
    class_weight,
    embedding,
    mixing,
    expand,
    shrink,
    classifier,
    scales,
    shifts,
    embedding_first,
    mixing_first,
    expand_first,
    shrink_first,
    classifier_first,
    scale_first_moments,
    shifts_first,
    embedding_second,
    mixing_second,
    expand_second,
    shrink_second,
    classifier_second,
    scales_second,
    shifts_second,
    embedding_outer,
    mixing_outer,
    expand_outer,
    shrink_outer,
    classifier_outer,
    scales_outer,
    shifts_outer,
):
    images = patches[0]
    own_labels = labels[0]
    pair_index = partner[0]
    mate_labels = own_labels[pair_index]
    blended = (mix_share * images + (1.0 - mix_share) * images[pair_index]).astype(jnp.bfloat16)
    pixel_rows = blended.reshape(blended.shape[0] * PATCH_EDGE, blended.shape[2])
    work = (embedding, expand, shrink, classifier, scales, shifts)
    work_embedding, work_expand, work_shrink, work_classifier, work_scales, work_shifts = work
    image_count = pixel_rows.shape[0] // PATCH_EDGE
    width = work_scales.shape[1]
    embed_table = work_embedding.astype(jnp.bfloat16)
    embedded = lax.psum_scatter(
        product(embed_table, pixel_rows, (0,), (1,)), "mp", scatter_dimension=0, tiled=True
    )
    stream = embedded + work_shifts[3 * LAYERS][:, None]
    layer_index = 0
    stream, saved = layer_forward(
        stream,
        mixing[layer_index],
        work_expand[layer_index],
        work_shrink[layer_index],
        work_scales[4 * layer_index : 4 * layer_index + 4],
        work_shifts[3 * layer_index : 3 * layer_index + 3],
    )
    saved_layers = [saved]
    final = work_scales[4 * LAYERS][:, None] * stream + work_shifts[3 * LAYERS + 1][:, None]
    pooled = jnp.mean(final.reshape(width, image_count, PATCH_EDGE), axis=2).astype(jnp.bfloat16)
    pooled_whole = lax.all_gather(pooled, "mp", axis=0, tiled=True)
    head_full = lax.all_gather(classifier.astype(jnp.bfloat16), "mp", axis=1, tiled=True)
    column_start = lax.axis_index("mp") * classifier.shape[1]
    feature_start = lax.axis_index("mp") * width
    share = jnp.where(lax.axis_index("mp") == 0, 1.0, 0.0).astype(jnp.float32)
    column_count = work_classifier.shape[1]
    logits = (
        product(pooled_whole, head_full[:D], (0,), (0,)) + head_full[D].astype(jnp.float32)[None, :]
    )
    maximum = jnp.max(logits, axis=1)
    all_classes = jnp.arange(class_weight.shape[0], dtype=jnp.int32)
    label_hot = (own_labels[:, None] == all_classes[None, :]).astype(jnp.float32)
    mate_hot = (mate_labels[:, None] == all_classes[None, :]).astype(jnp.float32)
    first_mix_weight = mix_share * jnp.sum(label_hot * class_weight[None, :], axis=1)
    weight_b = (1.0 - mix_share) * jnp.sum(mate_hot * class_weight[None, :], axis=1)
    exps = jnp.exp(logits - maximum[:, None])
    exp_sums = jnp.sum(exps, axis=1)
    log_total = maximum + jnp.log(exp_sums)
    target_a = jnp.sum(label_hot * logits, axis=1)
    target_b = jnp.sum(mate_hot * logits, axis=1)
    loss_local = jnp.sum(
        first_mix_weight * (log_total - target_a) + weight_b * (log_total - target_b)
    )
    weight_local = jnp.sum(first_mix_weight + weight_b)
    softmax = exps / exp_sums[:, None]
    d_logits = (
        (first_mix_weight + weight_b)[:, None] * softmax
        - first_mix_weight[:, None] * label_hot
        - weight_b[:, None] * mate_hot
    ).astype(jnp.bfloat16)
    own_columns = lax.dynamic_slice_in_dim(d_logits, column_start, column_count, 1)
    grad_classifier = jnp.concatenate(
        [
            product(pooled_whole, own_columns, (1,), (0,)),
            jnp.sum(own_columns.astype(jnp.float32), axis=0)[None, :],
        ],
        axis=0,
    )
    head_rows = lax.dynamic_slice_in_dim(head_full[:D], feature_start, width, 0)
    d_pooled = product(head_rows, d_logits, (1,), (1,))
    d_final = jnp.broadcast_to(
        (d_pooled / PATCH_EDGE)[:, :, None], (width, image_count, PATCH_EDGE)
    ).reshape(width, image_count * PATCH_EDGE)
    grad_final_scale = jnp.sum(d_final * stream, axis=1)
    grad_final_shift = jnp.sum(d_final, axis=1)
    d_stream = work_scales[4 * LAYERS][:, None] * d_final
    layer_grads = [None] * LAYERS
    for layer_index in reversed(range(LAYERS)):
        d_stream, layer_grads[layer_index] = layer_backward(
            d_stream,
            saved_layers[layer_index],
            mixing[layer_index],
            work_expand[layer_index],
            work_shrink[layer_index],
            work_scales[4 * layer_index : 4 * layer_index + 4],
            work_shifts[3 * layer_index : 3 * layer_index + 3],
        )
    grad_embed_shift = jnp.sum(d_stream, axis=1)
    d_stream_low = d_stream.astype(jnp.bfloat16)
    grad_embedding = product(
        pixel_rows, lax.all_gather(d_stream_low, "mp", axis=0, tiled=True), (0,), (1,)
    )
    grad_mixing = jnp.stack([entry[0] for entry in layer_grads])
    grad_expand = jnp.stack([entry[1] for entry in layer_grads])
    grad_shrink = jnp.stack([entry[2] for entry in layer_grads])
    grad_scales = jnp.concatenate(
        [entry[3] for entry in layer_grads] + [grad_final_scale[None, :]], axis=0
    )
    grad_shifts = jnp.concatenate(
        [entry[4] for entry in layer_grads]
        + [grad_embed_shift[None, :], grad_final_shift[None, :]],
        axis=0,
    )
    summed = lax.psum(
        (
            grad_embedding,
            grad_mixing,
            grad_expand,
            grad_shrink,
            grad_classifier,
            grad_scales,
            grad_shifts,
            loss_local,
            weight_local,
        ),
        "dp",
    )
    square_rest = sum((jnp.sum(summed[index] * summed[index]) for index in (0, 2, 3, 4, 5, 6)))
    square_total, mixing_whole, loss_sum, weight_total = lax.psum(
        (square_rest, summed[1], summed[7] * share, summed[8] * share), "mp"
    )
    grad_size = jnp.sqrt(square_total + jnp.sum(mixing_whole * mixing_whole)) / weight_total
    factor = clip_limit / jnp.maximum(grad_size, clip_limit)
    gradients = (
        summed[0] / weight_total,
        mixing_whole / weight_total,
        summed[2] / weight_total,
        summed[3] / weight_total,
        summed[4] / weight_total,
        summed[5] / weight_total,
        summed[6] / weight_total,
    )
    weights = (embedding, mixing, expand, shrink, classifier, scales, shifts)
    firsts = (
        embedding_first,
        mixing_first,
        expand_first,
        shrink_first,
        classifier_first,
        scale_first_moments,
        shifts_first,
    )
    seconds = (
        embedding_second,
        mixing_second,
        expand_second,
        shrink_second,
        classifier_second,
        scales_second,
        shifts_second,
    )
    outers = (
        embedding_outer,
        mixing_outer,
        expand_outer,
        shrink_outer,
        classifier_outer,
        scales_outer,
        shifts_outer,
    )
    step_rates = (matrix_rate,) * 4 + (head_rate,) + (vector_rate,) * 2
    means = []
    squares = []
    moved = []
    for member in range(7):
        inner, mean_new, square_new = adamw(
            weights[member],
            factor * gradients[member],
            firsts[member][0],
            seconds[member][0],
            step_rates[member],
        )
        moved.append(weights[member] - inner)
        means.append(mean_new[None])
        squares.append(square_new[None])
    group_sums = lax.psum(
        (moved[0], moved[1], moved[2], moved[3], moved[4], moved[5], moved[6]), "group"
    )
    groups = lax.axis_size("group")
    updates = []
    velocities = []
    for member in range(7):
        average = group_sums[member] / groups
        velocity = outer_momentum * outers[member] + average
        velocities.append(velocity)
        updates.append(weights[member] - outer_rate * (average + outer_momentum * velocity))
    losses = jnp.stack([loss_sum, weight_total])[None, :]
    return (
        losses,
        grad_size[None],
        updates[0],
        updates[1],
        updates[2],
        updates[3],
        updates[4],
        updates[5],
        updates[6],
        means[0],
        means[1],
        means[2],
        means[3],
        means[4],
        means[5],
        means[6],
        squares[0],
        squares[1],
        squares[2],
        squares[3],
        squares[4],
        squares[5],
        squares[6],
        velocities[0],
        velocities[1],
        velocities[2],
        velocities[3],
        velocities[4],
        velocities[5],
        velocities[6],
    )


def solution(mesh):
    return jax.shard_map(
        per_device,
        mesh=mesh,
        in_specs=(
            P("group", "dp", None, "mp"),
            P("group", "dp"),
            P("group", "dp"),
            P(),
            P("mp", None),
            P(),
            P(None, None, "mp"),
            P(None, "mp", None),
            P(None, "mp"),
            P(None, "mp"),
            P(None, "mp"),
            P("group", "mp", None),
            P("group", None, None, None),
            P("group", None, None, "mp"),
            P("group", None, "mp", None),
            P("group", None, "mp"),
            P("group", None, "mp"),
            P("group", None, "mp"),
            P("group", "mp", None),
            P("group", None, None, None),
            P("group", None, None, "mp"),
            P("group", None, "mp", None),
            P("group", None, "mp"),
            P("group", None, "mp"),
            P("group", None, "mp"),
            P("mp", None),
            P(),
            P(None, None, "mp"),
            P(None, "mp", None),
            P(None, "mp"),
            P(None, "mp"),
            P(None, "mp"),
        ),
        out_specs=(
            P("group", None),
            P("group"),
            P("mp", None),
            P(),
            P(None, None, "mp"),
            P(None, "mp", None),
            P(None, "mp"),
            P(None, "mp"),
            P(None, "mp"),
            P("group", "mp", None),
            P("group", None, None, None),
            P("group", None, None, "mp"),
            P("group", None, "mp", None),
            P("group", None, "mp"),
            P("group", None, "mp"),
            P("group", None, "mp"),
            P("group", "mp", None),
            P("group", None, None, None),
            P("group", None, None, "mp"),
            P("group", None, "mp", None),
            P("group", None, "mp"),
            P("group", None, "mp"),
            P("group", None, "mp"),
            P("mp", None),
            P(),
            P(None, None, "mp"),
            P(None, "mp", None),
            P(None, "mp"),
            P(None, "mp"),
            P(None, "mp"),
        ),
        check_vma=False,
    )
```

profile of v0, /device:TPU:0, one launch (start us, length us, event | category | flops | bytes accessed | tf_op | source)
XLA Modules:
  0.0 1635.4 jit_solution(13154122029919363356)
XLA Ops:
  7.9 8.8 broadcast_multiply_fusion.1
  16.7 8.5 gather_fusion
  25.2 4.9 broadcast_multiply_fusion
  30.0 9.1 copy.203
  39.2 10.0 mul.705
  49.2 12.8 copy.202
  62.0 9.8 mul.702
  71.8 5.8 add_convert_fusion
  79.5 6.6 convolution_bitcast_fusion
  86.1 15.4 copy.248
  103.2 244.7 %reduce-scatter.10.cloned.1.call-done = f32[96,9408]{1,0:T(8,128)} async-done(((f32[384,9408]{1,0:T(8,128)}), f32[96,9408]{1,0:T(8,128)}) %reduce-scatter.10.cloned.1.call-update) | async-done | bytes 3612688 | tf_op jit(solution)/shard_map/reduce_scatter | solution.py:181
  348.0 3.8 add_convert_fusion.2
  351.8 8.5 reshape.273
  363.2 6.1 reshape.274
  369.4 6.4 add_convert_fusion.1
  377.0 131.5 %all-gather.6.cloned.1.call-done = bf16[384,9408]{1,0:T(8,128)(2,1)} async-done(((bf16[96,9408]{1,0:T(8,128)(2,1)}), bf16[384,9408]{1,0:T(8,128)(2,1)}) %all-gather.6.cloned.1.call-update) | async-done | bytes 7225360 | tf_op jit(solution)/shard_map/all_gather | solution.py:52
  508.5 7.0 convolution_add_fusion
  515.5 5.1 copy-done.1
  520.6 8.7 convolution_bitcast_fusion.3
  529.3 15.4 copy.250
  546.3 29.5 %all-gather.1 = bf16[4,250,385]{1,2,0:T(8,128)(2,1)S(1)} all-gather(bf16[1,250,385]{1,2,0:T(8,128)(2,1)S(1)} %convert_bitcast_fusion), channel_id=1, replica_groups=mesh['group'=4,'dp'=2,'mp'=4] {'mp'}, dimensions={0}, use_global_device_ids=true | all-gather | bytes 962500 | tf_op jit(solution)/shard_map/all_gather | solution.py:198
  580.4 217.7 %reduce-scatter.12.cloned.1.call-done = f32[96,9408]{1,0:T(8,128)} async-done(((f32[384,9408]{1,0:T(8,128)}), f32[96,9408]{1,0:T(8,128)}) %reduce-scatter.12.cloned.1.call-update) | async-done | bytes 3612688 | tf_op jit(solution)/shard_map/reduce_scatter | solution.py:57
  798.1 5.6 multiply_add_fusion.2
  803.7 9.3 reshape.275
  816.2 14.0 all-gather
  836.2 6.2 reshape.276
  842.3 3.7 multiply_convert_fusion.1
  846.1 131.4 %all-gather.8.cloned.1.call-done = bf16[384,9408]{1,0:T(8,128)(2,1)} async-done(((bf16[96,9408]{1,0:T(8,128)(2,1)}), bf16[384,9408]{1,0:T(8,128)(2,1)}) %all-gather.8.cloned.1.call-update) | async-done | bytes 7225360 | tf_op jit(solution)/shard_map/all_gather | solution.py:80
  977.6 18.9 %convert_reduce_fusion = (f32[384]{0:T(512)S(1)}, bf16[384,9408]{0,1:T(8,128)(2,1)S(1)}) fusion(f32[9408,384]{1,0:T(8,128)} %copy-done.1, bf16[384,9408]{1,0:T(8,128)(2,1)} %all-gather.8.cloned.1.call-done, f32[1,384,384]{2,1,0:T(8,128)S(1)} %copy-done.13), kind=kOutput, calls=%fused_computation.20 | convolution fusion | flops 2854157824 | bytes 29492736 | tf_op jit(solution)/shard_map/dot_general | solution.py:26
  999.5 8.9 convolution_bitcast_fusion.1
  1008.4 15.4 copy.252
  1023.9 241.9 %reduce-scatter.14.cloned.1.call-done = f32[96,9408]{1,0:T(8,128)} async-done(((f32[384,9408]{1,0:T(8,128)}), f32[96,9408]{1,0:T(8,128)}) %reduce-scatter.14.cloned.1.call-update) | async-done | bytes 3612688 | tf_op jit(solution)/shard_map/reduce_scatter | solution.py:93
  1265.8 8.8 fusion.61
  1274.5 9.2 reshape.277
  1283.7 5.3 fusion.65
  1289.1 6.1 reshape.278
  1295.2 7.8 fusion.13
  1304.3 8.5 fusion.67
  1313.7 13.3 convolution_bitcast_fusion.4
  1330.7 105.1 %all-gather.10.cloned.1.call-done = bf16[384,9408]{1,0:T(8,128)(2,1)} async-done(((bf16[96,9408]{1,0:T(8,128)(2,1)}), bf16[384,9408]{1,0:T(8,128)(2,1)}) %all-gather.10.cloned.1.call-update) | async-done | bytes 7225360 | tf_op jit(solution)/shard_map/all_gather | solution.py:257
  1435.7 7.4 fusion.66
  1449.6 5.9 all-reduce.3
  1458.1 47.3 %all-reduce.13.cloned.1.call-done = (f32[192,384]{1,0:T(8,128)}, f32[1,385,384]{2,1,0:T(8,128)}, f32[1,384,384]{2,1,0:T(8,128)}, f32[385,250]{1,0:T(8,128)}, f32[1,196,197]{1,2,0:T(8,128)}) async-done(((f32[192,384]{1,0:T(8,128)}, f32[1,385,384]{2,1,0:T(8,128)}, f32[1,384,384]{2,1,0:T(8,128)}, f32[385,250]{1,0:T(8,128)}, f32[1,196,197]{1,2,0:T(8,128)}), (f32[192,384]{1,0:T(8,128)}, ...) | async-done | bytes 2015560 | tf_op jit(solution)/shard_map/psum | solution.py:270
  1516.4 12.9 all-reduce
  1529.3 14.8 all-reduce.9.cloned.1.call-done
  1554.2 3.6 fusion.57
  1575.8 6.8 all-reduce.1
  1583.8 30.1 %all-reduce.11.cloned.1.call-done = (f32[192,384]{1,0:T(8,128)}, f32[1,196,197]{1,2,0:T(8,128)}, f32[1,385,384]{2,1,0:T(8,128)}, f32[1,384,384]{2,1,0:T(8,128)}, f32[385,250]{1,0:T(8,128)}) async-done(((f32[192,384]{1,0:T(8,128)}, f32[1,196,197]{1,2,0:T(8,128)}, f32[1,385,384]{2,1,0:T(8,128)}, f32[1,384,384]{2,1,0:T(8,128)}, f32[385,250]{1,0:T(8,128)}), (f32[192,384]{1,0:T(8,128)}, ...) | async-done | bytes 2015560 | tf_op jit(solution)/shard_map/psum | solution.py:342
  (218 shorter events, 87.3 us)
Async XLA Ops:
  7.2 340.8 %reduce-scatter.10.cloned.1.call-start = ((), (), s32[]{:S(2)}) async-start(), calls=%async_computation.7 | async-start | bytes 18186240 | tf_op jit(solution)/shard_map/reduce_scatter | solution.py:181
  101.5 406.9 %all-gather.6.cloned.1.call-start = ((), (), s32[]{:S(2)}) async-start(), calls=%async_computation.3 | async-start | bytes 9093120 | tf_op jit(solution)/shard_map/all_gather | solution.py:52
  102.4 260.8 %copy-start.16 = (bf16[1,196,197]{2,1,0:T(8,128)(2,1)}, bf16[1,196,197]{2,1,0:T(8,128)(2,1)S(1)}, u32[]{:S(2)}) copy-start(bf16[1,196,197]{2,1,0:T(8,128)(2,1)S(1)} %copy.330) | copy-start | bytes 231676
  103.2 260.1 %copy-start.46 = (f32[96]{0:T(128)}, f32[96]{0:T(128)S(1)}, u32[]{:S(2)}) copy-start(f32[96]{0:T(128)S(1)} %get-tuple-element.254) | copy-start | bytes 1156
  103.2 266.2 %copy-start.38 = (f32[96]{0:T(128)}, f32[96]{0:T(128)S(1)}, u32[]{:S(2)}) copy-start(f32[96]{0:T(128)S(1)} %get-tuple-element.242) | copy-start | bytes 1156
  103.2 266.2 %copy-start.42 = (f32[96]{0:T(128)}, f32[96]{0:T(128)S(1)}, u32[]{:S(2)}) copy-start(f32[96]{0:T(128)S(1)} %get-tuple-element.253) | copy-start | bytes 1156
  103.2 266.2 %copy-start.44 = (f32[96]{0:T(128)}, f32[96]{0:T(128)S(1)}, u32[]{:S(2)}) copy-start(f32[96]{0:T(128)S(1)} %get-tuple-element.255) | copy-start | bytes 1156
  103.2 694.9 %copy-start.34 = (f32[96]{0:T(128)}, f32[96]{0:T(128)S(1)}, u32[]{:S(2)}) copy-start(f32[96]{0:T(128)S(1)} %get-tuple-element.256) | copy-start | bytes 1156
  103.2 694.9 %copy-start.36 = (f32[96]{0:T(128)}, f32[96]{0:T(128)S(1)}, u32[]{:S(2)}) copy-start(f32[96]{0:T(128)S(1)} %get-tuple-element.252) | copy-start | bytes 1156
  375.8 422.2 %reduce-scatter.12.cloned.1.call-start = ((), (), s32[]{:S(2)}) async-start(), calls=%async_computation.8 | async-start | bytes 18186240 | tf_op jit(solution)/shard_map/reduce_scatter | solution.py:57
  376.9 138.5 %copy-start.15 = (bf16[1,384,384]{2,0,1:T(2,128)(2,1)}, bf16[1,384,384]{2,0,1:T(2,128)(2,1)S(1)}, u32[]{:S(2)}) copy-start(bf16[1,384,384]{2,0,1:T(2,128)(2,1)S(1)} %slice.95) | copy-start | bytes 884740
  377.0 143.7 %copy-start.12 = (f32[1,384,384]{2,1,0:T(8,128)S(1)}, f32[1,384,384]{2,1,0:T(8,128)}, u32[]{:S(2)}) copy-start(f32[1,384,384]{2,1,0:T(8,128)} %param.39) | copy-start | bytes 1769476
  544.7 253.4 %copy-start.41 = (f32[96]{0:T(128)S(1)}, f32[96]{0:T(128)}, u32[]{:S(2)}) copy-start(f32[96]{0:T(128)} %get-tuple-element.238) | copy-start | bytes 1156
  544.7 253.4 %copy-start.58 = (f32[96]{0:T(128)S(1)}, f32[96]{0:T(128)}, u32[]{:S(2)}) copy-start(f32[96]{0:T(128)} %get-tuple-element.239) | copy-start | bytes 1156
  544.7 432.8 %all-gather.8.cloned.1.call-start = ((), (), s32[]{:S(2)}) async-start(), calls=%async_computation.4 | async-start | bytes 9093120 | tf_op jit(solution)/shard_map/all_gather | solution.py:80
  803.7 27.0 %copy-start.48 = (f32[1000]{0:T(1024)S(1)}, f32[1000]{0:T(1024)}, u32[]{:S(2)}) copy-start(f32[1000]{0:T(1024)} %param.35) | copy-start | bytes 12004
  836.1 141.4 %copy-start.13 = (f32[1,384,384]{2,1,0:T(8,128)S(1)}, f32[1,384,384]{2,1,0:T(8,128)}, u32[]{:S(2)}) copy-start(f32[1,384,384]{2,1,0:T(8,128)} %param.39) | copy-start | bytes 1769476
  846.1 419.7 %reduce-scatter.14.cloned.1.call-start = ((), (), s32[]{:S(2)}) async-start(), calls=%async_computation.9 | async-start | bytes 18186240 | tf_op jit(solution)/shard_map/reduce_scatter | solution.py:93
  1023.8 242.0 %copy-start.43 = (f32[96]{0:T(128)S(1)}, f32[96]{0:T(128)}, u32[]{:S(2)}) copy-start(f32[96]{0:T(128)} %copy-done.42) | copy-start | bytes 1156
  1023.8 242.0 %copy-start.45 = (f32[96]{0:T(128)S(1)}, f32[96]{0:T(128)}, u32[]{:S(2)}) copy-start(f32[96]{0:T(128)} %copy-done.44) | copy-start | bytes 1156
  1023.8 259.9 %copy-start.17 = (bf16[1,196,197]{2,1,0:T(8,128)(2,1)S(1)}, bf16[1,196,197]{2,1,0:T(8,128)(2,1)}, u32[]{:S(2)}) copy-start(bf16[1,196,197]{2,1,0:T(8,128)(2,1)} %copy-done.16) | copy-start | bytes 231676
  1023.8 411.9 %all-gather.10.cloned.1.call-start = ((), (), s32[]{:S(2)}) async-start(), calls=%async_computation.5 | async-start | bytes 9093120 | tf_op jit(solution)/shard_map/all_gather | solution.py:257
  1303.1 202.2 %all-reduce.13.cloned.1.call-start = ((), (), s32[]{:S(2)}) async-start(), calls=%async_computation.11 | async-start | bytes 4186112 | tf_op jit(solution)/shard_map/psum | solution.py:270
  1330.6 112.6 %copy-start.21 = (f32[1,196,197]{2,0,1:T(1,128)S(1)}, f32[1,196,197]{2,0,1:T(1,128)}, u32[]{:S(2)}) copy-start(f32[1,196,197]{2,0,1:T(1,128)} %param.37) | copy-start | bytes 463348
  1330.6 112.8 %copy-start.26 = (f32[1,1,196,197]{3,1,2,0:T(1,128)S(1)}, f32[1,1,196,197]{3,1,2,0:T(1,128)}, u32[]{:S(2)}) copy-start(f32[1,1,196,197]{3,1,2,0:T(1,128)} %param.44) | copy-start | bytes 463348
  1330.6 112.9 %copy-start.27 = (f32[1,1,196,197]{3,1,2,0:T(1,128)S(1)}, f32[1,1,196,197]{3,1,2,0:T(1,128)}, u32[]{:S(2)}) copy-start(f32[1,1,196,197]{3,1,2,0:T(1,128)} %param.51) | copy-start | bytes 463348
  1330.6 113.7 %copy-start.28 = (f32[1,196,197]{2,0,1:T(1,128)S(1)}, f32[1,196,197]{2,0,1:T(1,128)}, u32[]{:S(2)}) copy-start(f32[1,196,197]{2,0,1:T(1,128)} %param.58) | copy-start | bytes 463348
  1330.6 114.5 %copy-start.29 = (f32[96,48]{0,1:T(8,128)S(1)}, f32[96,48]{0,1:T(8,128)}, u32[]{:S(2)}) copy-start(f32[96,48]{0,1:T(8,128)} %get-tuple-element.225) | copy-start | bytes 55300
  1330.6 119.0 %copy-start.55 = (f32[96]{0:T(128)S(1)}, f32[96]{0:T(128)}, u32[]{:S(2)}) copy-start(f32[96]{0:T(128)} %get-tuple-element.156) | copy-start | bytes 1156
  1330.6 118.9 %copy-start.56 = (f32[96]{0:T(128)S(1)}, f32[96]{0:T(128)}, u32[]{:S(2)}) copy-start(f32[96]{0:T(128)} %get-tuple-element.157) | copy-start | bytes 1156
  1330.6 118.9 %copy-start.57 = (f32[96]{0:T(128)S(1)}, f32[96]{0:T(128)}, u32[]{:S(2)}) copy-start(f32[96]{0:T(128)} %get-tuple-element.158) | copy-start | bytes 1156
  1330.6 119.0 %copy-start.59 = (f32[96]{0:T(128)S(1)}, f32[96]{0:T(128)}, u32[]{:S(2)}) copy-start(f32[96]{0:T(128)} %get-tuple-element.248) | copy-start | bytes 1156
  1330.7 217.1 %copy-start.9 = (f32[192,384]{1,0:T(8,128)S(1)}, f32[192,384]{1,0:T(8,128)}, u32[]{:S(2)}) copy-start(f32[192,384]{1,0:T(8,128)} %param.36) | copy-start | bytes 884740
  1443.1 107.8 %copy-start.7 = (f32[385,250]{1,0:T(8,128)S(1)}, f32[385,250]{1,0:T(8,128)}, u32[]{:S(2)}) copy-start(f32[385,250]{1,0:T(8,128)} %param.40) | copy-start | bytes 1155004
  1443.1 114.7 %copy-start.5 = (f32[1,385,384]{2,0,1:T(1,128)S(1)}, f32[1,385,384]{2,0,1:T(1,128)}, u32[]{:S(2)}) copy-start(f32[1,385,384]{2,0,1:T(1,128)} %param.38) | copy-start | bytes 1774084
  1443.1 101.0 %all-reduce.9.cloned.1.call-start = ((), (), s32[]{:S(2)}) async-start(), calls=%async_computation.6 | async-start | bytes 409600 | tf_op jit(solution)/shard_map/psum | solution.py:285
  1505.3 48.9 %copy-start.11 = (f32[1,384,384]{2,1,0:T(8,128)S(1)}, f32[1,384,384]{2,1,0:T(8,128)}, u32[]{:S(2)}) copy-start(f32[1,384,384]{2,1,0:T(8,128)} %get-tuple-element.182) | copy-start | bytes 1769476
  1505.3 52.5 %copy-start.10 = (f32[1,385,384]{2,1,0:T(8,128)S(1)}, f32[1,385,384]{2,1,0:T(8,128)}, u32[]{:S(2)}) copy-start(f32[1,385,384]{2,1,0:T(8,128)} %get-tuple-element.181) | copy-start | bytes 1774084
  1509.1 104.8 %all-reduce.11.cloned.1.call-start = ((), (), s32[]{:S(2)}) async-start(), calls=%async_computation.10 | async-start | bytes 4186112 | tf_op jit(solution)/shard_map/psum | solution.py:342
  1550.9 13.2 copy-start.33
  1550.9 13.2 copy-start.51
  1550.9 13.2 copy-start.52
  1550.9 15.0 copy-start.31
  1550.9 15.0 copy-start.53
  1550.9 15.0 copy-start.54
  1557.8 24.8 %copy-start.49 = (f32[5,96]{1,0:T(8,128)S(1)}, f32[5,96]{1,0:T(8,128)}, u32[]{:S(2)}) copy-start(f32[5,96]{1,0:T(8,128)} %param.62) | copy-start | bytes 5764
  1557.8 25.4 %copy-start.50 = (f32[5,96]{1,0:T(8,128)S(1)}, f32[5,96]{1,0:T(8,128)}, u32[]{:S(2)}) copy-start(f32[5,96]{1,0:T(8,128)} %param.63) | copy-start | bytes 5764
  1568.6 56.4 %copy-start.14 = (f32[1,384,384]{2,1,0:T(8,128)S(1)}, f32[1,384,384]{2,1,0:T(8,128)}, u32[]{:S(2)}) copy-start(f32[1,384,384]{2,1,0:T(8,128)} %param.39) | copy-start | bytes 1769476
  (21 other events, 147.7 us)
Sparse Core Ops, SparseCore 0:
  101.6 246.2 reduce-scatter.9
  376.0 132.4 all-gather.5
  544.9 253.1 reduce-scatter.11
  846.2 131.3 all-gather.7
  1023.9 241.7 reduce-scatter.13
  1303.2 132.4 all-gather.9
  1443.3 62.0 all-reduce.12
  1509.2 34.8 all-reduce.8
  1561.5 52.3 all-reduce.10
where the time goes:
time: 1640 us
  waiting for transfers between devices  1160 us (71%)
  local copies, waits for them, and re-layouts  181 us (11%)
  other arithmetic  104 us (6%)
  matrix products  92.7 us (6%)
  blocking collectives  69.2 us (4%)
  between operations  23.4 us (1%)
    reduce_scatter x1, waiting for transfers between devices, per_device(): lax.psum_scatter(product(embed_table, pixel_rows, (0,), (1,)), 'mp', scat...  245 us
    reduce_scatter x1, waiting for transfers between devices, layer_backward(): lax.psum_scatter(product(lax.slice_in_dim(up_table, 0, width * lax.axis_s...  242 us
    reduce_scatter x1, waiting for transfers between devices, layer_forward(): lax.psum_scatter(product(down_table, active, (0,), (0,)), 'mp', scatter_d...  218 us
    all_gather x1, waiting for transfers between devices, layer_forward(): ffn_whole = lax.all_gather(ffn_input, 'mp', axis=0, tiled=True)  131 us
    all_gather x1, waiting for transfers between devices, layer_backward(): output_whole = lax.all_gather(d_output_low, 'mp', axis=0, tiled=True)  131 us
    all_gather x1, waiting for transfers between devices, per_device(): lax.all_gather(d_stream_low, 'mp', axis=0, tiled=True)  105 us
    dot_general x14, matrix products, product(): lax.dot_general(first_operand, second_operand, ((left_dims, right_dims),...  92.7 us
    unnamed x144, local copies, waits for them, and re-layouts  77.8 us
  transfers between devices with their start and end apart: 9, of which 9 were waited for; matrix products, arithmetic and copies ran while one was open for 4% of the time, Pallas kernels for 0%

commit v1 on v0

v1 whole, which is shorter than its diff:
```python
import functools

import jax
import jax.numpy as jnp
from jax import lax
from jax.experimental import pallas as pl
from jax.experimental.pallas import tpu as pltpu
from jax.sharding import PartitionSpec as P

F32 = jnp.float32
BF16 = jnp.bfloat16
MESH = pl.DeviceIdType.MESH
VMEM = pltpu.VMEM
SMEM = pltpu.SMEM

D = 384
PATCHES = 196
ROWS = 208
STEP = 10
LANE = 128

mix_share = 0.7
clip_limit = 0.01
beta_one = 0.9
beta_two = 0.999
adam_eps = 1e-08
weight_decay = 0.05
matrix_rate = 0.05
head_rate = 0.5
vector_rate = 0.4
outer_rate = 0.7
outer_momentum = 0.9

GELU_A = 0.7978845608028654
GELU_B = GELU_A * 0.044715

B_EXP, B_EMB, B_MIX, B_SMALL, B_ACT, B_ROWS = 0, 392, 584, 640, 656, 672
MIX_BLOCK = 56
A_EMB, A_EXP, A_SHR, A_ROWS = 0, 192, 584, 976
C_CLS, C_MIX, C_SCA, C_SHI, C_ROWS = 0, 392, 592, 600, 624


def dot(a, b, dims=((1,), (0,)), precision=None):
    return lax.dot_general(
        a, b, (dims, ((), ())), preferred_element_type=F32, precision=precision
    )


def exact(a, b, dims=((1,), (0,))):
    return dot(a, b, dims, lax.Precision.HIGHEST)


def rounded(a):
    return a.astype(BF16).astype(F32)


def greet(peers):
    barrier = pltpu.get_barrier_semaphore()
    for peer in peers:
        pl.semaphore_signal(barrier, inc=1, device_id=peer, device_id_type=MESH)
    pl.semaphore_wait(barrier, len(peers))


def remote(src, dst, send_sem, recv_sem, peer):
    return pltpu.make_async_remote_copy(
        src_ref=src, dst_ref=dst, send_sem=send_sem, recv_sem=recv_sem,
        device_id=peer, device_id_type=MESH,
    )


def move_kernel(
    G, MP, NI,
    partner, patches, emb, expa, shr, cls, sca, shi,
    rows, e_all, w1, w2, wc, small,
    stage, rs_send, rs_recv, wz_send, wz_recv, wg_send, wg_recv, sm_send, sm_recv,
):
    z = lax.axis_index("mp")
    g = lax.axis_index("group")
    NP = NI // 2
    zpeer = [lax.rem(z + d, MP) for d in range(1, MP)]
    gpeer = [lax.rem(g + d, G) for d in range(1, G)]
    greet([{"mp": t} for t in zpeer] + [{"group": t} for t in gpeer])

    hid = expa.shape[1]
    ncls = cls.shape[1]
    cpad = wc.shape[1] // MP

    e_all[z] = emb[...].astype(BF16)
    w1[:, pl.ds(pl.multiple_of(z * hid, LANE), hid)] = expa[0:D, :].astype(BF16)
    w2[pl.ds(pl.multiple_of(z * hid, 16), hid), :] = shr[...].astype(BF16)
    head = jnp.concatenate([cls[0:D, :], jnp.zeros((D, cpad - ncls), F32)], axis=1)
    wc[:, pl.ds(pl.multiple_of(z * cpad, LANE), cpad)] = head.astype(BF16)
    small[z] = jnp.zeros(small.shape[1:], F32)
    small[z, 0:5, 0 : D // MP] = sca[...]
    small[z, 5:10, 0 : D // MP] = shi[...]
    small[z, 10:11, :] = rounded(expa[D : D + 1, :])
    small[z, 11:12, 0:ncls] = rounded(cls[D : D + 1, :])

    er, hr, dr = emb.shape[0] // G, hid // G, D // G

    def pieces(t, j):
        return (
            e_all.at[t, pl.ds(pl.multiple_of(j * er, 16), er), :],
            w1.at[pl.ds(pl.multiple_of(j * dr, 16), dr), pl.ds(pl.multiple_of(t * hid, LANE), hid)],
            w2.at[pl.ds(pl.multiple_of(t * hid + j * hr, 16), hr), :],
            wc.at[pl.ds(pl.multiple_of(j * dr, 16), dr), pl.ds(pl.multiple_of(t * cpad, LANE), cpad)],
        )

    started = []
    for d, t in enumerate(zpeer):
        c = remote(small.at[z], small.at[z], sm_send.at[d], sm_recv.at[z], {"mp": t})
        c.start()
        started.append(c)
        for k, part in enumerate(pieces(z, g)):
            c = remote(part, part, wz_send.at[d, k], wz_recv.at[z, k], {"mp": t})
            c.start()
            started.append(c)

    share = F32(mix_share)
    other = F32(1.0 - mix_share)

    def blend(i):
        return share * patches[i] + other * patches[partner[i]]

    tail = rows.shape[-2] - 192

    def put(ref, lead, value):
        ref[lead + (slice(0, 192), slice(None))] = value[0:192].astype(BF16)
        last = jnp.concatenate([value[192:], jnp.zeros((tail - (PATCHES - 192), LANE), F32)], axis=0)
        ref[lead + (slice(192, 192 + tail), slice(None))] = last.astype(BF16)

    def blend_pair(t, p, ref, lead):
        a = blend(t * NI + 2 * p)
        b = blend(t * NI + 2 * p + 1)
        put(ref, lead + (0,), a[:, 0:LANE])
        put(ref, lead + (1,), b[:, 0:LANE])
        put(ref, lead + (2,), jnp.concatenate([a[:, LANE:], b[:, LANE:]], axis=1))

    def send(p, d):
        return remote(stage.at[d, p], rows.at[z, p], rs_send.at[d, p], rs_recv.at[z, p], {"mp": zpeer[d]})

    def each_pair(p, carry):
        for d in range(MP - 1):
            blend_pair(zpeer[d], p, stage, (d, p))
            send(p, d).start()
        return carry

    lax.fori_loop(0, NP, each_pair, 0)

    for d in range(1, MP):
        t = lax.rem(z + MP - d, MP)
        for k, part in enumerate(pieces(t, g)):
            remote(part, part, wz_send.at[d - 1, k], wz_recv.at[t, k], {"mp": t}).wait_recv()
            for e, j in enumerate(gpeer):
                c = remote(part, part, wg_send.at[d - 1, e, k], wg_recv.at[t, g, k], {"group": j})
                c.start()
                started.append(c)

    def own_pair(p, carry):
        blend_pair(z, p, rows, (z, p))
        return carry

    lax.fori_loop(0, NP, own_pair, 0)

    def drain(p, carry):
        for d in range(MP - 1):
            send(p, d).wait_send()
            t = zpeer[d]
            remote(stage.at[d, p], rows.at[t, p], rs_send.at[d, p], rs_recv.at[t, p], {"mp": t}).wait_recv()
        return carry

    lax.fori_loop(0, NP, drain, 0)
    for c in started:
        c.wait_send()
    for t in zpeer:
        remote(small.at[t], small.at[t], sm_send.at[0], sm_recv.at[t], {"mp": t}).wait_recv()
        for j in gpeer:
            for k, part in enumerate(pieces(t, j)):
                remote(part, part, wg_send.at[0, 0, k], wg_recv.at[t, j, k], {"group": j}).wait_recv()


def move(G, MP, partner, patches, emb, expa, shr, cls, sca, shi):
    NI = patches.shape[0] // MP
    NP = NI // 2
    hid = expa.shape[1]
    cpad = -(-cls.shape[1] // LANE) * LANE
    dma = pltpu.SemaphoreType.DMA
    vm = pl.BlockSpec(memory_space=VMEM)
    ge = max(G - 1, 1)
    return pl.pallas_call(
        functools.partial(move_kernel, G, MP, NI),
        out_shape=(
            jax.ShapeDtypeStruct((MP, NP, 3, ROWS, LANE), BF16),
            jax.ShapeDtypeStruct((MP, emb.shape[0], D), BF16),
            jax.ShapeDtypeStruct((D, hid * MP), BF16),
            jax.ShapeDtypeStruct((hid * MP, D), BF16),
            jax.ShapeDtypeStruct((D, cpad * MP), BF16),
            jax.ShapeDtypeStruct((MP, 16, hid), F32),
        ),
        in_specs=[pl.BlockSpec(memory_space=SMEM)] + [vm] * 7,
        out_specs=(vm,) * 6,
        scratch_shapes=[
            pltpu.VMEM((MP - 1, NP, 3, ROWS, LANE), BF16),
            dma((MP - 1, NP)),
            dma((MP, NP)),
            dma((MP - 1, 4)),
            dma((MP, 4)),
            dma((MP - 1, ge, 4)),
            dma((MP, G, 4)),
            dma((MP - 1,)),
            dma((MP,)),
        ],
        compiler_params=pltpu.CompilerParams(
            collective_id=0, has_side_effects=True, vmem_limit_bytes=56 << 20
        ),
    )(partner, patches, emb, expa, shr, cls, sca, shi)


def step_kernel(
    MP, NI, ncls,
    labels, partner, rows, e_all, w1, w2, wc, small, mixing, class_weight,
    bundle, factors,
    xs, gp, s0, s1, mx, mi, fi, ep, mm, mt, mbias, vec, b1, asum, s1sum, la, lb,
    dact, ds2, dh, csum, gw, ge, gm, gmb, gvec,
):
    z = lax.axis_index("mp")
    NP = NI // 2
    PR = 2 * ROWS
    hid_all = w1.shape[1]
    hid = hid_all // MP
    cpad = wc.shape[1] // MP
    CH = 256
    NCH = hid_all // CH
    er = e_all.shape[1]

    full = jnp.zeros((16, D), F32)
    for t in range(MP):
        block = small[t]
        full = full + (pltpu.roll(block, t * (D // MP), 1) if t else block)
    vec[...] = full
    for t in range(MP):
        b1[:, t * hid : (t + 1) * hid] = small[t, 10:11, :]
        ep[t * LANE : (t + 1) * LANE, :] = e_all[t, 0:LANE, :]
        half = er - LANE
        ep[MP * LANE + t * half : MP * LANE + (t + 1) * half, :] = e_all[t, LANE:er, :]

    wide = jnp.concatenate([mixing[...], jnp.zeros((PATCHES, 256 - PATCHES - 1), F32)], axis=1)
    wide = jnp.concatenate([wide, jnp.zeros((256 - PATCHES, 256), F32)], axis=0)
    column = lax.broadcasted_iota(jnp.int32, (256, 256), 1)
    square = jnp.where(column < PATCHES, wide, 0.0)
    mm[...] = square[0:ROWS, 0:ROWS].astype(BF16)
    mt[...] = jnp.transpose(square)[0:ROWS, 0:ROWS].astype(BF16)
    mbias[...] = rounded(jnp.sum(jnp.where(column == PATCHES, wide, 0.0), axis=1, keepdims=True)[0:ROWS])

    asum[...] = jnp.zeros_like(asum)
    s1sum[...] = jnp.zeros_like(s1sum)
    csum[...] = jnp.zeros_like(csum)
    gw[...] = jnp.zeros_like(gw)
    ge[...] = jnp.zeros_like(ge)
    gm[...] = jnp.zeros_like(gm)
    gmb[...] = jnp.zeros_like(gmb)
    gvec[...] = jnp.zeros_like(gvec)

    def scale(k):
        return vec[k : k + 1, :]

    def shift(k):
        return vec[5 + k : 6 + k, :]

    def forward(p, carry):
        for t in range(MP):
            xs[p, 0:ROWS, t * LANE : (t + 1) * LANE] = rows[t, p, 0]
            xs[p, ROWS:PR, t * LANE : (t + 1) * LANE] = rows[t, p, 1]
        for t in range(0, MP, 2):
            left, right = rows[t, p, 2], rows[t + 1, p, 2]
            at = MP * LANE + t * 64
            xs[p, 0:ROWS, at : at + LANE] = jnp.concatenate([left[:, 0:64], right[:, 0:64]], axis=1)
            xs[p, ROWS:PR, at : at + LANE] = jnp.concatenate([left[:, 64:], right[:, 64:]], axis=1)
        stream0 = dot(xs[p], ep[...]) + shift(3)
        s0[p] = stream0
        mi[p] = (scale(0) * stream0 + shift(0)).astype(BF16)
        for b in range(2):
            r = slice(b * ROWS, (b + 1) * ROWS)
            mixed = dot(mm[...], mi[p, r, :]) + mbias[...]
            mx[p, r, :] = mixed
            stream1 = s0[p, r, :] + scale(1) * mixed
            s1[p, r, :] = stream1
            fi[p, r, :] = (scale(2) * stream1 + shift(1)).astype(BF16)
            s1sum[pl.ds(2 * p + b, 1), :] = jnp.sum(stream1[0:PATCHES], axis=0, keepdims=True)

        def chunk(c, carry):
            cols = pl.ds(pl.multiple_of(c * CH, CH), CH)
            for b in range(2):
                r = slice(b * ROWS, (b + 1) * ROWS)
                h = dot(fi[p, r, :], w1[:, cols]) + b1[:, cols]
                sq = h * h
                s = 0.5 * jnp.tanh(h * (GELU_A + GELU_B * sq)) + 0.5
                act = rounded(h * s)
                asum[pl.ds(2 * p + b, 1), cols] = jnp.sum(act[0:PATCHES], axis=0, keepdims=True)
                gp[p, r, cols] = s + s * (1.0 - s) * (h * (2.0 * GELU_A + 6.0 * GELU_B * sq))
                gp[p, b * ROWS + PATCHES : (b + 1) * ROWS, cols] = jnp.zeros((ROWS - PATCHES, CH), F32)
            return carry

        lax.fori_loop(0, NCH, chunk, 0)
        return carry

    lax.fori_loop(0, NP, forward, 0)

    la[...] = jnp.full(la.shape, -1, jnp.int32)
    lb[...] = jnp.full(lb.shape, -1, jnp.int32)
    for i in range(NI):
        own = labels[z * NI + i]
        mate = labels[partner[z * NI + i]]
        la[i : i + 1, :] = jnp.full((1, LANE), own, jnp.int32)
        lb[i : i + 1, :] = jnp.full((1, LANE), mate, jnp.int32)
    outsum = exact(asum[...], w2[...].astype(F32)) + PATCHES * shift(2)
    stream2 = s1sum[...] + scale(3) * outsum
    pooled = (scale(4) * (stream2 * (1.0 / PATCHES)) + shift(4)).astype(BF16)
    bias = jnp.concatenate([small[t, 11:12, 0:cpad] for t in range(MP)], axis=1)
    lane = lax.broadcasted_iota(jnp.int32, (16, cpad * MP), 1)
    inside = lax.rem(lane, cpad)
    valid = inside < ncls
    class_id = (lane // cpad) * ncls + inside
    logits = jnp.where(valid, dot(pooled, wc[...]) + bias, -1e30)
    hot_a = jnp.where(valid & (class_id == la[:, 0:1]), 1.0, 0.0)
    hot_b = jnp.where(valid & (class_id == lb[:, 0:1]), 1.0, 0.0)
    weight_a = mix_share * jnp.sum(hot_a * class_weight[...], axis=1, keepdims=True)
    weight_b = (1.0 - mix_share) * jnp.sum(hot_b * class_weight[...], axis=1, keepdims=True)
    top = jnp.max(logits, axis=1, keepdims=True)
    exps = jnp.where(valid, jnp.exp(logits - top), 0.0)
    exp_sum = jnp.sum(exps, axis=1, keepdims=True)
    log_total = top + jnp.log(exp_sum)
    target_a = jnp.sum(hot_a * logits, axis=1, keepdims=True)
    target_b = jnp.sum(hot_b * logits, axis=1, keepdims=True)
    loss = jnp.sum(weight_a * (log_total - target_a) + weight_b * (log_total - target_b), axis=0, keepdims=True)
    total = jnp.sum(weight_a + weight_b, axis=0, keepdims=True)
    dlog = ((weight_a + weight_b) * (exps / exp_sum) - weight_a * hot_a - weight_b * hot_b).astype(BF16)
    dfinal = dot(dlog, wc[...], ((1,), (1,))) * (1.0 / PATCHES)
    dstream2 = scale(4) * dfinal
    ds2[...] = dstream2
    dout = scale(3) * dstream2
    low = dout.astype(BF16)
    dact[...] = dot(low, w2[...], ((1,), (1,)))
    factors[:, 0:16, :] = jnp.broadcast_to(low[None], (MP, 16, D))
    factors[:, 16:32, :] = jnp.broadcast_to(pooled[None], (MP, 16, D))
    for t in range(MP):
        factors[t, 32:48, 0:cpad] = dlog[:, t * cpad : (t + 1) * cpad]
        factors[t, 32:48, cpad:] = jnp.zeros((16, D - cpad), BF16)

    def backward(p, carry):
        def chunk(c, carry):
            cols = pl.ds(pl.multiple_of(c * CH, CH), CH)
            for b in range(2):
                r = slice(b * ROWS, (b + 1) * ROWS)
                dh[r, cols] = (gp[p, r, cols] * dact[pl.ds(2 * p + b, 1), cols]).astype(BF16)
            value = dh[:, cols]
            csum[0:1, cols] += jnp.sum(value.astype(F32), axis=0, keepdims=True)
            gw[:, cols] += dot(fi[p], value, ((0,), (0,)))
            return carry

        lax.fori_loop(0, NCH, chunk, 0)
        dffn = dot(dh[...], w1[...], ((1,), (1,)))
        gvec[2:3, :] += jnp.sum(dffn * s1[p], axis=0, keepdims=True)
        gvec[6:7, :] += jnp.sum(dffn, axis=0, keepdims=True)
        for b in range(2):
            r = slice(b * ROWS, (b + 1) * ROWS)
            d1 = ds2[pl.ds(2 * p + b, 1), :] + scale(2) * dffn[r]
            gvec[1:2, :] += jnp.sum(mx[p, r, :] * d1, axis=0, keepdims=True)
            dmixed = (scale(1) * d1).astype(BF16)
            gm[...] += dot(dmixed, mi[p, r, :], ((1,), (1,)))
            gmb[...] += dmixed.astype(F32)
            dmixer = dot(mt[...], dmixed)
            gvec[0:1, :] += jnp.sum(dmixer * s0[p, r, :], axis=0, keepdims=True)
            gvec[5:6, :] += jnp.sum(dmixer, axis=0, keepdims=True)
            d0 = (d1 + scale(0) * dmixer).astype(BF16)
            ge[...] += dot(xs[p, r, :], d0, ((0,), (0,)))
        return carry

    lax.fori_loop(0, NP, backward, 0)

    gvec[3:4, :] = jnp.sum(outsum * dstream2, axis=0, keepdims=True)
    gvec[4:5, :] = jnp.sum(dfinal * stream2, axis=0, keepdims=True)
    gvec[7:8, :] = PATCHES * jnp.sum(dout, axis=0, keepdims=True)
    gvec[8:9, :] = (
        PATCHES * jnp.sum(dstream2, axis=0, keepdims=True) + scale(2) * gvec[6:7, :] + scale(0) * gvec[5:6, :]
    )
    gvec[9:10, :] = PATCHES * jnp.sum(dfinal, axis=0, keepdims=True)
    lane = lax.broadcasted_iota(jnp.int32, (1, D), 1)
    gvec[10:11, :] = jnp.where(lane == 0, loss, jnp.where(lane == 1, total, 0.0))

    row = lax.broadcasted_iota(jnp.int32, (ROWS, 256), 0)
    column = lax.broadcasted_iota(jnp.int32, (ROWS, 256), 1)
    bias_grad = jnp.sum(gmb[...], axis=1, keepdims=True)
    grad = jnp.concatenate([gm[...], jnp.zeros((ROWS, 256 - ROWS), F32)], axis=1)
    grad = jnp.where(column < PATCHES, grad, jnp.where(column == PATCHES, bias_grad, 0.0))
    grad = jnp.where(row < PATCHES, grad, 0.0)
    for t in range(MP):
        bundle[t, B_EXP : B_EXP + D, :] = gw[:, t * hid : (t + 1) * hid]
        bundle[t, B_EXP + D : B_EMB, :] = jnp.concatenate(
            [csum[:, t * hid : (t + 1) * hid], jnp.zeros((B_EMB - B_EXP - D - 1, hid), F32)], axis=0
        )
        bundle[t, B_EMB : B_EMB + LANE, :] = ge[t * LANE : (t + 1) * LANE, :]
        half = er - LANE
        bundle[t, B_EMB + LANE : B_EMB + er, :] = ge[MP * LANE + t * half : MP * LANE + (t + 1) * half, :]
        bundle[t, B_MIX:B_SMALL, :] = jnp.zeros((MIX_BLOCK, D), F32)
        n = min(MIX_BLOCK, ROWS - t * MIX_BLOCK)
        bundle[t, B_MIX : B_MIX + n, 0:256] = grad[t * MIX_BLOCK : t * MIX_BLOCK + n]
        bundle[t, B_SMALL:B_ACT, :] = gvec[...]
        bundle[t, B_ACT:B_ROWS, :] = asum[:, t * hid : (t + 1) * hid]


def local_step(MP, ncls, labels, partner, rows, e_all, w1, w2, wc, small, mixing, class_weight):
    NP = rows.shape[1]
    NI = 2 * NP
    PR = 2 * ROWS
    hid_all = w1.shape[1]
    pd = e_all.shape[0] * e_all.shape[1]
    vm = pl.BlockSpec(memory_space=VMEM)
    sm = pl.BlockSpec(memory_space=SMEM)
    return pl.pallas_call(
        functools.partial(step_kernel, MP, NI, ncls),
        out_shape=(
            jax.ShapeDtypeStruct((MP, B_ROWS, D), F32),
            jax.ShapeDtypeStruct((MP, 48, D), BF16),
        ),
        in_specs=[sm, sm] + [vm] * 8,
        out_specs=(vm, vm),
        scratch_shapes=[
            VMEM((NP, PR, pd), BF16),
            VMEM((NP, PR, hid_all), F32),
            VMEM((NP, PR, D), F32),
            VMEM((NP, PR, D), F32),
            VMEM((NP, PR, D), F32),
            VMEM((NP, PR, D), BF16),
            VMEM((NP, PR, D), BF16),
            VMEM((pd, D), BF16),
            VMEM((ROWS, ROWS), BF16),
            VMEM((ROWS, ROWS), BF16),
            VMEM((ROWS, 1), F32),
            VMEM((16, D), F32),
            VMEM((1, hid_all), F32),
            VMEM((16, hid_all), F32),
            VMEM((16, D), F32),
            VMEM((16, LANE), jnp.int32),
            VMEM((16, LANE), jnp.int32),
            VMEM((16, hid_all), F32),
            VMEM((16, D), F32),
            VMEM((PR, hid_all), BF16),
            VMEM((1, hid_all), F32),
            VMEM((D, hid_all), F32),
            VMEM((pd, D), F32),
            VMEM((ROWS, ROWS), F32),
            VMEM((ROWS, D), F32),
            VMEM((16, D), F32),
        ],
        compiler_params=pltpu.CompilerParams(vmem_limit_bytes=62 << 20),
    )(labels, partner, rows, e_all, w1, w2, wc, small, mixing, class_weight)


def adamw(weight, gradient, moment_one, moment_two, rate):
    mean_new = beta_one * moment_one + (1.0 - beta_one) * gradient
    square_new = beta_two * moment_two + (1.0 - beta_two) * gradient * gradient
    mean_hat = mean_new * (1.0 / (1.0 - beta_one**STEP))
    square_hat = square_new * (1.0 / (1.0 - beta_two**STEP))
    moved = rate * (mean_hat / (jnp.sqrt(square_hat) + adam_eps) + weight_decay * weight)
    return moved, mean_new, square_new


def sum_kernel(
    G, DP, MP,
    bundle, factors,
    emb, mixing, expa, shr, cls, sca, shi,
    emb1, mixing1, expa1, shr1, cls1, sca1, shi1,
    emb2, mixing2, expa2, shr2, cls2, sca2, shi2,
    g_emb, g_mix, g_exp, g_shr, g_cls, g_vec, sum_a, sum_c, info,
    rb, rc, yb, yc, nz, mva, mvc, h1a, h1c, h2a, h2c,
    zs, zr, ys, yr, ns, nr, gs, gr,
):
    z = lax.axis_index("mp")
    y = lax.axis_index("dp")
    g = lax.axis_index("group")
    zpeer = [lax.rem(z + d, MP) for d in range(1, MP)]
    ypeer = [lax.rem(y + d, DP) for d in range(1, DP)]
    gstep = []
    if G > 1:
        gstep.append(g + 1 - 2 * lax.rem(g, 2))
    if G > 2:
        gstep.append(lax.rem(g + 2, 4))
    greet([{"mp": t} for t in zpeer] + [{"dp": t} for t in ypeer] + [{"group": t} for t in gstep])

    started = []

    def go(*args):
        c = remote(*args)
        c.start()
        started.append(c)

    for d, t in enumerate(zpeer):
        go(factors.at[t], rc.at[z], zs.at[d, 0], zr.at[z, 0], {"mp": t})
        go(bundle.at[t], rb.at[z], zs.at[d, 1], zr.at[z, 1], {"mp": t})
    rc[z] = factors[z]
    rb[z, B_SMALL:, :] = bundle[z, B_SMALL:, :]
    for t in zpeer:
        remote(factors.at[t], rc.at[t], zs.at[0, 0], zr.at[t, 0], {"mp": t}).wait_recv()
        remote(bundle.at[t], rb.at[t], zs.at[0, 1], zr.at[t, 1], {"mp": t}).wait_recv()

    total = bundle[z, 0:B_SMALL, :]
    for t in zpeer:
        total = total + rb[t, 0:B_SMALL, :]
    yb[y, 0:B_SMALL, :] = total
    vector = rb[0, B_SMALL:B_ACT, :]
    for t in range(1, MP):
        vector = vector + rb[t, B_SMALL:B_ACT, :]
    yb[y, B_SMALL:B_ACT, :] = vector
    for t in range(MP):
        yb[y, B_ACT + 16 * t : B_ACT + 16 * (t + 1), :] = rb[t, B_ACT:B_ROWS, :]
        for k in range(3):
            at = (k * MP + t) * 16
            yc[y, at : at + 16, :] = rc[t, 16 * k : 16 * (k + 1), :]
    for d, t in enumerate(ypeer):
        go(yb.at[y], yb.at[y], ys.at[d, 0], yr.at[y, 0], {"dp": t})
        go(yc.at[y], yc.at[y], ys.at[d, 1], yr.at[y, 1], {"dp": t})
    for t in ypeer:
        remote(yb.at[t], yb.at[t], ys.at[0, 0], yr.at[t, 0], {"dp": t}).wait_recv()
        remote(yc.at[t], yc.at[t], ys.at[0, 1], yr.at[t, 1], {"dp": t}).wait_recv()

    def over_dp(lo, hi):
        value = yb[0, lo:hi, :]
        for t in range(1, DP):
            value = value + yb[t, lo:hi, :]
        return value

    n = 16 * MP
    cpad = g_cls.shape[1]
    grad_shr = jnp.zeros((D, D), F32)
    grad_cls = jnp.zeros((D, cpad), F32)
    cls_bias = jnp.zeros((1, cpad), F32)
    for t in range(DP):
        acts = yb[t, B_ACT : B_ACT + n, :]
        dout, pooled, dlog = yc[t, 0:n, :], yc[t, n : 2 * n, :], yc[t, 2 * n : 3 * n, 0:cpad]
        grad_shr = grad_shr + exact(acts, dout.astype(F32), ((0,), (0,)))
        grad_cls = grad_cls + dot(pooled, dlog, ((0,), (0,)))
        cls_bias = cls_bias + jnp.sum(dlog.astype(F32), axis=0, keepdims=True)
    g_shr[...] = grad_shr
    g_cls[0:D, :] = grad_cls
    g_cls[D:, :] = jnp.concatenate([cls_bias, jnp.zeros((g_cls.shape[0] - D - 1, cpad), F32)], axis=0)
    g_exp[...] = over_dp(B_EXP, B_EMB)
    g_emb[...] = over_dp(B_EMB, B_MIX)
    vector = over_dp(B_SMALL, B_ACT)
    mix = over_dp(B_MIX, B_SMALL)[:, 0:256]

    def squares(v):
        return jnp.sum(jnp.sum(v * v, axis=1, keepdims=True), axis=0, keepdims=True)

    part = (
        squares(g_exp[...]) + squares(g_emb[...]) + squares(g_shr[...]) + squares(g_cls[...]) + squares(mix)
    )
    nz[z, 0:MIX_BLOCK, :] = mix
    nz[z, MIX_BLOCK:, :] = jnp.broadcast_to(part, (8, 256))
    for d, t in enumerate(zpeer):
        go(nz.at[z], nz.at[z], ns.at[d], nr.at[z], {"mp": t})
    for t in zpeer:
        remote(nz.at[t], nz.at[t], ns.at[0], nr.at[t], {"mp": t}).wait_recv()
    square = nz[0, MIX_BLOCK : MIX_BLOCK + 1, 0:1]
    for t in range(1, MP):
        square = square + nz[t, MIX_BLOCK : MIX_BLOCK + 1, 0:1]
    square = square + squares(vector[0:10])
    loss_sum = vector[10:11, 0:1]
    weight_total = vector[10:11, 1:2]
    size = jnp.sqrt(square) / weight_total
    factor = clip_limit / jnp.maximum(size, clip_limit)
    scaled = factor / weight_total
    lane = lax.broadcasted_iota(jnp.int32, (8, LANE), 1)
    info[...] = jnp.where(lane == 0, loss_sum, jnp.where(lane == 1, weight_total, size))

    g_exp[...] = g_exp[...] * scaled
    g_emb[...] = g_emb[...] * scaled
    g_shr[...] = g_shr[...] * scaled
    g_cls[...] = g_cls[...] * scaled
    for t in range(MP):
        g_mix[t * MIX_BLOCK : (t + 1) * MIX_BLOCK, :] = nz[t, 0:MIX_BLOCK, :] * scaled
    own = D // MP
    g_vec[...] = pltpu.roll(vector, lax.rem((MP - z) * own, D), 1)[:, 0:LANE] * scaled

    ncls = cls.shape[1]
    mva[A_EXP + D : A_SHR, :] = jnp.zeros((A_SHR - A_EXP - D, D), F32)
    mva[A_SHR + D :, :] = jnp.zeros((A_ROWS - A_SHR - D, D), F32)
    mvc[...] = jnp.zeros_like(mvc)
    mva[A_EMB : A_EMB + emb.shape[0], :] = adamw(emb[...], g_emb[...], emb1[...], emb2[...], matrix_rate)[0]
    mva[A_EXP : A_EXP + D + 1, :] = adamw(expa[...], g_exp[0 : D + 1, :], expa1[...], expa2[...], matrix_rate)[0]
    mva[A_SHR : A_SHR + shr.shape[0], :] = adamw(shr[...], g_shr[...], shr1[...], shr2[...], matrix_rate)[0]
    mvc[C_CLS : C_CLS + D + 1, 0:ncls] = adamw(cls[...], g_cls[0 : D + 1, 0:ncls], cls1[...], cls2[...], head_rate)[0]
    mvc[C_MIX : C_MIX + PATCHES, 0 : PATCHES + 1] = adamw(
        mixing[...], g_mix[0:PATCHES, 0 : PATCHES + 1], mixing1[...], mixing2[...], matrix_rate
    )[0]
    mvc[C_SCA : C_SCA + 5, 0:own] = adamw(sca[...], g_vec[0:5, 0:own], sca1[...], sca2[...], vector_rate)[0]
    mvc[C_SHI : C_SHI + 5, 0:own] = adamw(shi[...], g_vec[5:10, 0:own], shi1[...], shi2[...], vector_rate)[0]

    if G == 1:
        sum_a[...] = mva[...]
        sum_c[...] = mvc[...]
    else:
        ha, hc = A_ROWS // 2, C_ROWS // 2
        mine, theirs = lax.rem(g, 2), 1 - lax.rem(g, 2)

        def half(ref, k, n):
            return ref.at[pl.ds(pl.multiple_of(k * n, 8), n), :]

        peer = {"group": gstep[0]}
        go(half(mva, theirs, ha), h1a, gs.at[0], gr.at[0], peer)
        go(half(mvc, theirs, hc), h1c, gs.at[1], gr.at[1], peer)
        remote(h1a, h1a, gs.at[0], gr.at[0], peer).wait_recv()
        remote(h1c, h1c, gs.at[1], gr.at[1], peer).wait_recv()
        own_a = pl.ds(pl.multiple_of(mine * ha, 8), ha)
        own_c = pl.ds(pl.multiple_of(mine * hc, 8), hc)
        pa = mva[own_a, :] + h1a[...]
        pc = mvc[own_c, :] + h1c[...]
        if G > 2:
            h2a[0] = pa
            h2c[0] = pc
            far = {"group": gstep[1]}
            go(h2a.at[0], h2a.at[1], gs.at[2], gr.at[2], far)
            go(h2c.at[0], h2c.at[1], gs.at[3], gr.at[3], far)
            remote(h2a.at[0], h2a.at[1], gs.at[2], gr.at[2], far).wait_recv()
            remote(h2c.at[0], h2c.at[1], gs.at[3], gr.at[3], far).wait_recv()
            pa = h2a[0] + h2a[1]
            pc = h2c[0] + h2c[1]
        sum_a[own_a, :] = pa
        sum_c[own_c, :] = pc
        go(half(sum_a, mine, ha), half(sum_a, mine, ha), gs.at[4], gr.at[4], peer)
        go(half(sum_c, mine, hc), half(sum_c, mine, hc), gs.at[5], gr.at[5], peer)
        remote(h1a, half(sum_a, theirs, ha), gs.at[4], gr.at[4], peer).wait_recv()
        remote(h1c, half(sum_c, theirs, hc), gs.at[5], gr.at[5], peer).wait_recv()

    for c in started:
        c.wait_send()


def gradient_sums(G, DP, MP, bundle, factors, weights, firsts, seconds):
    dma = pltpu.SemaphoreType.DMA
    vm = pl.BlockSpec(memory_space=VMEM)
    cpad = -(-weights[4].shape[1] // LANE) * LANE
    s = jax.ShapeDtypeStruct
    rows_y = B_ACT + 16 * MP
    return pl.pallas_call(
        functools.partial(sum_kernel, G, DP, MP),
        out_shape=(
            s((weights[0].shape[0], D), F32),
            s((MP * MIX_BLOCK, 256), F32),
            s((B_EMB, D), F32),
            s((D, D), F32),
            s((392, cpad), F32),
            s((16, LANE), F32),
            s((A_ROWS, D), F32),
            s((C_ROWS, 256), F32),
            s((8, LANE), F32),
        ),
        in_specs=[vm] * 23,
        out_specs=(vm,) * 9,
        scratch_shapes=[
            VMEM((MP, B_ROWS, D), F32),
            VMEM((MP, 48, D), BF16),
            VMEM((DP, rows_y, D), F32),
            VMEM((DP, 48 * MP, D), BF16),
            VMEM((MP, MIX_BLOCK + 8, 256), F32),
            VMEM((A_ROWS, D), F32),
            VMEM((C_ROWS, 256), F32),
            VMEM((A_ROWS // 2, D), F32),
            VMEM((C_ROWS // 2, 256), F32),
            VMEM((2, A_ROWS // 2, D), F32),
            VMEM((2, C_ROWS // 2, 256), F32),
            dma((MP - 1, 2)),
            dma((MP, 2)),
            dma((max(DP - 1, 1), 2)),
            dma((DP, 2)),
            dma((MP - 1,)),
            dma((MP,)),
            dma((6,)),
            dma((6,)),
        ],
        compiler_params=pltpu.CompilerParams(
            collective_id=1, has_side_effects=True, vmem_limit_bytes=60 << 20
        ),
    )(bundle, factors, *weights, *firsts, *seconds)


def finish_kernel(groups, *refs):
    g_emb, g_mix, g_exp, g_shr, g_cls, g_vec, sum_a, sum_c = refs[:8]
    weights, firsts, seconds, outers = (refs[8 + 7 * k : 15 + 7 * k] for k in range(4))
    updates, means, squares, velocities = (refs[36 + 7 * k : 43 + 7 * k] for k in range(4))
    own = weights[5].shape[1]
    ncls = weights[4].shape[1]
    grads = (
        g_emb[...], g_mix[0:PATCHES, 0 : PATCHES + 1], g_exp[0 : D + 1, :], g_shr[...],
        g_cls[0 : D + 1, 0:ncls], g_vec[0:5, 0:own], g_vec[5:10, 0:own],
    )
    sums = (
        sum_a[A_EMB : A_EMB + weights[0].shape[0], :],
        sum_c[C_MIX : C_MIX + PATCHES, 0 : PATCHES + 1],
        sum_a[A_EXP : A_EXP + D + 1, :],
        sum_a[A_SHR : A_SHR + D, :],
        sum_c[C_CLS : C_CLS + D + 1, 0:ncls],
        sum_c[C_SCA : C_SCA + 5, 0:own],
        sum_c[C_SHI : C_SHI + 5, 0:own],
    )
    for k in range(7):
        gradient = grads[k]
        means[k][...] = beta_one * firsts[k][...] + (1.0 - beta_one) * gradient
        squares[k][...] = beta_two * seconds[k][...] + (1.0 - beta_two) * gradient * gradient
        average = sums[k] * (1.0 / groups)
        velocity = outer_momentum * outers[k][...] + average
        velocities[k][...] = velocity
        updates[k][...] = weights[k][...] - outer_rate * (average + outer_momentum * velocity)


def finish(G, grads, sums, weights, firsts, seconds, outers):
    vm = pl.BlockSpec(memory_space=VMEM)
    shapes = tuple(jax.ShapeDtypeStruct(w.shape, F32) for w in weights) * 4
    return pl.pallas_call(
        functools.partial(finish_kernel, G),
        out_shape=shapes,
        in_specs=[vm] * 36,
        out_specs=(vm,) * 28,
        compiler_params=pltpu.CompilerParams(vmem_limit_bytes=60 << 20),
    )(*grads, *sums, *weights, *firsts, *seconds, *outers)


def per_device(
    G, DP, MP,
    patches, labels, partner, class_weight,
    embedding, mixing, expand, shrink, classifier, scales, shifts, *state,
):
    weights = (embedding, mixing[0], expand[0], shrink[0], classifier, scales, shifts)
    flat = lambda group, lead: tuple(a.reshape(w.shape) for a, w in zip(group, weights, strict=True))
    firsts, seconds, outers = flat(state[0:7], 0), flat(state[7:14], 0), flat(state[14:21], 0)
    ncls = classifier.shape[1]
    cpad = -(-ncls // LANE) * LANE
    padded = jnp.pad(class_weight.reshape(MP, ncls), ((0, 0), (0, cpad - ncls))).reshape(1, MP * cpad)
    rows, e_all, w1, w2, wc, small = move(
        G, MP, partner[0], patches[0], embedding, expand[0], shrink[0], classifier, scales, shifts
    )
    bundle, factors = local_step(
        MP, ncls, labels[0], partner[0], rows, e_all, w1, w2, wc, small, mixing[0], padded
    )
    *grads, sum_a, sum_c, info = gradient_sums(G, DP, MP, bundle, factors, weights, firsts, seconds)
    done = finish(G, grads, (sum_a, sum_c), weights, firsts, seconds, outers)
    updates, means, squares, velocities = (list(done[7 * k : 7 * k + 7]) for k in range(4))
    for k in (1, 2, 3):
        updates[k], velocities[k] = updates[k][None], velocities[k][None]
        means[k], squares[k] = means[k][None], squares[k][None]
    means = [a[None] for a in means]
    squares = [a[None] for a in squares]
    return (info[0:1, 0:2], info[0, 2:3], *updates, *means, *squares, *velocities)


WEIGHT_SPECS = (
    P("mp", None),
    P(),
    P(None, None, "mp"),
    P(None, "mp", None),
    P(None, "mp"),
    P(None, "mp"),
    P(None, "mp"),
)
STATE_SPECS = (
    P("group", "mp", None),
    P("group", None, None, None),
    P("group", None, None, "mp"),
    P("group", None, "mp", None),
    P("group", None, "mp"),
    P("group", None, "mp"),
    P("group", None, "mp"),
)


def solution(mesh):
    G, DP, MP = mesh.shape["group"], mesh.shape["dp"], mesh.shape["mp"]
    return jax.shard_map(
        functools.partial(per_device, G, DP, MP),
        mesh=mesh,
        in_specs=(
            P("group", "dp", None, "mp"),
            P("group", "dp"),
            P("group", "dp"),
            P(),
            *WEIGHT_SPECS,
            *STATE_SPECS,
            *STATE_SPECS,
            *WEIGHT_SPECS,
        ),
        out_specs=(
            P("group", None),
            P("group"),
            *WEIGHT_SPECS,
            *STATE_SPECS,
            *STATE_SPECS,
            *WEIGHT_SPECS,
        ),
        check_vma=False,
    )
```

time: 1640 us -> 388 us (0.24)
  waiting for transfers between devices: 1160 us -> 0 us
  Pallas kernels: 0 us -> 348 us
  local copies, waits for them, and re-layouts: 181 us -> 39 us
  other arithmetic: 104 us -> 0 us
  matrix products: 92.7 us -> 0 us
  blocking collectives: 69.2 us -> 0 us
  between operations: 23.4 us -> 0.88 us
    reduce_scatter x3 -> x0, waiting for transfers between devices: 704 us -> none  [the longest x1 245 us: per_device(): lax.psum_scatter(product(embed_table, pixel_rows, (0,), (1,)), 'mp', scat...]
    all_gather x3 -> x0, waiting for transfers between devices: 368 us -> none  [the longest x1 131 us: layer_forward(): ffn_whole = lax.all_gather(ffn_input, 'mp', axis=0, tiled=True)]
    pallas_call x0 -> x4, Pallas kernels: none -> 348 us  [the longest x1 168 us: gradient_sums(): pl.pallas_call(functools.partial(sum_kernel, G, DP, MP), out_shape=(s((we...]
    dot_general x14 -> x0, matrix products: 92.7 us -> none  [product(): lax.dot_general(first_operand, second_operand, ((left_dims, right_dims),...]
    psum x3 -> x0, waiting for transfers between devices: 92.2 us -> none  [the longest x1 47.3 us: per_device(): lax.psum((grad_embedding, grad_mixing, grad_expand, grad_shrink, grad_cla...]
    reshape x6 -> x1, local copies, waits for them, and re-layouts: 45.5 us -> 0.08 us  [per_device(): class_weight.reshape(MP, ncls)]
    all_gather x2 -> x0, blocking collectives: 43.6 us -> none  [the longest x1 29.5 us: per_device(): lax.all_gather(classifier.astype(jnp.bfloat16), 'mp', axis=1, tiled=True)]
    mul x5 -> x0, local copies, waits for them, and re-layouts: 41.9 us -> none  [the longest x2 22.6 us: per_device(): mix_share * images + (1.0 - mix_share) * images[pair_index]]
  transfers between devices with their start and end apart: 9 -> 0, of which waited for: 9 -> 0; matrix products, arithmetic and copies ran while one was open for 4% -> 0% of each run, Pallas kernels for 0% -> 0%
where the time goes in v1:
time: 388 us
  Pallas kernels  348 us (90%)
  local copies, waits for them, and re-layouts  39 us (10%)
    pallas_call x1, Pallas kernels, gradient_sums(): pl.pallas_call(functools.partial(sum_kernel, G, DP, MP), out_shape=(s((we...  168 us
    pallas_call x1, Pallas kernels, move(): pl.pallas_call(functools.partial(move_kernel, G, MP, NI), out_shape=(jax....  117 us
    pallas_call x1, Pallas kernels, local_step(): pl.pallas_call(functools.partial(step_kernel, MP, NI, ncls), out_shape=(j...  54.1 us
    unnamed x72, local copies, waits for them, and re-layouts  36.4 us
    pallas_call x1, Pallas kernels, finish(): pl.pallas_call(functools.partial(finish_kernel, G), out_shape=shapes, in_...  8.43 us

profile of v1, /device:TPU:0, one launch (start us, length us, event | category | flops | bytes accessed | tf_op | source)
XLA Modules:
  0.0 387.9 jit_solution(4310864120345448832)
XLA Ops:
  0.7 2.4 copy_bitcast_fusion
  3.0 11.4 %copy.62 = f32[1,48,196,192]{3,2,1,0:T(8,128)} copy(f32[1,48,196,192]{2,3,1,0:T(8,128)} %param.32) | data formatting | bytes 14450688 | tf_op args[0]
  14.4 117.4 %shard_map.535 = (bf16[4,6,3,208,128]{4,3,2,1,0:T(8,128)(2,1)}, bf16[4,192,384]{2,1,0:T(8,128)(2,1)}, bf16[384,1536]{1,0:T(8,128)(2,1)}, bf16[1536,384]{1,0:T(8,...) custom-call(s32[48]{0:T(128)} %bitcast.90, f32[48,196,192]{2,1,0:T(8,128)} %bitcast.62, f32[192,384]{1,0:T(8,128)} %refs_8_.1, ...), custom_call_target="tpu_custom_call" | custom-call | tf_op jit(solution)/shard_map/pallas_call | solution.py:190
  131.8 0.0 copy-done.11
  131.9 0.0 copy-done.12
  131.9 0.8 copy_bitcast_fusion.6
  132.6 0.0 copy-done.15
  132.6 0.1 reshape.117
  132.7 0.6 copy.91
  133.3 54.1 %shard_map.536 = (f32[4,672,384]{2,1,0:T(8,128)}, bf16[4,48,384]{2,1,0:T(8,128)(2,1)}) custom-call(s32[48]{0:T(128)} %bitcast.92, s32[48]{0:T(128)} %bitcast.91, bf16[4,6,3,208,128]{4,3,2,1,0:T(8,128)(2,1)} %get-tuple-element.75.rows, bf16[4,192,384]{2,1,0:T(8,128)(2,1)} %get-tuple-element.76.e_all, bf16[384,1536]{1,0:T(8,128)(2,1)} %get-tuple-element.77.w1, ...), custom_call_target="tpu_custom_call" | custom-call | tf_op jit(solution)/shard_map/pallas_call | solution.py:420
  187.5 0.0 copy-start.20
  187.5 0.0 copy-start.21
  187.5 0.0 copy-start.22
  187.5 0.0 copy-start.23
  187.5 0.0 copy-done.1
  187.5 0.0 copy-done.2
  187.5 1.1 copy_bitcast_fusion.1
  188.6 0.0 copy-done.5
  188.6 0.0 copy-done.6
  188.6 0.9 copy_bitcast_fusion.4
  189.6 0.0 copy-done.14
  189.6 0.8 copy_bitcast_fusion.7
  190.4 0.6 copy_bitcast_fusion.10
  191.0 0.0 copy-done.23
  191.0 0.6 copy_bitcast_fusion.12
  191.6 168.1 %shard_map.537 = (f32[192,384]{1,0:T(8,128)}, f32[224,256]{1,0:T(8,128)}, f32[392,384]{1,0:T(8,128)}, f32[384,384]{1,0:T(8,128)}, f32[392,256]{1,0:T(8,128)}, /*...) custom-call(f32[4,672,384]{2,1,0:T(8,128)} %get-tuple-element.81.bundle, ...), custom_call_target="tpu_custom_call" | custom-call | tf_op jit(solution)/shard_map/pallas_call | solution.py:645
  359.6 8.4 %shard_map.538 = (f32[192,384]{1,0:T(8,128)}, f32[196,197]{1,0:T(8,128)}, f32[385,384]{1,0:T(8,128)}, f32[384,384]{1,0:T(8,128)}, f32[385,250]{1,0:T(8,128)}, /*...) custom-call(f32[192,384]{1,0:T(8,128)} %get-tuple-element.84.refs_0_, ...), custom_call_target="tpu_custom_call" | custom-call | tf_op jit(solution)/shard_map/pallas_call | solution.py:719
  368.2 2.6 copy.64
  370.8 2.5 copy.66
  373.3 2.5 copy.71
  375.8 1.4 copy.76
  377.2 1.2 copy.67
  378.4 1.2 copy.72
  379.5 0.0 copy-done.10
  379.5 0.9 copy.63
  380.4 0.0 copy-done.9
  380.4 0.9 copy.65
  381.3 0.0 copy-done.8
  381.3 0.9 copy.70
  382.2 0.0 copy-done.7
  382.2 0.9 copy.75
  383.1 0.0 copy-done.19
  383.1 0.6 copy.68
  383.7 0.6 copy.69
  384.3 0.6 copy.73
  384.8 0.6 copy.74
  385.4 1.3 slice.7
  386.7 1.2 slice.6
  (31 shorter events, 0.1 us)
Async XLA Ops:
  14.4 117.5 %copy-start.11 = (f32[1,196,197]{2,0,1:T(1,128)S(1)}, f32[1,196,197]{2,0,1:T(1,128)}, u32[]{:S(2)}) copy-start(f32[1,196,197]{2,0,1:T(1,128)} %param.58) | copy-start | bytes 463348
  14.4 117.5 %copy-start.12 = (f32[1,196,197]{2,0,1:T(1,128)S(1)}, f32[1,196,197]{2,0,1:T(1,128)}, u32[]{:S(2)}) copy-start(f32[1,196,197]{2,0,1:T(1,128)} %param.37) | copy-start | bytes 463348
  14.4 118.3 %copy-start.15 = (f32[1000]{0:T(1024)S(1)}, f32[1000]{0:T(1024)}, u32[]{:S(2)}) copy-start(f32[1000]{0:T(1024)} %param.35) | copy-start | bytes 12004
  133.3 54.2 %copy-start.1 = (f32[1,1,385,384]{3,1,2,0:T(1,128)S(1)}, f32[1,1,385,384]{3,1,2,0:T(1,128)}, u32[]{:S(2)}) copy-start(f32[1,1,385,384]{3,1,2,0:T(1,128)} %param.52) | copy-start | bytes 1774084
  133.3 54.2 %copy-start.2 = (f32[1,1,385,384]{3,1,2,0:T(1,128)S(1)}, f32[1,1,385,384]{3,1,2,0:T(1,128)}, u32[]{:S(2)}) copy-start(f32[1,1,385,384]{3,1,2,0:T(1,128)} %param.45) | copy-start | bytes 1774084
  133.3 55.3 %copy-start.5 = (f32[1,385,250]{2,0,1:T(1,128)S(1)}, f32[1,385,250]{2,0,1:T(1,128)}, u32[]{:S(2)}) copy-start(f32[1,385,250]{2,0,1:T(1,128)} %param.54) | copy-start | bytes 1155004
  133.3 55.3 %copy-start.6 = (f32[1,385,250]{2,0,1:T(1,128)S(1)}, f32[1,385,250]{2,0,1:T(1,128)}, u32[]{:S(2)}) copy-start(f32[1,385,250]{2,0,1:T(1,128)} %param.47) | copy-start | bytes 1155004
  187.4 2.1 copy-start.13
  187.4 2.1 copy-start.14
  187.5 2.9 copy-start.20
  187.5 2.9 copy-start.21
  187.5 3.5 copy-start.22
  187.5 3.5 copy-start.23
  368.1 7.7 %copy-start = (f32[385,384]{1,0:T(8,128)S(1)}, f32[385,384]{1,0:T(8,128)}, u32[]{:S(2)}) copy-start(f32[385,384]{1,0:T(8,128)} %get-tuple-element.115) | copy-start | bytes 1774084
  368.1 9.1 %copy-start.4 = (f32[385,250]{1,0:T(8,128)S(1)}, f32[385,250]{1,0:T(8,128)}, u32[]{:S(2)}) copy-start(f32[385,250]{1,0:T(8,128)} %get-tuple-element.103) | copy-start | bytes 1155004
  368.1 10.3 %copy-start.3 = (f32[385,250]{1,0:T(8,128)S(1)}, f32[385,250]{1,0:T(8,128)}, u32[]{:S(2)}) copy-start(f32[385,250]{1,0:T(8,128)} %get-tuple-element.110) | copy-start | bytes 1155004
  368.1 11.4 %copy-start.10 = (f32[196,197]{1,0:T(8,128)S(1)}, f32[196,197]{1,0:T(8,128)}, u32[]{:S(2)}) copy-start(f32[196,197]{1,0:T(8,128)} %get-tuple-element.93) | copy-start | bytes 463348
  368.1 12.3 %copy-start.9 = (f32[196,197]{1,0:T(8,128)S(1)}, f32[196,197]{1,0:T(8,128)}, u32[]{:S(2)}) copy-start(f32[196,197]{1,0:T(8,128)} %get-tuple-element.100) | copy-start | bytes 463348
  368.1 13.2 %copy-start.8 = (f32[196,197]{1,0:T(8,128)S(1)}, f32[196,197]{1,0:T(8,128)}, u32[]{:S(2)}) copy-start(f32[196,197]{1,0:T(8,128)} %get-tuple-element.107) | copy-start | bytes 463348
  368.1 14.1 %copy-start.7 = (f32[196,197]{1,0:T(8,128)S(1)}, f32[196,197]{1,0:T(8,128)}, u32[]{:S(2)}) copy-start(f32[196,197]{1,0:T(8,128)} %get-tuple-element.114) | copy-start | bytes 463348
  368.1 14.9 %copy-start.19 = (f32[5,96]{1,0:T(8,128)S(1)}, f32[5,96]{1,0:T(8,128)}, u32[]{:S(2)}) copy-start(f32[5,96]{1,0:T(8,128)} %get-tuple-element.104) | copy-start | bytes 5764
  368.2 15.5 %copy-start.18 = (f32[5,96]{1,0:T(8,128)S(1)}, f32[5,96]{1,0:T(8,128)}, u32[]{:S(2)}) copy-start(f32[5,96]{1,0:T(8,128)} %get-tuple-element.105) | copy-start | bytes 5764
  368.2 16.1 %copy-start.17 = (f32[5,96]{1,0:T(8,128)S(1)}, f32[5,96]{1,0:T(8,128)}, u32[]{:S(2)}) copy-start(f32[5,96]{1,0:T(8,128)} %get-tuple-element.111) | copy-start | bytes 5764
  368.2 16.7 %copy-start.16 = (f32[5,96]{1,0:T(8,128)S(1)}, f32[5,96]{1,0:T(8,128)}, u32[]{:S(2)}) copy-start(f32[5,96]{1,0:T(8,128)} %get-tuple-element.112) | copy-start | bytes 5764

commit v2 on v1

--- a/solution.py
+++ b/solution.py
@@ -34,9 +34,8 @@
 GELU_A = 0.7978845608028654
 GELU_B = GELU_A * 0.044715
 
-B_EXP, B_EMB, B_MIX, B_SMALL, B_ACT, B_ROWS = 0, 392, 584, 640, 656, 672
-MIX_BLOCK = 56
-A_EMB, A_EXP, A_SHR, A_ROWS = 0, 192, 584, 976
+S_VEC, S_ROWS = 56, 72
+A_EMB, A_EXP, A_SHR, A_ROWS = 0, 192, 584, 992
 C_CLS, C_MIX, C_SCA, C_SHI, C_ROWS = 0, 392, 592, 600, 624
 
 
@@ -219,7 +218,7 @@
 def step_kernel(
     MP, NI, ncls,
     labels, partner, rows, e_all, w1, w2, wc, small, mixing, class_weight,
-    bundle, factors,
+    big, sm, acts, factors,
     xs, gp, s0, s1, mx, mi, fi, ep, mm, mt, mbias, vec, b1, asum, s1sum, la, lb,
     dact, ds2, dh, csum, gw, ge, gm, gmb, gvec,
 ):
@@ -394,22 +393,31 @@
     grad = jnp.concatenate([gm[...], jnp.zeros((ROWS, 256 - ROWS), F32)], axis=1)
     grad = jnp.where(column < PATCHES, grad, jnp.where(column == PATCHES, bias_grad, 0.0))
     grad = jnp.where(row < PATCHES, grad, 0.0)
+    half = er - LANE
+    own = D // MP
+    lane = lax.broadcasted_iota(jnp.int32, (16, LANE), 1)
     for t in range(MP):
-        bundle[t, B_EXP : B_EXP + D, :] = gw[:, t * hid : (t + 1) * hid]
-        bundle[t, B_EXP + D : B_EMB, :] = jnp.concatenate(
-            [csum[:, t * hid : (t + 1) * hid], jnp.zeros((B_EMB - B_EXP - D - 1, hid), F32)], axis=0
-        )
-        bundle[t, B_EMB : B_EMB + LANE, :] = ge[t * LANE : (t + 1) * LANE, :]
-        half = er - LANE
-        bundle[t, B_EMB + LANE : B_EMB + er, :] = ge[MP * LANE + t * half : MP * LANE + (t + 1) * half, :]
-        bundle[t, B_MIX:B_SMALL, :] = jnp.zeros((MIX_BLOCK, D), F32)
-        n = min(MIX_BLOCK, ROWS - t * MIX_BLOCK)
-        bundle[t, B_MIX : B_MIX + n, 0:256] = grad[t * MIX_BLOCK : t * MIX_BLOCK + n]
-        bundle[t, B_SMALL:B_ACT, :] = gvec[...]
-        bundle[t, B_ACT:B_ROWS, :] = asum[:, t * hid : (t + 1) * hid]
-
-
-def local_step(MP, ncls, labels, partner, rows, e_all, w1, w2, wc, small, mixing, class_weight):
+        big[t, 0:D, :] = gw[:, t * hid : (t + 1) * hid]
+        big[t, D : D + LANE, :] = ge[t * LANE : (t + 1) * LANE, :]
+        big[t, D + LANE : D + er, :] = ge[MP * LANE + t * half : MP * LANE + (t + 1) * half, :]
+        if D + er < big.shape[1]:
+            big[t, D + er :, :] = jnp.zeros((big.shape[1] - D - er, D), F32)
+        sm[t, 0:S_VEC, :] = jnp.zeros((S_VEC, 256), F32)
+        n = min(S_VEC, ROWS - t * S_VEC)
+        sm[t, 0:n, :] = grad[t * S_VEC : t * S_VEC + n]
+        vector = gvec[...]
+        if t:
+            vector = pltpu.roll(vector, D - t * own, 1)
+        sm[t, S_VEC:S_ROWS, 0:LANE] = jnp.where(lane < own, vector[:, 0:LANE], 0.0)
+        sm[t, S_VEC:S_ROWS, LANE:] = jnp.zeros((16, LANE), F32)
+        sm[t, S_VEC + 10 : S_VEC + 11, 0:LANE] = gvec[10:11, 0:LANE]
+        for k in range(hid // LANE):
+            at = t * hid + k * LANE
+            sm[t, S_VEC + 11 + k : S_VEC + 12 + k, 0:LANE] = csum[:, at : at + LANE]
+        acts[t] = asum[:, t * hid : (t + 1) * hid]
+
+
+def local_step(DP, MP, ncls, labels, partner, rows, e_all, w1, w2, wc, small, mixing, class_weight):
     NP = rows.shape[1]
     NI = 2 * NP
     PR = 2 * ROWS
@@ -420,11 +428,13 @@
     return pl.pallas_call(
         functools.partial(step_kernel, MP, NI, ncls),
         out_shape=(
-            jax.ShapeDtypeStruct((MP, B_ROWS, D), F32),
+            jax.ShapeDtypeStruct((MP, DP * part_rows(DP, e_all.shape[1]), D), F32),
+            jax.ShapeDtypeStruct((MP, S_ROWS, 256), F32),
+            jax.ShapeDtypeStruct((MP, 16, hid_all // MP), F32),
             jax.ShapeDtypeStruct((MP, 48, D), BF16),
         ),
         in_specs=[sm, sm] + [vm] * 8,
-        out_specs=(vm, vm),
+        out_specs=(vm,) * 4,
         scratch_shapes=[
             VMEM((NP, PR, pd), BF16),
             VMEM((NP, PR, hid_all), F32),
@@ -457,28 +467,38 @@
     )(labels, partner, rows, e_all, w1, w2, wc, small, mixing, class_weight)
 
 
+def part_rows(DP, er):
+    return -(-(D + er) // (16 * DP)) * 16
+
+
 def adamw(weight, gradient, moment_one, moment_two, rate):
     mean_new = beta_one * moment_one + (1.0 - beta_one) * gradient
     square_new = beta_two * moment_two + (1.0 - beta_two) * gradient * gradient
     mean_hat = mean_new * (1.0 / (1.0 - beta_one**STEP))
     square_hat = square_new * (1.0 / (1.0 - beta_two**STEP))
-    moved = rate * (mean_hat / (jnp.sqrt(square_hat) + adam_eps) + weight_decay * weight)
-    return moved, mean_new, square_new
-
-
-def sum_kernel(
-    G, DP, MP,
-    bundle, factors,
-    emb, mixing, expa, shr, cls, sca, shi,
-    emb1, mixing1, expa1, shr1, cls1, sca1, shi1,
-    emb2, mixing2, expa2, shr2, cls2, sca2, shi2,
-    g_emb, g_mix, g_exp, g_shr, g_cls, g_vec, sum_a, sum_c, info,
-    rb, rc, yb, yc, nz, mva, mvc, h1a, h1c, h2a, h2c,
-    zs, zr, ys, yr, ns, nr, gs, gr,
-):
+    return rate * (mean_hat / (jnp.sqrt(square_hat) + adam_eps) + weight_decay * weight)
+
+
+def flat(ref):
+    return ref.at[:, 0, :] if len(ref.shape) == 3 else ref
+
+
+def sum_kernel(G, DP, MP, big, sm, acts, fac, *refs):
+    states, refs = refs[:21], refs[21:]
+    (g_big, g_mix, g_shr, g_cls, g_vec, sum_a, sum_c, info), refs = refs[:8], refs[8:]
+    held, refs = refs[:21], refs[21:]
+    (
+        ys16, yr16, zs16, zr16, zsm, zacts, zfac, ysm, yacts, yfac, nmix, nsq,
+        mva, mvc, h1a, h1c, h2a, h2c,
+        y_s, y_r, z_s, z_r, zf_s, zf_r, yf_s, yf_r, ag_s, ag_r, nm_s, nm_r, g_s, g_r, load,
+    ) = refs
     z = lax.axis_index("mp")
     y = lax.axis_index("dp")
     g = lax.axis_index("group")
+    HR = g_big.shape[0] // DP
+    loads = [pltpu.make_async_copy(flat(a), b, load.at[k]) for k, (a, b) in enumerate(zip(states, held, strict=True))]
+    for c in loads:
+        c.start()
     zpeer = [lax.rem(z + d, MP) for d in range(1, MP)]
     ypeer = [lax.rem(y + d, DP) for d in range(1, DP)]
     gstep = []
@@ -495,76 +515,112 @@
         c.start()
         started.append(c)
 
-    for d, t in enumerate(zpeer):
-        go(factors.at[t], rc.at[z], zs.at[d, 0], zr.at[z, 0], {"mp": t})
-        go(bundle.at[t], rb.at[z], zs.at[d, 1], zr.at[z, 1], {"mp": t})
-    rc[z] = factors[z]
-    rb[z, B_SMALL:, :] = bundle[z, B_SMALL:, :]
-    for t in zpeer:
-        remote(factors.at[t], rc.at[t], zs.at[0, 0], zr.at[t, 0], {"mp": t}).wait_recv()
-        remote(bundle.at[t], rb.at[t], zs.at[0, 1], zr.at[t, 1], {"mp": t}).wait_recv()
-
-    total = bundle[z, 0:B_SMALL, :]
-    for t in zpeer:
-        total = total + rb[t, 0:B_SMALL, :]
-    yb[y, 0:B_SMALL, :] = total
-    vector = rb[0, B_SMALL:B_ACT, :]
-    for t in range(1, MP):
-        vector = vector + rb[t, B_SMALL:B_ACT, :]
-    yb[y, B_SMALL:B_ACT, :] = vector
-    for t in range(MP):
-        yb[y, B_ACT + 16 * t : B_ACT + 16 * (t + 1), :] = rb[t, B_ACT:B_ROWS, :]
-        for k in range(3):
-            at = (k * MP + t) * 16
-            yc[y, at : at + 16, :] = rc[t, 16 * k : 16 * (k + 1), :]
-    for d, t in enumerate(ypeer):
-        go(yb.at[y], yb.at[y], ys.at[d, 0], yr.at[y, 0], {"dp": t})
-        go(yc.at[y], yc.at[y], ys.at[d, 1], yr.at[y, 1], {"dp": t})
-    for t in ypeer:
-        remote(yb.at[t], yb.at[t], ys.at[0, 0], yr.at[t, 0], {"dp": t}).wait_recv()
-        remote(yc.at[t], yc.at[t], ys.at[0, 1], yr.at[t, 1], {"dp": t}).wait_recv()
-
-    def over_dp(lo, hi):
-        value = yb[0, lo:hi, :]
-        for t in range(1, DP):
-            value = value + yb[t, lo:hi, :]
-        return value
-
+    def arrived(dst, sem, peer):
+        remote(dst, dst, sem, sem, peer).wait_recv()
+
+    def mine(k):
+        return pl.ds(pl.multiple_of(k * HR, 8), HR)
+
+    order = zpeer + [z]
+    for i, t in enumerate(order):
+        for d, u in enumerate(ypeer):
+            ys16[i, d] = big[t, mine(u), :].astype(BF16)
+            go(ys16.at[i, d], yr16.at[t, y], y_s.at[i, d], y_r.at[t, y], {"dp": u})
+        if i == 0:
+            for d, v in enumerate(zpeer):
+                go(acts.at[v], zacts.at[z], zf_s.at[d, 0], zf_r.at[z, 0], {"mp": v})
+                go(fac.at[v], zfac.at[z], zf_s.at[d, 1], zf_r.at[z, 1], {"mp": v})
+                go(sm.at[v], zsm.at[z], zf_s.at[d, 2], zf_r.at[z, 2], {"mp": v})
+    zacts[z] = acts[z]
+    zfac[z] = fac[z]
+    zsm[z] = sm[z]
+    own = None
+    for i, t in enumerate(order):
+        part = big[t, mine(y), :]
+        for u in ypeer:
+            arrived(yr16.at[t, u], y_r.at[t, u], {"dp": u})
+            part = part + yr16[t, u].astype(F32)
+        if i < MP - 1:
+            zs16[i] = part.astype(BF16)
+            go(zs16.at[i], zr16.at[z], z_s.at[i], z_r.at[z], {"mp": t})
+        else:
+            g_big[mine(y), :] = part
+
+    for v in zpeer:
+        arrived(zacts.at[v], zf_r.at[v, 0], {"mp": v})
+        arrived(zfac.at[v], zf_r.at[v, 1], {"mp": v})
+        arrived(zsm.at[v], zf_r.at[v, 2], {"mp": v})
+    small = zsm[0]
+    for v in range(1, MP):
+        small = small + zsm[v]
+    ysm[y] = small
+    yacts[y] = zacts[...]
+    yfac[y] = zfac[...]
+    for d, u in enumerate(ypeer):
+        go(ysm.at[y], ysm.at[y], yf_s.at[d, 0], yf_r.at[y, 0], {"dp": u})
+        go(yacts.at[y], yacts.at[y], yf_s.at[d, 1], yf_r.at[y, 1], {"dp": u})
+        go(yfac.at[y], yfac.at[y], yf_s.at[d, 2], yf_r.at[y, 2], {"dp": u})
+
+    total = g_big[mine(y), :]
+    for v in zpeer:
+        arrived(zr16.at[v], z_r.at[v], {"mp": v})
+        total = total + zr16[v].astype(F32)
+    g_big[mine(y), :] = total
+    shared = []
+    for d, u in enumerate(ypeer):
+        c = remote(g_big.at[mine(y), :], g_big.at[mine(y), :], ag_s.at[d], ag_r.at[y], {"dp": u})
+        c.start()
+        shared.append(c)
+
+    for u in ypeer:
+        arrived(ysm.at[u], yf_r.at[u, 0], {"dp": u})
+    small = ysm[0]
+    for u in range(1, DP):
+        small = small + ysm[u]
+    nmix[z] = small[0:S_VEC]
+    for d, v in enumerate(zpeer):
+        go(nmix.at[z], nmix.at[z], nm_s.at[d, 0], nm_r.at[z, 0], {"mp": v})
+    for u in ypeer:
+        arrived(yacts.at[u], yf_r.at[u, 1], {"dp": u})
+        arrived(yfac.at[u], yf_r.at[u, 2], {"dp": u})
+
+    cpad = g_cls.shape[1]
     n = 16 * MP
-    cpad = g_cls.shape[1]
     grad_shr = jnp.zeros((D, D), F32)
     grad_cls = jnp.zeros((D, cpad), F32)
     cls_bias = jnp.zeros((1, cpad), F32)
-    for t in range(DP):
-        acts = yb[t, B_ACT : B_ACT + n, :]
-        dout, pooled, dlog = yc[t, 0:n, :], yc[t, n : 2 * n, :], yc[t, 2 * n : 3 * n, 0:cpad]
-        grad_shr = grad_shr + exact(acts, dout.astype(F32), ((0,), (0,)))
+    for u in range(DP):
+        whole = yfac[u]
+        dout = whole[:, 0:16, :].reshape(n, D)
+        pooled = whole[:, 16:32, :].reshape(n, D)
+        dlog = whole[:, 32:48, 0:cpad].reshape(n, cpad)
+        grad_shr = grad_shr + exact(yacts[u].reshape(n, D), dout.astype(F32), ((0,), (0,)))
         grad_cls = grad_cls + dot(pooled, dlog, ((0,), (0,)))
         cls_bias = cls_bias + jnp.sum(dlog.astype(F32), axis=0, keepdims=True)
     g_shr[...] = grad_shr
     g_cls[0:D, :] = grad_cls
     g_cls[D:, :] = jnp.concatenate([cls_bias, jnp.zeros((g_cls.shape[0] - D - 1, cpad), F32)], axis=0)
-    g_exp[...] = over_dp(B_EXP, B_EMB)
-    g_emb[...] = over_dp(B_EMB, B_MIX)
-    vector = over_dp(B_SMALL, B_ACT)
-    mix = over_dp(B_MIX, B_SMALL)[:, 0:256]
 
     def squares(v):
-        return jnp.sum(jnp.sum(v * v, axis=1, keepdims=True), axis=0, keepdims=True)
-
-    part = (
-        squares(g_exp[...]) + squares(g_emb[...]) + squares(g_shr[...]) + squares(g_cls[...]) + squares(mix)
-    )
-    nz[z, 0:MIX_BLOCK, :] = mix
-    nz[z, MIX_BLOCK:, :] = jnp.broadcast_to(part, (8, 256))
-    for d, t in enumerate(zpeer):
-        go(nz.at[z], nz.at[z], ns.at[d], nr.at[z], {"mp": t})
-    for t in zpeer:
-        remote(nz.at[t], nz.at[t], ns.at[0], nr.at[t], {"mp": t}).wait_recv()
-    square = nz[0, MIX_BLOCK : MIX_BLOCK + 1, 0:1]
-    for t in range(1, MP):
-        square = square + nz[t, MIX_BLOCK : MIX_BLOCK + 1, 0:1]
-    square = square + squares(vector[0:10])
+        return jnp.sum(jnp.sum(v * v, axis=0, keepdims=True), axis=1, keepdims=True)
+
+    vector = small[S_VEC:S_ROWS, 0:LANE]
+    part = squares(g_shr[...]) + squares(g_cls[...]) + squares(small[0:S_VEC])
+    part = part + squares(vector[0:10]) + squares(vector[11:14])
+    for u in ypeer:
+        arrived(g_big.at[mine(u), :], ag_r.at[u], {"dp": u})
+    part = part + squares(g_big[...])
+    nsq[z] = jnp.broadcast_to(part, (8, LANE))
+    for d, v in enumerate(zpeer):
+        go(nsq.at[z], nsq.at[z], nm_s.at[d, 1], nm_r.at[z, 1], {"mp": v})
+    for c in loads:
+        c.wait()
+    for v in zpeer:
+        arrived(nmix.at[v], nm_r.at[v, 0], {"mp": v})
+        arrived(nsq.at[v], nm_r.at[v, 1], {"mp": v})
+    square = nsq[0, 0:1, 0:1]
+    for v in range(1, MP):
+        square = square + nsq[v, 0:1, 0:1]
     loss_sum = vector[10:11, 0:1]
     weight_total = vector[10:11, 1:2]
     size = jnp.sqrt(square) / weight_total
@@ -573,81 +629,90 @@
     lane = lax.broadcasted_iota(jnp.int32, (8, LANE), 1)
     info[...] = jnp.where(lane == 0, loss_sum, jnp.where(lane == 1, weight_total, size))
 
-    g_exp[...] = g_exp[...] * scaled
-    g_emb[...] = g_emb[...] * scaled
+    (emb, mixing, expa, shr, cls, sca, shi) = held[:7]
+    (emb1, mixing1, expa1, shr1, cls1, sca1, shi1) = held[7:14]
+    (emb2, mixing2, expa2, shr2, cls2, sca2, shi2) = held[14:21]
+    er, ncls, wide = emb.shape[0], cls.shape[1], sca.shape[1]
+    for c in shared:
+        c.wait_send()
+    g_big[...] = g_big[...] * scaled
     g_shr[...] = g_shr[...] * scaled
     g_cls[...] = g_cls[...] * scaled
+    g_vec[...] = vector * scaled
     for t in range(MP):
-        g_mix[t * MIX_BLOCK : (t + 1) * MIX_BLOCK, :] = nz[t, 0:MIX_BLOCK, :] * scaled
-    own = D // MP
-    g_vec[...] = pltpu.roll(vector, lax.rem((MP - z) * own, D), 1)[:, 0:LANE] * scaled
-
-    ncls = cls.shape[1]
+        g_mix[t * S_VEC : (t + 1) * S_VEC, :] = nmix[t] * scaled
+    bias = jnp.concatenate([g_vec[11 + k : 12 + k, :] for k in range(D // LANE)], axis=1)
+    mva[A_EMB : A_EMB + er, :] = adamw(emb[...], g_big[D : D + er, :], emb1[...], emb2[...], matrix_rate)
+    mva[A_EXP : A_EXP + D, :] = adamw(expa[0:D, :], g_big[0:D, :], expa1[0:D, :], expa2[0:D, :], matrix_rate)
     mva[A_EXP + D : A_SHR, :] = jnp.zeros((A_SHR - A_EXP - D, D), F32)
+    last = slice(D, D + 1)
+    mva[A_EXP + D : A_EXP + D + 1, :] = adamw(expa[last, :], bias, expa1[last, :], expa2[last, :], matrix_rate)
+    mva[A_SHR : A_SHR + D, :] = adamw(shr[...], g_shr[...], shr1[...], shr2[...], matrix_rate)
     mva[A_SHR + D :, :] = jnp.zeros((A_ROWS - A_SHR - D, D), F32)
+    ha, hc = A_ROWS // 2, C_ROWS // 2
+
+    def half(ref, k, n):
+        return ref.at[pl.ds(pl.multiple_of(k * n, 8), n), :]
+
+    if G > 1:
+        core, other = lax.rem(g, 2), 1 - lax.rem(g, 2)
+        near = {"group": gstep[0]}
+        go(half(mva, other, ha), h1a, g_s.at[0], g_r.at[0], near)
     mvc[...] = jnp.zeros_like(mvc)
-    mva[A_EMB : A_EMB + emb.shape[0], :] = adamw(emb[...], g_emb[...], emb1[...], emb2[...], matrix_rate)[0]
-    mva[A_EXP : A_EXP + D + 1, :] = adamw(expa[...], g_exp[0 : D + 1, :], expa1[...], expa2[...], matrix_rate)[0]
-    mva[A_SHR : A_SHR + shr.shape[0], :] = adamw(shr[...], g_shr[...], shr1[...], shr2[...], matrix_rate)[0]
-    mvc[C_CLS : C_CLS + D + 1, 0:ncls] = adamw(cls[...], g_cls[0 : D + 1, 0:ncls], cls1[...], cls2[...], head_rate)[0]
+    mvc[C_CLS : C_CLS + D + 1, 0:ncls] = adamw(cls[...], g_cls[0 : D + 1, 0:ncls], cls1[...], cls2[...], head_rate)
     mvc[C_MIX : C_MIX + PATCHES, 0 : PATCHES + 1] = adamw(
         mixing[...], g_mix[0:PATCHES, 0 : PATCHES + 1], mixing1[...], mixing2[...], matrix_rate
-    )[0]
-    mvc[C_SCA : C_SCA + 5, 0:own] = adamw(sca[...], g_vec[0:5, 0:own], sca1[...], sca2[...], vector_rate)[0]
-    mvc[C_SHI : C_SHI + 5, 0:own] = adamw(shi[...], g_vec[5:10, 0:own], shi1[...], shi2[...], vector_rate)[0]
+    )
+    mvc[C_SCA : C_SCA + 5, 0:wide] = adamw(sca[...], g_vec[0:5, 0:wide], sca1[...], sca2[...], vector_rate)
+    mvc[C_SHI : C_SHI + 5, 0:wide] = adamw(shi[...], g_vec[5:10, 0:wide], shi1[...], shi2[...], vector_rate)
 
     if G == 1:
         sum_a[...] = mva[...]
         sum_c[...] = mvc[...]
     else:
-        ha, hc = A_ROWS // 2, C_ROWS // 2
-        mine, theirs = lax.rem(g, 2), 1 - lax.rem(g, 2)
-
-        def half(ref, k, n):
-            return ref.at[pl.ds(pl.multiple_of(k * n, 8), n), :]
-
-        peer = {"group": gstep[0]}
-        go(half(mva, theirs, ha), h1a, gs.at[0], gr.at[0], peer)
-        go(half(mvc, theirs, hc), h1c, gs.at[1], gr.at[1], peer)
-        remote(h1a, h1a, gs.at[0], gr.at[0], peer).wait_recv()
-        remote(h1c, h1c, gs.at[1], gr.at[1], peer).wait_recv()
-        own_a = pl.ds(pl.multiple_of(mine * ha, 8), ha)
-        own_c = pl.ds(pl.multiple_of(mine * hc, 8), hc)
+        go(half(mvc, other, hc), h1c, g_s.at[1], g_r.at[1], near)
+        own_a = pl.ds(pl.multiple_of(core * ha, 8), ha)
+        own_c = pl.ds(pl.multiple_of(core * hc, 8), hc)
+        far = {"group": gstep[-1]}
+        arrived(h1a, g_r.at[0], near)
         pa = mva[own_a, :] + h1a[...]
+        if G > 2:
+            h2a[0] = pa.astype(BF16)
+            go(h2a.at[0], h2a.at[1], g_s.at[2], g_r.at[2], far)
+        arrived(h1c, g_r.at[1], near)
         pc = mvc[own_c, :] + h1c[...]
         if G > 2:
-            h2a[0] = pa
             h2c[0] = pc
-            far = {"group": gstep[1]}
-            go(h2a.at[0], h2a.at[1], gs.at[2], gr.at[2], far)
-            go(h2c.at[0], h2c.at[1], gs.at[3], gr.at[3], far)
-            remote(h2a.at[0], h2a.at[1], gs.at[2], gr.at[2], far).wait_recv()
-            remote(h2c.at[0], h2c.at[1], gs.at[3], gr.at[3], far).wait_recv()
-            pa = h2a[0] + h2a[1]
+            go(h2c.at[0], h2c.at[1], g_s.at[3], g_r.at[3], far)
+            arrived(h2a.at[1], g_r.at[2], far)
+            pa = h2a[0].astype(F32) + h2a[1].astype(F32)
+        sum_a[own_a, :] = pa
+        go(half(sum_a, core, ha), half(sum_a, core, ha), g_s.at[4], g_r.at[4], near)
+        if G > 2:
+            arrived(h2c.at[1], g_r.at[3], far)
             pc = h2c[0] + h2c[1]
-        sum_a[own_a, :] = pa
         sum_c[own_c, :] = pc
-        go(half(sum_a, mine, ha), half(sum_a, mine, ha), gs.at[4], gr.at[4], peer)
-        go(half(sum_c, mine, hc), half(sum_c, mine, hc), gs.at[5], gr.at[5], peer)
-        remote(h1a, half(sum_a, theirs, ha), gs.at[4], gr.at[4], peer).wait_recv()
-        remote(h1c, half(sum_c, theirs, hc), gs.at[5], gr.at[5], peer).wait_recv()
+        go(half(sum_c, core, hc), half(sum_c, core, hc), g_s.at[5], g_r.at[5], near)
+        arrived(half(sum_a, other, ha), g_r.at[4], near)
+        arrived(half(sum_c, other, hc), g_r.at[5], near)
 
     for c in started:
         c.wait_send()
 
 
-def gradient_sums(G, DP, MP, bundle, factors, weights, firsts, seconds):
+def gradient_sums(G, DP, MP, big, sm, acts, fac, shapes, states):
     dma = pltpu.SemaphoreType.DMA
     vm = pl.BlockSpec(memory_space=VMEM)
-    cpad = -(-weights[4].shape[1] // LANE) * LANE
+    hbm = pl.BlockSpec(memory_space=pl.ANY)
+    cpad = -(-shapes[4][1] // LANE) * LANE
     s = jax.ShapeDtypeStruct
-    rows_y = B_ACT + 16 * MP
+    HR = big.shape[1] // DP
+    dp1 = max(DP - 1, 1)
     return pl.pallas_call(
         functools.partial(sum_kernel, G, DP, MP),
         out_shape=(
-            s((weights[0].shape[0], D), F32),
-            s((MP * MIX_BLOCK, 256), F32),
-            s((B_EMB, D), F32),
+            s((DP * HR, D), F32),
+            s((MP * S_VEC, 256), F32),
             s((D, D), F32),
             s((392, cpad), F32),
             s((16, LANE), F32),
@@ -655,74 +720,124 @@
             s((C_ROWS, 256), F32),
             s((8, LANE), F32),
         ),
-        in_specs=[vm] * 23,
-        out_specs=(vm,) * 9,
-        scratch_shapes=[
-            VMEM((MP, B_ROWS, D), F32),
+        in_specs=[vm] * 4 + [hbm] * 21,
+        out_specs=(vm,) * 8,
+        scratch_shapes=[VMEM(shape, F32) for shape in shapes] * 3
+        + [
+            VMEM((MP, dp1, HR, D), BF16),
+            VMEM((MP, DP, HR, D), BF16),
+            VMEM((MP - 1, HR, D), BF16),
+            VMEM((MP, HR, D), BF16),
+            VMEM((MP, S_ROWS, 256), F32),
+            VMEM((MP, 16, D), F32),
             VMEM((MP, 48, D), BF16),
-            VMEM((DP, rows_y, D), F32),
-            VMEM((DP, 48 * MP, D), BF16),
-            VMEM((MP, MIX_BLOCK + 8, 256), F32),
+            VMEM((DP, S_ROWS, 256), F32),
+            VMEM((DP, MP, 16, D), F32),
+            VMEM((DP, MP, 48, D), BF16),
+            VMEM((MP, S_VEC, 256), F32),
+            VMEM((MP, 8, LANE), F32),
             VMEM((A_ROWS, D), F32),
             VMEM((C_ROWS, 256), F32),
             VMEM((A_ROWS // 2, D), F32),
             VMEM((C_ROWS // 2, 256), F32),
-            VMEM((2, A_ROWS // 2, D), F32),
+            VMEM((2, A_ROWS // 2, D), BF16),
             VMEM((2, C_ROWS // 2, 256), F32),
+            dma((MP, dp1)),
+            dma((MP, DP)),
+            dma((MP - 1,)),
+            dma((MP,)),
+            dma((MP - 1, 3)),
+            dma((MP, 3)),
+            dma((dp1, 3)),
+            dma((DP, 3)),
+            dma((dp1,)),
+            dma((DP,)),
             dma((MP - 1, 2)),
             dma((MP, 2)),
-            dma((max(DP - 1, 1), 2)),
-            dma((DP, 2)),
-            dma((MP - 1,)),
-            dma((MP,)),
             dma((6,)),
             dma((6,)),
+            dma((21,)),
         ],
         compiler_params=pltpu.CompilerParams(
-            collective_id=1, has_side_effects=True, vmem_limit_bytes=60 << 20
+            collective_id=1, has_side_effects=True, vmem_limit_bytes=62 << 20
         ),
-    )(bundle, factors, *weights, *firsts, *seconds)
+    )(big, sm, acts, fac, *states)
 
 
 def finish_kernel(groups, *refs):
-    g_emb, g_mix, g_exp, g_shr, g_cls, g_vec, sum_a, sum_c = refs[:8]
-    weights, firsts, seconds, outers = (refs[8 + 7 * k : 15 + 7 * k] for k in range(4))
-    updates, means, squares, velocities = (refs[36 + 7 * k : 43 + 7 * k] for k in range(4))
-    own = weights[5].shape[1]
-    ncls = weights[4].shape[1]
-    grads = (
-        g_emb[...], g_mix[0:PATCHES, 0 : PATCHES + 1], g_exp[0 : D + 1, :], g_shr[...],
-        g_cls[0 : D + 1, 0:ncls], g_vec[0:5, 0:own], g_vec[5:10, 0:own],
+    (info, *grads_in), refs = refs[:8], refs[8:]
+    states, refs = refs[:28], refs[28:]
+    (losses, norm), refs = refs[:2], refs[2:]
+    outs, refs = refs[:28], refs[28:]
+    grads_held, refs = refs[:7], refs[7:]
+    held, refs = refs[:28], refs[28:]
+    new, (load, load_grad, save) = refs[:28], refs[28:]
+    first = [pltpu.make_async_copy(a, b, load_grad.at[k]) for k, (a, b) in enumerate(zip(grads_in, grads_held, strict=True))]
+    loads = [pltpu.make_async_copy(flat(a), b, load.at[k]) for k, (a, b) in enumerate(zip(states, held, strict=True))]
+    saves = [pltpu.make_async_copy(a, flat(b), save.at[k]) for k, (a, b) in enumerate(zip(new, outs, strict=True))]
+    for c in first:
+        c.start()
+    for k in (3, 2, 0, 4, 1, 5, 6):
+        for j in range(4):
+            loads[7 * j + k].start()
+    losses[...] = info[0:1, 0:2]
+    norm[...] = info[0:1, 2:3]
+    g_big, g_mix, g_shr, g_cls, g_vec, sum_a, sum_c = grads_held
+    for c in first:
+        c.wait()
+    wide = held[5].shape[1]
+    ncls = held[4].shape[1]
+    er = held[0].shape[0]
+    all_rows = slice(None)
+    bias = jnp.concatenate([g_vec[11 + k : 12 + k, :] for k in range(D // LANE)], axis=1)
+    work = (
+        (3, all_rows, lambda: g_shr[...], lambda: sum_a[A_SHR : A_SHR + D, :]),
+        (2, slice(0, D), lambda: g_big[0:D, :], lambda: sum_a[A_EXP : A_EXP + D, :]),
+        (2, slice(D, D + 1), lambda: bias, lambda: sum_a[A_EXP + D : A_EXP + D + 1, :]),
+        (0, all_rows, lambda: g_big[D : D + er, :], lambda: sum_a[A_EMB : A_EMB + er, :]),
+        (4, all_rows, lambda: g_cls[0 : D + 1, 0:ncls], lambda: sum_c[C_CLS : C_CLS + D + 1, 0:ncls]),
+        (1, all_rows, lambda: g_mix[0:PATCHES, 0 : PATCHES + 1], lambda: sum_c[C_MIX : C_MIX + PATCHES, 0 : PATCHES + 1]),
+        (5, all_rows, lambda: g_vec[0:5, 0:wide], lambda: sum_c[C_SCA : C_SCA + 5, 0:wide]),
+        (6, all_rows, lambda: g_vec[5:10, 0:wide], lambda: sum_c[C_SHI : C_SHI + 5, 0:wide]),
     )
-    sums = (
-        sum_a[A_EMB : A_EMB + weights[0].shape[0], :],
-        sum_c[C_MIX : C_MIX + PATCHES, 0 : PATCHES + 1],
-        sum_a[A_EXP : A_EXP + D + 1, :],
-        sum_a[A_SHR : A_SHR + D, :],
-        sum_c[C_CLS : C_CLS + D + 1, 0:ncls],
-        sum_c[C_SCA : C_SCA + 5, 0:own],
-        sum_c[C_SHI : C_SHI + 5, 0:own],
-    )
-    for k in range(7):
-        gradient = grads[k]
-        means[k][...] = beta_one * firsts[k][...] + (1.0 - beta_one) * gradient
-        squares[k][...] = beta_two * seconds[k][...] + (1.0 - beta_two) * gradient * gradient
-        average = sums[k] * (1.0 / groups)
-        velocity = outer_momentum * outers[k][...] + average
-        velocities[k][...] = velocity
-        updates[k][...] = weights[k][...] - outer_rate * (average + outer_momentum * velocity)
-
-
-def finish(G, grads, sums, weights, firsts, seconds, outers):
+    for n, (k, r, gradient, total) in enumerate(work):
+        if n == 0 or work[n - 1][0] != k:
+            for j in range(4):
+                loads[7 * j + k].wait()
+        weight, one, two, outer = (held[7 * j + k] for j in range(4))
+        update, mean, square, velocity = (new[7 * j + k] for j in range(4))
+        grad = gradient()
+        mean[r, :] = beta_one * one[r, :] + (1.0 - beta_one) * grad
+        square[r, :] = beta_two * two[r, :] + (1.0 - beta_two) * grad * grad
+        average = total() * (1.0 / groups)
+        moving = outer_momentum * outer[r, :] + average
+        velocity[r, :] = moving
+        update[r, :] = weight[r, :] - outer_rate * (average + outer_momentum * moving)
+        if n + 1 == len(work) or work[n + 1][0] != k:
+            for j in range(4):
+                saves[7 * j + k].start()
+    for c in saves:
+        c.wait()
+
+
+def finish(G, info, grads, shapes, states, out_shapes):
+    dma = pltpu.SemaphoreType.DMA
     vm = pl.BlockSpec(memory_space=VMEM)
-    shapes = tuple(jax.ShapeDtypeStruct(w.shape, F32) for w in weights) * 4
+    hbm = pl.BlockSpec(memory_space=pl.ANY)
     return pl.pallas_call(
         functools.partial(finish_kernel, G),
-        out_shape=shapes,
-        in_specs=[vm] * 36,
-        out_specs=(vm,) * 28,
-        compiler_params=pltpu.CompilerParams(vmem_limit_bytes=60 << 20),
-    )(*grads, *sums, *weights, *firsts, *seconds, *outers)
+        out_shape=tuple(jax.ShapeDtypeStruct(shape, F32) for shape in ((1, 2), (1, 1), *out_shapes)),
+        in_specs=[vm] + [hbm] * 35,
+        out_specs=(vm,) * 2 + (hbm,) * 28,
+        scratch_shapes=[VMEM(a.shape, F32) for a in grads]
+        + [VMEM(shape, F32) for shape in shapes] * 8
+        + [dma((28,)), dma((7,)), dma((28,))],
+        compiler_params=pltpu.CompilerParams(vmem_limit_bytes=62 << 20),
+    )(info, *grads, *states)
+
+
+def thin(a):
+    return jnp.swapaxes(a, 0, 1)
 
 
 def per_device(
@@ -730,27 +845,39 @@
     patches, labels, partner, class_weight,
     embedding, mixing, expand, shrink, classifier, scales, shifts, *state,
 ):
-    weights = (embedding, mixing[0], expand[0], shrink[0], classifier, scales, shifts)
-    flat = lambda group, lead: tuple(a.reshape(w.shape) for a, w in zip(group, weights, strict=True))
-    firsts, seconds, outers = flat(state[0:7], 0), flat(state[7:14], 0), flat(state[14:21], 0)
+    weights = (embedding, thin(mixing), thin(expand), shrink[0], classifier, scales, shifts)
+
+    def moments(a):
+        return (a[0][0], thin(a[1][0]), thin(a[2][0]), a[3][0, 0], thin(a[4]), thin(a[5]), thin(a[6]))
+
+    firsts, seconds = moments(state[0:7]), moments(state[7:14])
+    o = state[14:21]
+    outers = (o[0], thin(o[1]), thin(o[2]), o[3][0], o[4], o[5], o[6])
+    shapes = tuple((a.shape[0], a.shape[-1]) for a in weights)
     ncls = classifier.shape[1]
     cpad = -(-ncls // LANE) * LANE
     padded = jnp.pad(class_weight.reshape(MP, ncls), ((0, 0), (0, cpad - ncls))).reshape(1, MP * cpad)
     rows, e_all, w1, w2, wc, small = move(
         G, MP, partner[0], patches[0], embedding, expand[0], shrink[0], classifier, scales, shifts
     )
-    bundle, factors = local_step(
-        MP, ncls, labels[0], partner[0], rows, e_all, w1, w2, wc, small, mixing[0], padded
+    big, sm, acts, fac = local_step(
+        DP, MP, ncls, labels[0], partner[0], rows, e_all, w1, w2, wc, small, mixing[0], padded
     )
-    *grads, sum_a, sum_c, info = gradient_sums(G, DP, MP, bundle, factors, weights, firsts, seconds)
-    done = finish(G, grads, (sum_a, sum_c), weights, firsts, seconds, outers)
+    *grads, info = gradient_sums(G, DP, MP, big, sm, acts, fac, shapes, (*weights, *firsts, *seconds))
+    out_shapes = tuple(a.shape for a in (*weights, *firsts, *seconds, *outers))
+    losses, norm, *done = finish(G, info, grads, shapes, (*weights, *firsts, *seconds, *outers), out_shapes)
     updates, means, squares, velocities = (list(done[7 * k : 7 * k + 7]) for k in range(4))
-    for k in (1, 2, 3):
-        updates[k], velocities[k] = updates[k][None], velocities[k][None]
-        means[k], squares[k] = means[k][None], squares[k][None]
-    means = [a[None] for a in means]
-    squares = [a[None] for a in squares]
-    return (info[0:1, 0:2], info[0, 2:3], *updates, *means, *squares, *velocities)
+
+    def whole(a):
+        return (a[0], thin(a[1]), thin(a[2]), a[3][None], a[4], a[5], a[6])
+
+    def by_group(a):
+        return (a[0][None], thin(a[1])[None], thin(a[2])[None], a[3][None, None], thin(a[4]), thin(a[5]), thin(a[6]))
+
+    return (
+        losses, norm[0],
+        *whole(updates), *by_group(means), *by_group(squares), *whole(velocities),
+    )
 
 
 WEIGHT_SPECS = (

time: 388 us -> 273 us (0.70)
  Pallas kernels: 348 us -> 258 us
  local copies, waits for them, and re-layouts: 39 us -> 13.8 us
    pallas_call x2, Pallas kernels: 176 us -> 87.1 us  [the longest x1 78.2 us: gradient_sums(): pl.pallas_call(functools.partial(sum_kernel, G, DP, MP), out_shape=(s((DP...]
    unnamed x72 -> x11, local copies, waits for them, and re-layouts: 36.4 us -> 13.7 us
where the time goes in v2:
time: 273 us
  Pallas kernels  258 us (95%)
  local copies, waits for them, and re-layouts  13.8 us (5%)
    pallas_call x1, Pallas kernels, move(): pl.pallas_call(functools.partial(move_kernel, G, MP, NI), out_shape=(jax....  117 us
    pallas_call x1, Pallas kernels, gradient_sums(): pl.pallas_call(functools.partial(sum_kernel, G, DP, MP), out_shape=(s((DP...  78.2 us
    pallas_call x1, Pallas kernels, local_step(): pl.pallas_call(functools.partial(step_kernel, MP, NI, ncls), out_shape=(j...  53.9 us
    unnamed x11, local copies, waits for them, and re-layouts  13.7 us
    pallas_call x1, Pallas kernels, finish(): pl.pallas_call(functools.partial(finish_kernel, G), out_shape=tuple((jax....  8.91 us

profile of v2, /device:TPU:0, one launch (start us, length us, event | category | flops | bytes accessed | tf_op | source)
XLA Modules:
  0.0 273.0 jit_solution(8460817749079746811)
XLA Ops:
  0.7 0.0 copy-start
  0.7 11.5 %copy.62 = f32[1,48,196,192]{3,2,1,0:T(8,128)} copy(f32[1,48,196,192]{2,3,1,0:T(8,128)} %param.32) | data formatting | bytes 14450688 | tf_op args[0]
  12.2 0.0 copy-done
  12.2 0.9 copy.72
  13.1 0.0 copy-start.1
  13.1 0.0 copy-start.2
  13.1 117.4 %shard_map.535 = (bf16[4,6,3,208,128]{4,3,2,1,0:T(8,128)(2,1)}, bf16[4,192,384]{2,1,0:T(8,128)(2,1)}, bf16[384,1536]{1,0:T(8,128)(2,1)}, bf16[1536,384]{1,0:T(8,...) custom-call(s32[48]{0:T(128)} %bitcast.104, f32[48,196,192]{2,1,0:T(8,128)} %bitcast.62, f32[192,384]{1,0:T(8,128)} %refs_8_.1, ...), custom_call_target="tpu_custom_call" | custom-call | tf_op jit(solution)/shard_map/pallas_call | solution.py:189
  130.5 0.0 copy-done.1
  130.5 0.7 copy.73
  131.2 0.0 copy-done.2
  131.2 0.1 reshape.66
  131.3 0.6 copy.69
  131.9 53.9 %shard_map.536 = (f32[4,576,384]{2,1,0:T(8,128)}, f32[4,72,256]{2,1,0:T(8,128)}, f32[4,16,384]{2,1,0:T(8,128)}, bf16[4,48,384]{2,1,0:T(8,128)(2,1)}) custom-call(s32[48]{0:T(128)} %bitcast.106, s32[48]{0:T(128)} %bitcast.105, bf16[4,6,3,208,128]{4,3,2,1,0:T(8,128)(2,1)} %get-tuple-element.78.rows, bf16[4,192,384]{2,1,0:T(8,128)(2,1)} %get-tuple-element.79.e_all, ...), custom_call_target="tpu_custom_call" | custom-call | tf_op jit(solution)/shard_map/pallas_call | solution.py:428
  185.7 78.2 %shard_map.537 = (f32[576,384]{1,0:T(8,128)}, f32[224,256]{1,0:T(8,128)}, f32[384,384]{1,0:T(8,128)}, f32[392,256]{1,0:T(8,128)}, f32[16,128]{1,0:T(8,128)}, /*i...) custom-call(f32[4,576,384]{2,1,0:T(8,128)} %get-tuple-element.84.big, f32[4,72,256]{2,1,0:T(8,128)} %get-tuple-element.85.sm, ...), custom_call_target="tpu_custom_call" | custom-call | tf_op jit(solution)/shard_map/pallas_call | solution.py:711
  263.9 8.9 %shard_map.538 = (f32[1,2]{1,0:T(1,128)}, f32[1,1]{1,0:T(1,128)}, f32[192,384]{1,0:T(8,128)}, f32[196,1,197]{2,1,0:T(1,128)}, f32[385,1,384]{2,1,0:T(1,128)}, /*...) custom-call(f32[8,128]{1,0:T(8,128)} %get-tuple-element.88.refs_0_, ...), custom_call_target="tpu_custom_call" | custom-call | tf_op jit(solution)/shard_map/pallas_call | solution.py:827
  (1 shorter events, 0.0 us)
Async XLA Ops:
  0.7 11.5 %copy-start = (f32[1,385,384]{2,0,1:T(1,128)S(1)}, f32[1,385,384]{2,0,1:T(1,128)}, u32[]{:S(2)}) copy-start(f32[1,385,384]{2,0,1:T(1,128)} %param.38) | copy-start | bytes 1774084
  13.1 117.4 %copy-start.1 = (f32[1,196,197]{2,0,1:T(1,128)S(1)}, f32[1,196,197]{2,0,1:T(1,128)}, u32[]{:S(2)}) copy-start(f32[1,196,197]{2,0,1:T(1,128)} %param.37) | copy-start | bytes 463348
  13.1 118.1 %copy-start.2 = (f32[1000]{0:T(1024)S(1)}, f32[1000]{0:T(1024)}, u32[]{:S(2)}) copy-start(f32[1000]{0:T(1024)} %param.35) | copy-start | bytes 12004

commit v3 on v2

--- a/solution.py
+++ b/solution.py
@@ -67,182 +67,148 @@
     )
 
 
-def move_kernel(
-    G, MP, NI,
-    partner, patches, emb, expa, shr, cls, sca, shi,
-    rows, e_all, w1, w2, wc, small,
-    stage, rs_send, rs_recv, wz_send, wz_recv, wg_send, wg_recv, sm_send, sm_recv,
-):
+CHUNK = 256
+AHEAD = 2
+
+
+def waves_of(pairs):
+    cuts = [0, pairs // 2, pairs - 1, pairs] if pairs > 2 else list(range(pairs + 1))
+    return list(zip(cuts[:-1], cuts[1:], strict=True))
+
+
+def step_kernel(G, DP, MP, NI, ncls, *refs):
+    (labels, partner, sca, shi, class_weight, patches, emb_in, exp_in, shr_in, cls_in, mix_in), refs = refs[:11], refs[11:]
+    (big, sm, acts, factors), refs = refs[:4], refs[4:]
+    (
+        pv, emb, expa, shr, cls, mixing, stage, rows, e_all, w1, w2, wc, small,
+        xs, gp, s0, s1, mx, mi, fi, ep, mm, mt, eye, mbias, vec, b1, cw, asum, s1sum, la, lb,
+        dact, ds2, dh, csum, gw, ge, gm, gmb, gvec,
+        load, rs_send, rs_recv, wz_send, wz_recv, wg_send, wg_recv, sm_send, sm_recv,
+    ) = refs
     z = lax.axis_index("mp")
+    y = lax.axis_index("dp")
     g = lax.axis_index("group")
     NP = NI // 2
+    PR = 2 * ROWS
+    hid = expa.shape[1]
+    hid_all = hid * MP
+    cpad = wc.shape[1] // MP
+    er = emb.shape[0]
+    NCH = hid_all // CHUNK
+    pair = 2 if DP % 2 == 0 else 1
+
+    loads = [
+        pltpu.make_async_copy(flat(a), b, load.at[k])
+        for k, (a, b) in enumerate(
+            ((emb_in, emb), (exp_in, expa), (patches, pv), (shr_in, shr), (cls_in, cls), (mix_in, mixing))
+        )
+    ]
+    for c in loads:
+        c.start()
+
     zpeer = [lax.rem(z + d, MP) for d in range(1, MP)]
-    gpeer = [lax.rem(g + d, G) for d in range(1, G)]
-    greet([{"mp": t} for t in zpeer] + [{"group": t} for t in gpeer])
-
-    hid = expa.shape[1]
-    ncls = cls.shape[1]
-    cpad = wc.shape[1] // MP
-
+    half = lax.rem(y, pair)
+    plane = []
+    for e in range(pair):
+        for d in range(G):
+            if d or e:
+                j = lax.rem(g + d, G)
+                h = half if e == 0 else 1 - half
+                plane.append((j, y if e == 0 else y + 1 - 2 * half, j * pair + h, e))
+    place = g * pair + half
+    parts = G * pair
+    greet([{"mp": t} for t in zpeer] + [{"group": j, "dp": u} for j, u, _, _ in plane])
+
+    def pieces(t, j):
+        ee, hh, dd = er // G, hid // parts, D // parts
+        return (
+            e_all.at[t, pl.ds(pl.multiple_of(j // pair * ee, 16), ee), :],
+            w1.at[pl.ds(pl.multiple_of(j * dd, 16), dd), pl.ds(pl.multiple_of(t * hid, LANE), hid)],
+            w2.at[pl.ds(pl.multiple_of(t * hid + j * hh, 16), hh), :],
+            wc.at[pl.ds(pl.multiple_of(j * dd, 16), dd), pl.ds(pl.multiple_of(t * cpad, LANE), cpad)],
+        )
+
+    started = []
+
+    def go(*args):
+        c = remote(*args)
+        c.start()
+        started.append(c)
+
+    def spread(k):
+        part = pieces(z, place)[k]
+        for d, t in enumerate(zpeer):
+            go(part, part, wz_send.at[d, k], wz_recv.at[z, k], {"mp": t})
+
+    def pass_on(k):
+        for d in range(1, MP):
+            t = lax.rem(z + MP - d, MP)
+            part = pieces(t, place)[k]
+            remote(part, part, wz_send.at[d - 1, k], wz_recv.at[t, k], {"mp": t}).wait_recv()
+            for e, (j, u, _, other) in enumerate(plane):
+                if k or not other:
+                    go(part, part, wg_send.at[d - 1, e, k], wg_recv.at[t, place, k], {"group": j, "dp": u})
+
+    def gathered(k):
+        for t in zpeer:
+            for j, u, at, other in plane:
+                if k or not other:
+                    part = pieces(t, at)[k]
+                    remote(part, part, wg_send.at[0, 0, k], wg_recv.at[t, at, k], {"group": j, "dp": u}).wait_recv()
+
+    loads[0].wait()
     e_all[z] = emb[...].astype(BF16)
+    spread(0)
+    loads[1].wait()
     w1[:, pl.ds(pl.multiple_of(z * hid, LANE), hid)] = expa[0:D, :].astype(BF16)
+    spread(1)
+
+    row = lax.broadcasted_iota(jnp.int32, (ROWS, PATCHES), 0)
+    column = lax.broadcasted_iota(jnp.int32, (ROWS, PATCHES), 1)
+    eye[...] = jnp.where(row == column, 1.0, 0.0).astype(BF16)
+    share = F32(mix_share)
+    rest = F32(1.0 - mix_share)
+
+    def blend(i):
+        return (share * pv[i] + rest * pv[partner[i]]).astype(BF16)
+
+    def blend_pair(t, p):
+        a = blend(t * NI + 2 * p)
+        b = blend(t * NI + 2 * p + 1)
+        both = jnp.concatenate([a[0:LANE], b[0:LANE], a[LANE:], b[LANE:]], axis=0)
+        return dot(eye[...], both, ((1,), (1,))).astype(BF16)
+
+    def send(p, d):
+        return remote(stage.at[d, p], rows.at[z, p], rs_send.at[d, p], rs_recv.at[z, p], {"mp": zpeer[d]})
+
+    def issue(p):
+        for d in range(MP - 1):
+            stage[d, p] = blend_pair(zpeer[d], p)
+            send(p, d).start()
+
+    loads[2].wait()
+    issue(0)
+
+    loads[3].wait()
     w2[pl.ds(pl.multiple_of(z * hid, 16), hid), :] = shr[...].astype(BF16)
+    loads[4].wait()
     head = jnp.concatenate([cls[0:D, :], jnp.zeros((D, cpad - ncls), F32)], axis=1)
     wc[:, pl.ds(pl.multiple_of(z * cpad, LANE), cpad)] = head.astype(BF16)
+    spread(2)
+    spread(3)
     small[z] = jnp.zeros(small.shape[1:], F32)
     small[z, 0:5, 0 : D // MP] = sca[...]
     small[z, 5:10, 0 : D // MP] = shi[...]
     small[z, 10:11, :] = rounded(expa[D : D + 1, :])
     small[z, 11:12, 0:ncls] = rounded(cls[D : D + 1, :])
-
-    er, hr, dr = emb.shape[0] // G, hid // G, D // G
-
-    def pieces(t, j):
-        return (
-            e_all.at[t, pl.ds(pl.multiple_of(j * er, 16), er), :],
-            w1.at[pl.ds(pl.multiple_of(j * dr, 16), dr), pl.ds(pl.multiple_of(t * hid, LANE), hid)],
-            w2.at[pl.ds(pl.multiple_of(t * hid + j * hr, 16), hr), :],
-            wc.at[pl.ds(pl.multiple_of(j * dr, 16), dr), pl.ds(pl.multiple_of(t * cpad, LANE), cpad)],
-        )
-
-    started = []
     for d, t in enumerate(zpeer):
-        c = remote(small.at[z], small.at[z], sm_send.at[d], sm_recv.at[z], {"mp": t})
-        c.start()
-        started.append(c)
-        for k, part in enumerate(pieces(z, g)):
-            c = remote(part, part, wz_send.at[d, k], wz_recv.at[z, k], {"mp": t})
-            c.start()
-            started.append(c)
-
-    share = F32(mix_share)
-    other = F32(1.0 - mix_share)
-
-    def blend(i):
-        return share * patches[i] + other * patches[partner[i]]
-
-    tail = rows.shape[-2] - 192
-
-    def put(ref, lead, value):
-        ref[lead + (slice(0, 192), slice(None))] = value[0:192].astype(BF16)
-        last = jnp.concatenate([value[192:], jnp.zeros((tail - (PATCHES - 192), LANE), F32)], axis=0)
-        ref[lead + (slice(192, 192 + tail), slice(None))] = last.astype(BF16)
-
-    def blend_pair(t, p, ref, lead):
-        a = blend(t * NI + 2 * p)
-        b = blend(t * NI + 2 * p + 1)
-        put(ref, lead + (0,), a[:, 0:LANE])
-        put(ref, lead + (1,), b[:, 0:LANE])
-        put(ref, lead + (2,), jnp.concatenate([a[:, LANE:], b[:, LANE:]], axis=1))
-
-    def send(p, d):
-        return remote(stage.at[d, p], rows.at[z, p], rs_send.at[d, p], rs_recv.at[z, p], {"mp": zpeer[d]})
-
-    def each_pair(p, carry):
-        for d in range(MP - 1):
-            blend_pair(zpeer[d], p, stage, (d, p))
-            send(p, d).start()
-        return carry
-
-    lax.fori_loop(0, NP, each_pair, 0)
-
-    for d in range(1, MP):
-        t = lax.rem(z + MP - d, MP)
-        for k, part in enumerate(pieces(t, g)):
-            remote(part, part, wz_send.at[d - 1, k], wz_recv.at[t, k], {"mp": t}).wait_recv()
-            for e, j in enumerate(gpeer):
-                c = remote(part, part, wg_send.at[d - 1, e, k], wg_recv.at[t, g, k], {"group": j})
-                c.start()
-                started.append(c)
-
-    def own_pair(p, carry):
-        blend_pair(z, p, rows, (z, p))
-        return carry
-
-    lax.fori_loop(0, NP, own_pair, 0)
-
-    def drain(p, carry):
-        for d in range(MP - 1):
-            send(p, d).wait_send()
-            t = zpeer[d]
-            remote(stage.at[d, p], rows.at[t, p], rs_send.at[d, p], rs_recv.at[t, p], {"mp": t}).wait_recv()
-        return carry
-
-    lax.fori_loop(0, NP, drain, 0)
-    for c in started:
-        c.wait_send()
-    for t in zpeer:
-        remote(small.at[t], small.at[t], sm_send.at[0], sm_recv.at[t], {"mp": t}).wait_recv()
-        for j in gpeer:
-            for k, part in enumerate(pieces(t, j)):
-                remote(part, part, wg_send.at[0, 0, k], wg_recv.at[t, j, k], {"group": j}).wait_recv()
-
-
-def move(G, MP, partner, patches, emb, expa, shr, cls, sca, shi):
-    NI = patches.shape[0] // MP
-    NP = NI // 2
-    hid = expa.shape[1]
-    cpad = -(-cls.shape[1] // LANE) * LANE
-    dma = pltpu.SemaphoreType.DMA
-    vm = pl.BlockSpec(memory_space=VMEM)
-    ge = max(G - 1, 1)
-    return pl.pallas_call(
-        functools.partial(move_kernel, G, MP, NI),
-        out_shape=(
-            jax.ShapeDtypeStruct((MP, NP, 3, ROWS, LANE), BF16),
-            jax.ShapeDtypeStruct((MP, emb.shape[0], D), BF16),
-            jax.ShapeDtypeStruct((D, hid * MP), BF16),
-            jax.ShapeDtypeStruct((hid * MP, D), BF16),
-            jax.ShapeDtypeStruct((D, cpad * MP), BF16),
-            jax.ShapeDtypeStruct((MP, 16, hid), F32),
-        ),
-        in_specs=[pl.BlockSpec(memory_space=SMEM)] + [vm] * 7,
-        out_specs=(vm,) * 6,
-        scratch_shapes=[
-            pltpu.VMEM((MP - 1, NP, 3, ROWS, LANE), BF16),
-            dma((MP - 1, NP)),
-            dma((MP, NP)),
-            dma((MP - 1, 4)),
-            dma((MP, 4)),
-            dma((MP - 1, ge, 4)),
-            dma((MP, G, 4)),
-            dma((MP - 1,)),
-            dma((MP,)),
-        ],
-        compiler_params=pltpu.CompilerParams(
-            collective_id=0, has_side_effects=True, vmem_limit_bytes=56 << 20
-        ),
-    )(partner, patches, emb, expa, shr, cls, sca, shi)
-
-
-def step_kernel(
-    MP, NI, ncls,
-    labels, partner, rows, e_all, w1, w2, wc, small, mixing, class_weight,
-    big, sm, acts, factors,
-    xs, gp, s0, s1, mx, mi, fi, ep, mm, mt, mbias, vec, b1, asum, s1sum, la, lb,
-    dact, ds2, dh, csum, gw, ge, gm, gmb, gvec,
-):
-    z = lax.axis_index("mp")
-    NP = NI // 2
-    PR = 2 * ROWS
-    hid_all = w1.shape[1]
-    hid = hid_all // MP
-    cpad = wc.shape[1] // MP
-    CH = 256
-    NCH = hid_all // CH
-    er = e_all.shape[1]
-
-    full = jnp.zeros((16, D), F32)
-    for t in range(MP):
-        block = small[t]
-        full = full + (pltpu.roll(block, t * (D // MP), 1) if t else block)
-    vec[...] = full
-    for t in range(MP):
-        b1[:, t * hid : (t + 1) * hid] = small[t, 10:11, :]
-        ep[t * LANE : (t + 1) * LANE, :] = e_all[t, 0:LANE, :]
-        half = er - LANE
-        ep[MP * LANE + t * half : MP * LANE + (t + 1) * half, :] = e_all[t, LANE:er, :]
-
+        go(small.at[z], small.at[z], sm_send.at[d], sm_recv.at[z], {"mp": t})
+    for p in range(1, min(AHEAD, NP)):
+        issue(p)
+    pass_on(0)
+    pass_on(1)
+
+    loads[5].wait()
     wide = jnp.concatenate([mixing[...], jnp.zeros((PATCHES, 256 - PATCHES - 1), F32)], axis=1)
     wide = jnp.concatenate([wide, jnp.zeros((256 - PATCHES, 256), F32)], axis=0)
     column = lax.broadcasted_iota(jnp.int32, (256, 256), 1)
@@ -250,7 +216,9 @@
     mm[...] = square[0:ROWS, 0:ROWS].astype(BF16)
     mt[...] = jnp.transpose(square)[0:ROWS, 0:ROWS].astype(BF16)
     mbias[...] = rounded(jnp.sum(jnp.where(column == PATCHES, wide, 0.0), axis=1, keepdims=True)[0:ROWS])
-
+    for t in range(MP):
+        block = class_weight[:, t * ncls : (t + 1) * ncls]
+        cw[:, t * cpad : (t + 1) * cpad] = jnp.concatenate([block, jnp.zeros((1, cpad - ncls), F32)], axis=1)
     asum[...] = jnp.zeros_like(asum)
     s1sum[...] = jnp.zeros_like(s1sum)
     csum[...] = jnp.zeros_like(csum)
@@ -259,52 +227,6 @@
     gm[...] = jnp.zeros_like(gm)
     gmb[...] = jnp.zeros_like(gmb)
     gvec[...] = jnp.zeros_like(gvec)
-
-    def scale(k):
-        return vec[k : k + 1, :]
-
-    def shift(k):
-        return vec[5 + k : 6 + k, :]
-
-    def forward(p, carry):
-        for t in range(MP):
-            xs[p, 0:ROWS, t * LANE : (t + 1) * LANE] = rows[t, p, 0]
-            xs[p, ROWS:PR, t * LANE : (t + 1) * LANE] = rows[t, p, 1]
-        for t in range(0, MP, 2):
-            left, right = rows[t, p, 2], rows[t + 1, p, 2]
-            at = MP * LANE + t * 64
-            xs[p, 0:ROWS, at : at + LANE] = jnp.concatenate([left[:, 0:64], right[:, 0:64]], axis=1)
-            xs[p, ROWS:PR, at : at + LANE] = jnp.concatenate([left[:, 64:], right[:, 64:]], axis=1)
-        stream0 = dot(xs[p], ep[...]) + shift(3)
-        s0[p] = stream0
-        mi[p] = (scale(0) * stream0 + shift(0)).astype(BF16)
-        for b in range(2):
-            r = slice(b * ROWS, (b + 1) * ROWS)
-            mixed = dot(mm[...], mi[p, r, :]) + mbias[...]
-            mx[p, r, :] = mixed
-            stream1 = s0[p, r, :] + scale(1) * mixed
-            s1[p, r, :] = stream1
-            fi[p, r, :] = (scale(2) * stream1 + shift(1)).astype(BF16)
-            s1sum[pl.ds(2 * p + b, 1), :] = jnp.sum(stream1[0:PATCHES], axis=0, keepdims=True)
-
-        def chunk(c, carry):
-            cols = pl.ds(pl.multiple_of(c * CH, CH), CH)
-            for b in range(2):
-                r = slice(b * ROWS, (b + 1) * ROWS)
-                h = dot(fi[p, r, :], w1[:, cols]) + b1[:, cols]
-                sq = h * h
-                s = 0.5 * jnp.tanh(h * (GELU_A + GELU_B * sq)) + 0.5
-                act = rounded(h * s)
-                asum[pl.ds(2 * p + b, 1), cols] = jnp.sum(act[0:PATCHES], axis=0, keepdims=True)
-                gp[p, r, cols] = s + s * (1.0 - s) * (h * (2.0 * GELU_A + 6.0 * GELU_B * sq))
-                gp[p, b * ROWS + PATCHES : (b + 1) * ROWS, cols] = jnp.zeros((ROWS - PATCHES, CH), F32)
-            return carry
-
-        lax.fori_loop(0, NCH, chunk, 0)
-        return carry
-
-    lax.fori_loop(0, NP, forward, 0)
-
     la[...] = jnp.full(la.shape, -1, jnp.int32)
     lb[...] = jnp.full(lb.shape, -1, jnp.int32)
     for i in range(NI):
@@ -312,94 +234,178 @@
         mate = labels[partner[z * NI + i]]
         la[i : i + 1, :] = jnp.full((1, LANE), own, jnp.int32)
         lb[i : i + 1, :] = jnp.full((1, LANE), mate, jnp.int32)
-    outsum = exact(asum[...], w2[...].astype(F32)) + PATCHES * shift(2)
-    stream2 = s1sum[...] + scale(3) * outsum
-    pooled = (scale(4) * (stream2 * (1.0 / PATCHES)) + shift(4)).astype(BF16)
-    bias = jnp.concatenate([small[t, 11:12, 0:cpad] for t in range(MP)], axis=1)
-    lane = lax.broadcasted_iota(jnp.int32, (16, cpad * MP), 1)
-    inside = lax.rem(lane, cpad)
-    valid = inside < ncls
-    class_id = (lane // cpad) * ncls + inside
-    logits = jnp.where(valid, dot(pooled, wc[...]) + bias, -1e30)
-    hot_a = jnp.where(valid & (class_id == la[:, 0:1]), 1.0, 0.0)
-    hot_b = jnp.where(valid & (class_id == lb[:, 0:1]), 1.0, 0.0)
-    weight_a = mix_share * jnp.sum(hot_a * class_weight[...], axis=1, keepdims=True)
-    weight_b = (1.0 - mix_share) * jnp.sum(hot_b * class_weight[...], axis=1, keepdims=True)
-    top = jnp.max(logits, axis=1, keepdims=True)
-    exps = jnp.where(valid, jnp.exp(logits - top), 0.0)
-    exp_sum = jnp.sum(exps, axis=1, keepdims=True)
-    log_total = top + jnp.log(exp_sum)
-    target_a = jnp.sum(hot_a * logits, axis=1, keepdims=True)
-    target_b = jnp.sum(hot_b * logits, axis=1, keepdims=True)
-    loss = jnp.sum(weight_a * (log_total - target_a) + weight_b * (log_total - target_b), axis=0, keepdims=True)
-    total = jnp.sum(weight_a + weight_b, axis=0, keepdims=True)
-    dlog = ((weight_a + weight_b) * (exps / exp_sum) - weight_a * hot_a - weight_b * hot_b).astype(BF16)
-    dfinal = dot(dlog, wc[...], ((1,), (1,))) * (1.0 / PATCHES)
-    dstream2 = scale(4) * dfinal
-    ds2[...] = dstream2
-    dout = scale(3) * dstream2
-    low = dout.astype(BF16)
-    dact[...] = dot(low, w2[...], ((1,), (1,)))
-    factors[:, 0:16, :] = jnp.broadcast_to(low[None], (MP, 16, D))
-    factors[:, 16:32, :] = jnp.broadcast_to(pooled[None], (MP, 16, D))
+
+    for t in zpeer:
+        remote(small.at[t], small.at[t], sm_send.at[0], sm_recv.at[t], {"mp": t}).wait_recv()
+    full = jnp.zeros((16, D), F32)
     for t in range(MP):
-        factors[t, 32:48, 0:cpad] = dlog[:, t * cpad : (t + 1) * cpad]
-        factors[t, 32:48, cpad:] = jnp.zeros((16, D - cpad), BF16)
-
-    def backward(p, carry):
+        block = small[t]
+        full = full + (pltpu.roll(block, t * (D // MP), 1) if t else block)
+        b1[:, t * hid : (t + 1) * hid] = small[t, 10:11, :]
+    vec[...] = full
+    gathered(0)
+    rest_rows = er - LANE
+    for t in range(MP):
+        ep[t * LANE : (t + 1) * LANE, :] = e_all[t, 0:LANE, :]
+        ep[MP * LANE + t * rest_rows : MP * LANE + (t + 1) * rest_rows, :] = e_all[t, LANE:er, :]
+    gathered(1)
+    pass_on(2)
+    pass_on(3)
+
+    def scale(k):
+        return vec[k : k + 1, :]
+
+    def shift(k):
+        return vec[5 + k : 6 + k, :]
+
+    def forward(base, p, carry):
+        @pl.when(p + AHEAD < NP)
+        def _():
+            issue(p + AHEAD)
+
+        q = p - base
+        rows[z, p] = blend_pair(z, p)
+        for t in zpeer:
+            remote(stage.at[0, p], rows.at[t, p], rs_send.at[0, p], rs_recv.at[t, p], {"mp": t}).wait_recv()
+        for t in range(MP):
+            xs[q, 0:ROWS, t * LANE : (t + 1) * LANE] = rows[t, p, :, 0:LANE]
+            xs[q, ROWS:PR, t * LANE : (t + 1) * LANE] = rows[t, p, :, LANE : 2 * LANE]
+        for t in range(0, MP, 2):
+            left, right = rows[t, p, :, 2 * LANE :], rows[t + 1, p, :, 2 * LANE :]
+            at = MP * LANE + t * 64
+            xs[q, 0:ROWS, at : at + LANE] = jnp.concatenate([left[:, 0:64], right[:, 0:64]], axis=1)
+            xs[q, ROWS:PR, at : at + LANE] = jnp.concatenate([left[:, 64:], right[:, 64:]], axis=1)
+        stream0 = dot(xs[q], ep[...]) + shift(3)
+        s0[q] = stream0
+        mi[q] = (scale(0) * stream0 + shift(0)).astype(BF16)
+        for b in range(2):
+            r = slice(b * ROWS, (b + 1) * ROWS)
+            mixed = dot(mm[...], mi[q, r, :]) + mbias[...]
+            mx[q, r, :] = mixed
+            stream1 = s0[q, r, :] + scale(1) * mixed
+            s1[q, r, :] = stream1
+            fi[q, r, :] = (scale(2) * stream1 + shift(1)).astype(BF16)
+            s1sum[pl.ds(2 * p + b, 1), :] = jnp.sum(stream1[0:PATCHES], axis=0, keepdims=True)
+
         def chunk(c, carry):
-            cols = pl.ds(pl.multiple_of(c * CH, CH), CH)
+            cols = pl.ds(pl.multiple_of(c * CHUNK, CHUNK), CHUNK)
             for b in range(2):
                 r = slice(b * ROWS, (b + 1) * ROWS)
-                dh[r, cols] = (gp[p, r, cols] * dact[pl.ds(2 * p + b, 1), cols]).astype(BF16)
+                h = dot(fi[q, r, :], w1[:, cols]) + b1[:, cols]
+                sq = h * h
+                s = 0.5 * jnp.tanh(h * (GELU_A + GELU_B * sq)) + 0.5
+                act = rounded(h * s)
+                asum[pl.ds(2 * p + b, 1), cols] = jnp.sum(act[0:PATCHES], axis=0, keepdims=True)
+                gp[q, r, cols] = s + s * (1.0 - s) * (h * (2.0 * GELU_A + 6.0 * GELU_B * sq))
+                gp[q, b * ROWS + PATCHES : (b + 1) * ROWS, cols] = jnp.zeros((ROWS - PATCHES, CHUNK), F32)
+            return carry
+
+        lax.fori_loop(0, NCH, chunk, 0)
+        return carry
+
+    def class_head():
+        outsum = exact(asum[...], w2[...].astype(F32)) + PATCHES * shift(2)
+        stream2 = s1sum[...] + scale(3) * outsum
+        pooled = (scale(4) * (stream2 * (1.0 / PATCHES)) + shift(4)).astype(BF16)
+        bias = jnp.concatenate([small[t, 11:12, 0:cpad] for t in range(MP)], axis=1)
+        lane = lax.broadcasted_iota(jnp.int32, (16, cpad * MP), 1)
+        inside = lax.rem(lane, cpad)
+        valid = inside < ncls
+        class_id = (lane // cpad) * ncls + inside
+        logits = jnp.where(valid, dot(pooled, wc[...]) + bias, -1e30)
+        hot_a = jnp.where(valid & (class_id == la[:, 0:1]), 1.0, 0.0)
+        hot_b = jnp.where(valid & (class_id == lb[:, 0:1]), 1.0, 0.0)
+        weight_a = mix_share * jnp.sum(hot_a * cw[...], axis=1, keepdims=True)
+        weight_b = (1.0 - mix_share) * jnp.sum(hot_b * cw[...], axis=1, keepdims=True)
+        top = jnp.max(logits, axis=1, keepdims=True)
+        exps = jnp.where(valid, jnp.exp(logits - top), 0.0)
+        exp_sum = jnp.sum(exps, axis=1, keepdims=True)
+        soft = exps / exp_sum
+        dlog = ((weight_a + weight_b) * soft - weight_a * hot_a - weight_b * hot_b).astype(BF16)
+        dfinal = dot(dlog, wc[...], ((1,), (1,))) * (1.0 / PATCHES)
+        dstream2 = scale(4) * dfinal
+        ds2[...] = dstream2
+        dout = scale(3) * dstream2
+        low = dout.astype(BF16)
+        dact[...] = dot(low, w2[...], ((1,), (1,)))
+
+        def last():
+            log_total = top + jnp.log(exp_sum)
+            target_a = jnp.sum(hot_a * logits, axis=1, keepdims=True)
+            target_b = jnp.sum(hot_b * logits, axis=1, keepdims=True)
+            loss = weight_a * (log_total - target_a) + weight_b * (log_total - target_b)
+            loss = jnp.sum(loss, axis=0, keepdims=True)
+            total = jnp.sum(weight_a + weight_b, axis=0, keepdims=True)
+            factors[:, 0:16, :] = jnp.broadcast_to(low[None], (MP, 16, D))
+            factors[:, 16:32, :] = jnp.broadcast_to(pooled[None], (MP, 16, D))
+            for t in range(MP):
+                factors[t, 32:48, 0:cpad] = dlog[:, t * cpad : (t + 1) * cpad]
+                factors[t, 32:48, cpad:] = jnp.zeros((16, D - cpad), BF16)
+                acts[t] = asum[:, t * hid : (t + 1) * hid]
+            gvec[3:4, :] = jnp.sum(outsum * dstream2, axis=0, keepdims=True)
+            gvec[4:5, :] = jnp.sum(dfinal * stream2, axis=0, keepdims=True)
+            gvec[7:8, :] = PATCHES * jnp.sum(dout, axis=0, keepdims=True)
+            gvec[8:9, :] = PATCHES * jnp.sum(dstream2, axis=0, keepdims=True)
+            gvec[9:10, :] = PATCHES * jnp.sum(dfinal, axis=0, keepdims=True)
+            lane = lax.broadcasted_iota(jnp.int32, (1, D), 1)
+            gvec[10:11, :] = jnp.where(lane == 0, loss, jnp.where(lane == 1, total, 0.0))
+
+        return last
+
+    def backward(base, p, carry):
+        q = p - base
+
+        def chunk(c, carry):
+            cols = pl.ds(pl.multiple_of(c * CHUNK, CHUNK), CHUNK)
+            for b in range(2):
+                r = slice(b * ROWS, (b + 1) * ROWS)
+                dh[r, cols] = (gp[q, r, cols] * dact[pl.ds(2 * p + b, 1), cols]).astype(BF16)
             value = dh[:, cols]
             csum[0:1, cols] += jnp.sum(value.astype(F32), axis=0, keepdims=True)
-            gw[:, cols] += dot(fi[p], value, ((0,), (0,)))
+            gw[:, cols] += dot(fi[q], value, ((0,), (0,)))
             return carry
 
         lax.fori_loop(0, NCH, chunk, 0)
         dffn = dot(dh[...], w1[...], ((1,), (1,)))
-        gvec[2:3, :] += jnp.sum(dffn * s1[p], axis=0, keepdims=True)
+        gvec[2:3, :] += jnp.sum(dffn * s1[q], axis=0, keepdims=True)
         gvec[6:7, :] += jnp.sum(dffn, axis=0, keepdims=True)
         for b in range(2):
             r = slice(b * ROWS, (b + 1) * ROWS)
             d1 = ds2[pl.ds(2 * p + b, 1), :] + scale(2) * dffn[r]
-            gvec[1:2, :] += jnp.sum(mx[p, r, :] * d1, axis=0, keepdims=True)
+            gvec[1:2, :] += jnp.sum(mx[q, r, :] * d1, axis=0, keepdims=True)
             dmixed = (scale(1) * d1).astype(BF16)
-            gm[...] += dot(dmixed, mi[p, r, :], ((1,), (1,)))
+            gm[...] += dot(dmixed, mi[q, r, :], ((1,), (1,)))
             gmb[...] += dmixed.astype(F32)
             dmixer = dot(mt[...], dmixed)
-            gvec[0:1, :] += jnp.sum(dmixer * s0[p, r, :], axis=0, keepdims=True)
+            gvec[0:1, :] += jnp.sum(dmixer * s0[q, r, :], axis=0, keepdims=True)
             gvec[5:6, :] += jnp.sum(dmixer, axis=0, keepdims=True)
             d0 = (d1 + scale(0) * dmixer).astype(BF16)
-            ge[...] += dot(xs[p, r, :], d0, ((0,), (0,)))
+            ge[...] += dot(xs[q, r, :], d0, ((0,), (0,)))
         return carry
 
-    lax.fori_loop(0, NP, backward, 0)
-
-    gvec[3:4, :] = jnp.sum(outsum * dstream2, axis=0, keepdims=True)
-    gvec[4:5, :] = jnp.sum(dfinal * stream2, axis=0, keepdims=True)
-    gvec[7:8, :] = PATCHES * jnp.sum(dout, axis=0, keepdims=True)
-    gvec[8:9, :] = (
-        PATCHES * jnp.sum(dstream2, axis=0, keepdims=True) + scale(2) * gvec[6:7, :] + scale(0) * gvec[5:6, :]
-    )
-    gvec[9:10, :] = PATCHES * jnp.sum(dfinal, axis=0, keepdims=True)
-    lane = lax.broadcasted_iota(jnp.int32, (1, D), 1)
-    gvec[10:11, :] = jnp.where(lane == 0, loss, jnp.where(lane == 1, total, 0.0))
-
+    for n, (lo, hi) in enumerate(waves_of(NP)):
+        lax.fori_loop(lo, hi, functools.partial(forward, lo), 0)
+        if n == 0:
+            gathered(2)
+            gathered(3)
+        last = class_head()
+        if hi == NP:
+            last()
+        lax.fori_loop(lo, hi, functools.partial(backward, lo), 0)
+
+    gvec[8:9, :] += scale(2) * gvec[6:7, :] + scale(0) * gvec[5:6, :]
     row = lax.broadcasted_iota(jnp.int32, (ROWS, 256), 0)
     column = lax.broadcasted_iota(jnp.int32, (ROWS, 256), 1)
     bias_grad = jnp.sum(gmb[...], axis=1, keepdims=True)
     grad = jnp.concatenate([gm[...], jnp.zeros((ROWS, 256 - ROWS), F32)], axis=1)
     grad = jnp.where(column < PATCHES, grad, jnp.where(column == PATCHES, bias_grad, 0.0))
     grad = jnp.where(row < PATCHES, grad, 0.0)
-    half = er - LANE
     own = D // MP
     lane = lax.broadcasted_iota(jnp.int32, (16, LANE), 1)
     for t in range(MP):
         big[t, 0:D, :] = gw[:, t * hid : (t + 1) * hid]
         big[t, D : D + LANE, :] = ge[t * LANE : (t + 1) * LANE, :]
-        big[t, D + LANE : D + er, :] = ge[MP * LANE + t * half : MP * LANE + (t + 1) * half, :]
+        big[t, D + LANE : D + er, :] = ge[MP * LANE + t * rest_rows : MP * LANE + (t + 1) * rest_rows, :]
         if D + er < big.shape[1]:
             big[t, D + er :, :] = jnp.zeros((big.shape[1] - D - er, D), F32)
         sm[t, 0:S_VEC, :] = jnp.zeros((S_VEC, 256), F32)
@@ -414,41 +420,71 @@
         for k in range(hid // LANE):
             at = t * hid + k * LANE
             sm[t, S_VEC + 11 + k : S_VEC + 12 + k, 0:LANE] = csum[:, at : at + LANE]
-        acts[t] = asum[:, t * hid : (t + 1) * hid]
-
-
-def local_step(DP, MP, ncls, labels, partner, rows, e_all, w1, w2, wc, small, mixing, class_weight):
-    NP = rows.shape[1]
-    NI = 2 * NP
+
+    def drain(p, carry):
+        for d in range(MP - 1):
+            send(p, d).wait_send()
+        return carry
+
+    lax.fori_loop(0, NP, drain, 0)
+    for c in started:
+        c.wait_send()
+
+
+def local_step(G, DP, MP, ncls, labels, partner, sca, shi, class_weight, patches, emb, expa, shr, cls, mixing):
+    NI = patches.shape[0] // MP
+    NP = NI // 2
     PR = 2 * ROWS
-    hid_all = w1.shape[1]
-    pd = e_all.shape[0] * e_all.shape[1]
+    hid = expa.shape[-1]
+    hid_all = hid * MP
+    er = emb.shape[0]
+    pd = er * MP
+    cpad = -(-ncls // LANE) * LANE
+    wave = max(hi - lo for lo, hi in waves_of(NP))
+    pair = 2 if DP % 2 == 0 else 1
+    dma = pltpu.SemaphoreType.DMA
     vm = pl.BlockSpec(memory_space=VMEM)
-    sm = pl.BlockSpec(memory_space=SMEM)
+    smem = pl.BlockSpec(memory_space=SMEM)
+    hbm = pl.BlockSpec(memory_space=pl.ANY)
     return pl.pallas_call(
-        functools.partial(step_kernel, MP, NI, ncls),
+        functools.partial(step_kernel, G, DP, MP, NI, ncls),
         out_shape=(
-            jax.ShapeDtypeStruct((MP, DP * part_rows(DP, e_all.shape[1]), D), F32),
+            jax.ShapeDtypeStruct((MP, DP * part_rows(DP, er), D), F32),
             jax.ShapeDtypeStruct((MP, S_ROWS, 256), F32),
-            jax.ShapeDtypeStruct((MP, 16, hid_all // MP), F32),
+            jax.ShapeDtypeStruct((MP, 16, hid), F32),
             jax.ShapeDtypeStruct((MP, 48, D), BF16),
         ),
-        in_specs=[sm, sm] + [vm] * 8,
+        in_specs=[smem, smem, vm, vm, vm] + [hbm] * 6,
         out_specs=(vm,) * 4,
         scratch_shapes=[
-            VMEM((NP, PR, pd), BF16),
-            VMEM((NP, PR, hid_all), F32),
-            VMEM((NP, PR, D), F32),
-            VMEM((NP, PR, D), F32),
-            VMEM((NP, PR, D), F32),
-            VMEM((NP, PR, D), BF16),
-            VMEM((NP, PR, D), BF16),
+            VMEM(patches.shape, F32),
+            VMEM((er, D), F32),
+            VMEM((D + 1, hid), F32),
+            VMEM((hid, D), F32),
+            VMEM((D + 1, ncls), F32),
+            VMEM((PATCHES, PATCHES + 1), F32),
+            VMEM((MP - 1, NP, ROWS, 2 * er), BF16),
+            VMEM((MP, NP, ROWS, 2 * er), BF16),
+            VMEM((MP, er, D), BF16),
+            VMEM((D, hid_all), BF16),
+            VMEM((hid_all, D), BF16),
+            VMEM((D, cpad * MP), BF16),
+            VMEM((MP, 16, hid), F32),
+            VMEM((wave, PR, pd), BF16),
+            VMEM((wave, PR, hid_all), F32),
+            VMEM((wave, PR, D), F32),
+            VMEM((wave, PR, D), F32),
+            VMEM((wave, PR, D), F32),
+            VMEM((wave, PR, D), BF16),
+            VMEM((wave, PR, D), BF16),
             VMEM((pd, D), BF16),
             VMEM((ROWS, ROWS), BF16),
             VMEM((ROWS, ROWS), BF16),
+            VMEM((ROWS, PATCHES), BF16),
             VMEM((ROWS, 1), F32),
             VMEM((16, D), F32),
             VMEM((1, hid_all), F32),
+            VMEM((1, cpad * MP), F32),
             VMEM((16, hid_all), F32),
             VMEM((16, D), F32),
             VMEM((16, LANE), jnp.int32),
@@ -462,9 +498,20 @@
             VMEM((ROWS, ROWS), F32),
             VMEM((ROWS, D), F32),
             VMEM((16, D), F32),
+            dma((6,)),
+            dma((MP - 1, NP)),
+            dma((MP, NP)),
+            dma((MP - 1, 4)),
+            dma((MP, 4)),
+            dma((MP - 1, G * pair - 1 or 1, 4)),
+            dma((MP, G * pair, 4)),
+            dma((MP - 1,)),
+            dma((MP,)),
         ],
-        compiler_params=pltpu.CompilerParams(vmem_limit_bytes=62 << 20),
-    )(labels, partner, rows, e_all, w1, w2, wc, small, mixing, class_weight)
+        compiler_params=pltpu.CompilerParams(
+            collective_id=0, has_side_effects=True, vmem_limit_bytes=63 << 20
+        ),
+    )(labels, partner, sca, shi, class_weight, patches, emb, expa, shr, cls, mixing)
 
 
 def part_rows(DP, er):
@@ -480,7 +527,7 @@
 
 
 def flat(ref):
-    return ref.at[:, 0, :] if len(ref.shape) == 3 else ref
+    return ref.at[:, 0, :] if len(ref.shape) == 3 and ref.shape[1] == 1 else ref
 
 
 def sum_kernel(G, DP, MP, big, sm, acts, fac, *refs):
@@ -855,13 +902,9 @@
     outers = (o[0], thin(o[1]), thin(o[2]), o[3][0], o[4], o[5], o[6])
     shapes = tuple((a.shape[0], a.shape[-1]) for a in weights)
     ncls = classifier.shape[1]
-    cpad = -(-ncls // LANE) * LANE
-    padded = jnp.pad(class_weight.reshape(MP, ncls), ((0, 0), (0, cpad - ncls))).reshape(1, MP * cpad)
-    rows, e_all, w1, w2, wc, small = move(
-        G, MP, partner[0], patches[0], embedding, expand[0], shrink[0], classifier, scales, shifts
-    )
     big, sm, acts, fac = local_step(
-        DP, MP, ncls, labels[0], partner[0], rows, e_all, w1, w2, wc, small, mixing[0], padded
+        G, DP, MP, ncls, labels[0], partner[0], scales, shifts, class_weight.reshape(1, -1),
+        jnp.swapaxes(patches[0], 1, 2), embedding, weights[2], weights[3], classifier, weights[1],
     )
     *grads, info = gradient_sums(G, DP, MP, big, sm, acts, fac, shapes, (*weights, *firsts, *seconds))
     out_shapes = tuple(a.shape for a in (*weights, *firsts, *seconds, *outers))

time: 273 us -> 215 us (0.79)
  Pallas kernels: 258 us -> 214 us
  local copies, waits for them, and re-layouts: 13.8 us -> 0 us
    pallas_call x2 -> x1, Pallas kernels: 171 us -> 126 us  [local_step(): pl.pallas_call(functools.partial(step_kernel, G, DP, MP, NI, ncls), out_s...]
    unnamed x11 -> x0, local copies, waits for them, and re-layouts: 13.7 us -> none
where the time goes in v3:
time: 215 us; the launch traced here: 214 us
  Pallas kernels  214 us (100%)
    pallas_call x1, Pallas kernels, local_step(): pl.pallas_call(functools.partial(step_kernel, G, DP, MP, NI, ncls), out_s...  126 us
    pallas_call x1, Pallas kernels, gradient_sums(): pl.pallas_call(functools.partial(sum_kernel, G, DP, MP), out_shape=(s((DP...  78.5 us
    pallas_call x1, Pallas kernels, finish(): pl.pallas_call(functools.partial(finish_kernel, G), out_shape=tuple((jax....  8.92 us

profile of v3, /device:TPU:0, one launch (start us, length us, event | category | flops | bytes accessed | tf_op | source)
XLA Modules:
  0.0 214.4 jit_solution(17409635043797068370)
XLA Ops:
  0.7 126.1 %shard_map.535 = (f32[4,576,384]{2,1,0:T(8,128)}, f32[4,72,256]{2,1,0:T(8,128)}, f32[4,16,384]{2,1,0:T(8,128)}, bf16[4,48,384]{2,1,0:T(8,128)(2,1)}) custom-call(s32[48]{0:T(128)} %bitcast.97, s32[48]{0:T(128)} %bitcast.98, f32[5,96]{1,0:T(8,128)} %refs_13_.1, f32[5,96]{1,0:T(8,128)} %refs_14_.1, f32[1,1000]{1,0:T(1,128)} %bitcast.96, ...), custom_call_target="tpu_custom_call" | custom-call | tf_op jit(solution)/shard_map/pallas_call | solution.py:449
  126.8 78.5 %shard_map.536 = (f32[576,384]{1,0:T(8,128)}, f32[224,256]{1,0:T(8,128)}, f32[384,384]{1,0:T(8,128)}, f32[392,256]{1,0:T(8,128)}, f32[16,128]{1,0:T(8,128)}, /*i...) custom-call(f32[4,576,384]{2,1,0:T(8,128)} %get-tuple-element.72.big, f32[4,72,256]{2,1,0:T(8,128)} %get-tuple-element.73.sm, ...), custom_call_target="tpu_custom_call" | custom-call | tf_op jit(solution)/shard_map/pallas_call | solution.py:758
  205.3 8.9 %shard_map.537 = (f32[1,2]{1,0:T(1,128)}, f32[1,1]{1,0:T(1,128)}, f32[192,384]{1,0:T(8,128)}, f32[196,1,197]{2,1,0:T(1,128)}, f32[385,1,384]{2,1,0:T(1,128)}, /*...) custom-call(f32[8,128]{1,0:T(8,128)} %get-tuple-element.76.refs_0_, ...), custom_call_target="tpu_custom_call" | custom-call | tf_op jit(solution)/shard_map/pallas_call | solution.py:874

commit v4 on v3

v4 whole, which is shorter than its diff:
```python
import functools

import jax
import jax.numpy as jnp
from jax import lax
from jax.experimental import pallas as pl
from jax.experimental.pallas import tpu as pltpu
from jax.sharding import PartitionSpec as P

F32 = jnp.float32
BF16 = jnp.bfloat16
MESH = pl.DeviceIdType.MESH
VMEM = pltpu.VMEM
SMEM = pltpu.SMEM

D = 384
PATCHES = 196
ROWS = 208
MAIN = 192
STEP = 10
LANE = 128

mix_share = 0.7
clip_limit = 0.01
beta_one = 0.9
beta_two = 0.999
adam_eps = 1e-08
weight_decay = 0.05
matrix_rate = 0.05
head_rate = 0.5
vector_rate = 0.4
outer_rate = 0.7
outer_momentum = 0.9

GELU_A = 0.7978845608028654
GELU_B = GELU_A * 0.044715

S_VEC, S_ROWS = 56, 72
C_CLS, C_MIX, C_VEC, C_ROWS = 0, 392, 592, 608
E_EXP, E_EMB, E_ROWS = 0, 392, 608


def dot(a, b, dims=((1,), (0,)), precision=None):
    return lax.dot_general(
        a, b, (dims, ((), ())), preferred_element_type=F32, precision=precision
    )


def thirds(a, axis):
    high = a.astype(BF16)
    rest = a - high.astype(F32)
    middle = rest.astype(BF16)
    low = (rest - middle.astype(F32)).astype(BF16)
    return jnp.concatenate([high, middle, low], axis=axis)


def rounded(a):
    return a.astype(BF16).astype(F32)


def greet(peers):
    barrier = pltpu.get_barrier_semaphore()
    for peer in peers:
        pl.semaphore_signal(barrier, inc=1, device_id=peer, device_id_type=MESH)
    pl.semaphore_wait(barrier, len(peers))


def remote(src, dst, send_sem, recv_sem, peer):
    return pltpu.make_async_remote_copy(
        src_ref=src, dst_ref=dst, send_sem=send_sem, recv_sem=recv_sem,
        device_id=peer, device_id_type=MESH,
    )


CHUNK = 256
AHEAD = 2
SLOTS = AHEAD + 1


def waves_of(pairs):
    cuts = list(range(0, pairs - 1, 2)) + [pairs - 1, pairs]
    return list(zip(cuts[:-1], cuts[1:], strict=True))


def part_rows(rows, DP):
    return -(-rows // (16 * DP)) * 16


def adamw(weight, gradient, moment_one, moment_two, rate):
    mean_new = beta_one * moment_one + (1.0 - beta_one) * gradient
    square_new = beta_two * moment_two + (1.0 - beta_two) * gradient * gradient
    mean_hat = mean_new * (1.0 / (1.0 - beta_one**STEP))
    square_hat = square_new * (1.0 / (1.0 - beta_two**STEP))
    return rate * (mean_hat / (jnp.sqrt(square_hat) + adam_eps) + weight_decay * weight)


def flat(ref):
    return ref.at[:, 0, :] if len(ref.shape) == 3 and ref.shape[1] == 1 else ref


def step_kernel(G, DP, MP, NI, ncls, *refs):
    (labels, partner, sca, shi, class_weight, patches), refs = refs[:6], refs[6:]
    states, refs = refs[:21], refs[21:]
    (g_w, g_e, g_mix, g_shr, g_cls, g_vec, sum_s, sum_c, sum_e, info), refs = refs[:10], refs[10:]
    held, refs = list(refs[:17]), refs[17:]
    (
        pv, stage, rows, e_all, w1, w2, wc, small,
        xs, gp, s0, s1, mx, mi, fi, ep, mm, mt, eye, mbias, vec, b1, cw, asum, s1sum, la, lb,
        dact, ds2, dh, csum, gw, ge, gm, gmb, gvec,
        sm, fac, zsm, ysm, yacts, yfac,
        ysw, yrw, zsw, zrw, yse, yre, zse, zre, nsq,
        h2s, h2c, h2e,
        load, rs_send, rs_recv, wz_send, wz_recv, wg_send, wg_recv, sm_send, sm_recv,
        zf_s, zf_r, yf_s, yf_r, yw_s, yw_r, zw_s, zw_r, ye_s, ye_r, ze_s, ze_r, ag_s, ag_r,
        nm_s, nm_r, nq_s, nq_r, g_s, g_r,
    ) = refs
    late = {7: mx.at[0, 0 : held[0].shape[0], :], 14: mx.at[1, 0 : held[0].shape[0], :]}
    late |= {10: s1.at[0, 0:D, :], 17: s1.at[1, 0:D, :]}
    for k in sorted(late):
        held.insert(k, late[k])
    emb, mixing, expa, shr, cls = held[:5]
    z = lax.axis_index("mp")
    y = lax.axis_index("dp")
    g = lax.axis_index("group")
    NP = NI // 2
    PR = 2 * ROWS
    hid = expa.shape[1]
    hid_all = hid * MP
    cpad = wc.shape[1] // MP
    er = emb.shape[0]
    NCH = hid_all // CHUNK
    PW, PE = g_w.shape[0] // DP, g_e.shape[0] // DP
    pair = 2 if DP % 2 == 0 else 1

    loads = [pltpu.make_async_copy(flat(a), b, load.at[k]) for k, (a, b) in enumerate(zip(states, held, strict=True))]
    load_patches = pltpu.make_async_copy(patches, pv, load.at[21])
    loads[0].start()
    loads[2].start()
    load_patches.start()
    for k in range(21):
        if k not in (0, 2, *late):
            loads[k].start()

    zpeer = [lax.rem(z + d, MP) for d in range(1, MP)]
    half = lax.rem(y, pair)
    plane, plane_far = [], []
    for e in range(pair):
        for d in range(G):
            if d or e:
                j = lax.rem(g + d, G)
                h = half if e == 0 else 1 - half
                plane_far.append(d > 0)
                plane.append((j, y if e == 0 else y + 1 - 2 * half, j * pair + h, e))
    place = g * pair + half
    parts = G * pair
    ypeer = [lax.rem(y + d, DP) for d in range(1, DP)]
    others = [{"mp": lax.rem(z + c, MP), "dp": lax.rem(y + d, DP)} for d in range(DP) for c in range(MP) if c or d]
    greet(others + [{"group": j, "dp": u} for (j, u, _, _), far in zip(plane, plane_far, strict=True) if far])

    def pieces(t, j):
        ee, hh, dd = er // G, hid // parts, D // parts
        return (
            e_all.at[t, pl.ds(pl.multiple_of(j // pair * ee, 16), ee), :],
            w1.at[pl.ds(pl.multiple_of(j * dd, 16), dd), pl.ds(pl.multiple_of(t * hid, LANE), hid)],
            w2.at[pl.ds(pl.multiple_of(t * hid + j * hh, 16), hh), :],
            wc.at[pl.ds(pl.multiple_of(j * dd, 16), dd), pl.ds(pl.multiple_of(t * cpad, LANE), cpad)],
        )

    started = []

    def go(*args):
        c = remote(*args)
        c.start()
        started.append(c)

    def spread(k):
        part = pieces(z, place)[k]
        for d, t in enumerate(zpeer):
            go(part, part, wz_send.at[d, k], wz_recv.at[z, k], {"mp": t})

    def pass_on(k):
        for d in range(1, MP):
            t = lax.rem(z + MP - d, MP)
            part = pieces(t, place)[k]
            remote(part, part, wz_send.at[d - 1, k], wz_recv.at[t, k], {"mp": t}).wait_recv()
            for e, (j, u, _, other) in enumerate(plane):
                if k or not other:
                    go(part, part, wg_send.at[d - 1, e, k], wg_recv.at[t, place, k], {"group": j, "dp": u})

    def gathered(k):
        for t in zpeer:
            for j, u, at, other in plane:
                if k or not other:
                    part = pieces(t, at)[k]
                    remote(part, part, wg_send.at[0, 0, k], wg_recv.at[t, at, k], {"group": j, "dp": u}).wait_recv()

    loads[0].wait()
    e_all[z] = emb[...].astype(BF16)
    spread(0)
    loads[2].wait()
    w1[:, pl.ds(pl.multiple_of(z * hid, LANE), hid)] = expa[0:D, :].astype(BF16)
    spread(1)

    row = lax.broadcasted_iota(jnp.int32, (ROWS, PATCHES), 0)
    column = lax.broadcasted_iota(jnp.int32, (ROWS, PATCHES), 1)
    eye[...] = jnp.where(row == column, 1.0, 0.0).astype(BF16)
    share = F32(mix_share)
    rest = F32(1.0 - mix_share)

    def blend(i):
        return (share * pv[i] + rest * pv[partner[i]]).astype(BF16)

    def blend_pair(t, p, ref, lead):
        a = blend(t * NI + 2 * p)
        b = blend(t * NI + 2 * p + 1)
        both = jnp.concatenate([a[0:LANE], b[0:LANE], a[LANE:], b[LANE:]], axis=0)
        turned = dot(eye[...], both, ((1,), (1,)))
        tail = None
        for k in range(3):
            lanes = turned[:, k * LANE : (k + 1) * LANE]
            ref[lead + (slice(k * MAIN, (k + 1) * MAIN), slice(None))] = lanes[0:MAIN].astype(BF16)
            last = lanes[MAIN:ROWS]
            tail = last if k == 0 else tail + pltpu.roll(last, k * (PATCHES - MAIN), 0)
        ref[lead + (slice(3 * MAIN, 3 * MAIN + 16), slice(None))] = tail.astype(BF16)

    def slab(t, p, k):
        tail = rows[t, p, 3 * MAIN :, :].astype(F32)
        if k:
            tail = pltpu.roll(tail, 16 - k * (PATCHES - MAIN), 0)
        row = lax.broadcasted_iota(jnp.int32, (16, LANE), 0)
        tail = jnp.where(row < PATCHES - MAIN, tail, 0.0).astype(BF16)
        return rows[t, p, k * MAIN : (k + 1) * MAIN, :], tail

    def send(p, d):
        slot = lax.rem(p, SLOTS)
        return remote(stage.at[d, slot], rows.at[z, p], rs_send.at[d, slot], rs_recv.at[z, p], {"mp": zpeer[d]})

    def issue(p):
        for d in range(MP - 1):
            blend_pair(zpeer[d], p, stage, (d, lax.rem(p, SLOTS)))
            send(p, d).start()

    load_patches.wait()
    issue(0)

    loads[3].wait()
    w2[pl.ds(pl.multiple_of(z * hid, 16), hid), :] = shr[...].astype(BF16)
    loads[4].wait()
    head = jnp.concatenate([cls[0:D, :], jnp.zeros((D, cpad - ncls), F32)], axis=1)
    wc[:, pl.ds(pl.multiple_of(z * cpad, LANE), cpad)] = head.astype(BF16)
    spread(2)
    spread(3)
    small[z] = jnp.zeros(small.shape[1:], F32)
    small[z, 0:5, 0 : D // MP] = sca[...]
    small[z, 5:10, 0 : D // MP] = shi[...]
    small[z, 10:11, :] = rounded(expa[D : D + 1, :])
    small[z, 11:12, 0:ncls] = rounded(cls[D : D + 1, :])
    for d, t in enumerate(zpeer):
        go(small.at[z], small.at[z], sm_send.at[d], sm_recv.at[z], {"mp": t})
    for p in range(1, min(AHEAD, NP)):
        issue(p)
    pass_on(0)
    pass_on(1)

    loads[1].wait()
    wide = jnp.concatenate([mixing[...], jnp.zeros((PATCHES, 256 - PATCHES - 1), F32)], axis=1)
    wide = jnp.concatenate([wide, jnp.zeros((256 - PATCHES, 256), F32)], axis=0)
    column = lax.broadcasted_iota(jnp.int32, (256, 256), 1)
    square = jnp.where(column < PATCHES, wide, 0.0)
    mm[...] = square[0:ROWS, 0:ROWS].astype(BF16)
    mt[...] = jnp.transpose(square)[0:ROWS, 0:ROWS].astype(BF16)
    mbias[...] = rounded(jnp.sum(jnp.where(column == PATCHES, wide, 0.0), axis=1, keepdims=True)[0:ROWS])
    for t in range(MP):
        block = class_weight[:, t * ncls : (t + 1) * ncls]
        cw[:, t * cpad : (t + 1) * cpad] = jnp.concatenate([block, jnp.zeros((1, cpad - ncls), F32)], axis=1)
    asum[...] = jnp.zeros_like(asum)
    s1sum[...] = jnp.zeros_like(s1sum)
    csum[...] = jnp.zeros_like(csum)
    gw[...] = jnp.zeros_like(gw)
    ge[...] = jnp.zeros_like(ge)
    gm[...] = jnp.zeros_like(gm)
    gmb[...] = jnp.zeros_like(gmb)
    gvec[...] = jnp.zeros_like(gvec)
    la[...] = jnp.full(la.shape, -1, jnp.int32)
    lb[...] = jnp.full(lb.shape, -1, jnp.int32)
    for i in range(NI):
        own = labels[z * NI + i]
        mate = labels[partner[z * NI + i]]
        la[i : i + 1, :] = jnp.full((1, LANE), own, jnp.int32)
        lb[i : i + 1, :] = jnp.full((1, LANE), mate, jnp.int32)

    for t in zpeer:
        remote(small.at[t], small.at[t], sm_send.at[0], sm_recv.at[t], {"mp": t}).wait_recv()
    full = jnp.zeros((16, D), F32)
    for t in range(MP):
        block = small[t]
        full = full + (pltpu.roll(block, t * (D // MP), 1) if t else block)
        b1[:, t * hid : (t + 1) * hid] = small[t, 10:11, :]
    vec[...] = full
    gathered(0)
    rest_rows = er - LANE
    for t in range(MP):
        ep[t * LANE : (t + 1) * LANE, :] = e_all[t, 0:LANE, :]
        ep[MP * LANE + t * rest_rows : MP * LANE + (t + 1) * rest_rows, :] = e_all[t, LANE:er, :]
    gathered(1)
    pass_on(2)
    pass_on(3)

    def scale(k):
        return vec[k : k + 1, :]

    def shift(k):
        return vec[5 + k : 6 + k, :]

    def forward(base, p, carry):
        @pl.when(p + AHEAD < NP)
        def _():
            @pl.when(p + AHEAD >= SLOTS)
            def _():
                for d in range(MP - 1):
                    send(p + AHEAD - SLOTS, d).wait_send()

            issue(p + AHEAD)

        q = p - base
        blend_pair(z, p, rows, (z, p))
        for t in zpeer:
            remote(stage.at[0, 0], rows.at[t, p], rs_send.at[0, 0], rs_recv.at[t, p], {"mp": t}).wait_recv()
        for t in range(MP):
            lanes = slice(t * LANE, (t + 1) * LANE)
            for k in range(2):
                xs[q, k * ROWS : k * ROWS + MAIN, lanes], xs[q, k * ROWS + MAIN : (k + 1) * ROWS, lanes] = slab(t, p, k)
        for t in range(0, MP, 2):
            lanes = slice(MP * LANE + t * 64, MP * LANE + t * 64 + LANE)
            left, right = slab(t, p, 2), slab(t + 1, p, 2)
            for k in range(2):
                half = slice(k * 64, (k + 1) * 64)
                main, tail = (jnp.concatenate([v[:, half], w[:, half]], axis=1) for v, w in zip(left, right, strict=True))
                xs[q, k * ROWS : k * ROWS + MAIN, lanes] = main
                xs[q, k * ROWS + MAIN : (k + 1) * ROWS, lanes] = tail
        stream0 = dot(xs[q], ep[...]) + shift(3)
        s0[q] = stream0
        mi[q] = (scale(0) * stream0 + shift(0)).astype(BF16)
        for b in range(2):
            r = slice(b * ROWS, (b + 1) * ROWS)
            mixed = dot(mm[...], mi[q, r, :]) + mbias[...]
            mx[q, r, :] = mixed
            stream1 = s0[q, r, :] + scale(1) * mixed
            s1[q, r, :] = stream1
            fi[q, r, :] = (scale(2) * stream1 + shift(1)).astype(BF16)
            s1sum[pl.ds(2 * p + b, 1), :] = jnp.sum(stream1[0:PATCHES], axis=0, keepdims=True)

        def chunk(c, carry):
            cols = pl.ds(pl.multiple_of(c * CHUNK, CHUNK), CHUNK)
            for b in range(2):
                r = slice(b * ROWS, (b + 1) * ROWS)
                h = dot(fi[q, r, :], w1[:, cols]) + b1[:, cols]
                sq = h * h
                s = 0.5 * jnp.tanh(h * (GELU_A + GELU_B * sq)) + 0.5
                act = rounded(h * s)
                asum[pl.ds(2 * p + b, 1), cols] = jnp.sum(act[0:PATCHES], axis=0, keepdims=True)
                gp[q, r, cols] = s + s * (1.0 - s) * (h * (2.0 * GELU_A + 6.0 * GELU_B * sq))
                gp[q, b * ROWS + PATCHES : (b + 1) * ROWS, cols] = jnp.zeros((ROWS - PATCHES, CHUNK), F32)
            return carry

        lax.fori_loop(0, NCH, chunk, 0)
        return carry

    def class_head():
        three = dot(thirds(asum[...], 0), w2[...])
        outsum = three[0:16] + three[16:32] + three[32:48] + PATCHES * shift(2)
        stream2 = s1sum[...] + scale(3) * outsum
        pooled = (scale(4) * (stream2 * (1.0 / PATCHES)) + shift(4)).astype(BF16)
        bias = jnp.concatenate([small[t, 11:12, 0:cpad] for t in range(MP)], axis=1)
        lane = lax.broadcasted_iota(jnp.int32, (16, cpad * MP), 1)
        inside = lax.rem(lane, cpad)
        valid = inside < ncls
        class_id = (lane // cpad) * ncls + inside
        logits = jnp.where(valid, dot(pooled, wc[...]) + bias, -1e30)
        hot_a = jnp.where(valid & (class_id == la[:, 0:1]), 1.0, 0.0)
        hot_b = jnp.where(valid & (class_id == lb[:, 0:1]), 1.0, 0.0)
        weight_a = mix_share * jnp.sum(hot_a * cw[...], axis=1, keepdims=True)
        weight_b = (1.0 - mix_share) * jnp.sum(hot_b * cw[...], axis=1, keepdims=True)
        top = jnp.max(logits, axis=1, keepdims=True)
        exps = jnp.where(valid, jnp.exp(logits - top), 0.0)
        exp_sum = jnp.sum(exps, axis=1, keepdims=True)
        soft = exps / exp_sum
        dlog = ((weight_a + weight_b) * soft - weight_a * hot_a - weight_b * hot_b).astype(BF16)
        dfinal = dot(dlog, wc[...], ((1,), (1,))) * (1.0 / PATCHES)
        dstream2 = scale(4) * dfinal
        ds2[...] = dstream2
        dout = scale(3) * dstream2
        low = dout.astype(BF16)
        dact[...] = dot(low, w2[...], ((1,), (1,)))

        def last():
            log_total = top + jnp.log(exp_sum)
            target_a = jnp.sum(hot_a * logits, axis=1, keepdims=True)
            target_b = jnp.sum(hot_b * logits, axis=1, keepdims=True)
            loss = weight_a * (log_total - target_a) + weight_b * (log_total - target_b)
            loss = jnp.sum(loss, axis=0, keepdims=True)
            total = jnp.sum(weight_a + weight_b, axis=0, keepdims=True)
            fac[:, 0:16, :] = jnp.broadcast_to(low[None], (MP, 16, D))
            fac[:, 16:32, :] = jnp.broadcast_to(pooled[None], (MP, 16, D))
            for t in range(MP):
                fac[t, 32:48, 0:cpad] = dlog[:, t * cpad : (t + 1) * cpad]
                fac[t, 32:48, cpad:] = jnp.zeros((16, D - cpad), BF16)
            gvec[3:4, :] = jnp.sum(outsum * dstream2, axis=0, keepdims=True)
            gvec[4:5, :] = jnp.sum(dfinal * stream2, axis=0, keepdims=True)
            gvec[7:8, :] = PATCHES * jnp.sum(dout, axis=0, keepdims=True)
            gvec[8:9, :] = PATCHES * jnp.sum(dstream2, axis=0, keepdims=True)
            gvec[9:10, :] = PATCHES * jnp.sum(dfinal, axis=0, keepdims=True)
            lane = lax.broadcasted_iota(jnp.int32, (1, D), 1)
            gvec[10:11, :] = jnp.where(lane == 0, loss, jnp.where(lane == 1, total, 0.0))

        return last

    def backward_hidden(base, p):
        q = p - base

        def chunk(c, carry):
            cols = pl.ds(pl.multiple_of(c * CHUNK, CHUNK), CHUNK)
            for b in range(2):
                r = slice(b * ROWS, (b + 1) * ROWS)
                dh[r, cols] = (gp[q, r, cols] * dact[pl.ds(2 * p + b, 1), cols]).astype(BF16)
            value = dh[:, cols]
            csum[0:1, cols] += jnp.sum(value.astype(F32), axis=0, keepdims=True)
            gw[0:D, cols] += dot(fi[q], value, ((0,), (0,)))
            return carry

        lax.fori_loop(0, NCH, chunk, 0)

    def backward_rest(base, p):
        q = p - base
        dffn = dot(dh[...], w1[...], ((1,), (1,)))
        gvec[2:3, :] += jnp.sum(dffn * s1[q], axis=0, keepdims=True)
        gvec[6:7, :] += jnp.sum(dffn, axis=0, keepdims=True)
        for b in range(2):
            r = slice(b * ROWS, (b + 1) * ROWS)
            d1 = ds2[pl.ds(2 * p + b, 1), :] + scale(2) * dffn[r]
            gvec[1:2, :] += jnp.sum(mx[q, r, :] * d1, axis=0, keepdims=True)
            dmixed = (scale(1) * d1).astype(BF16)
            gm[...] += dot(dmixed, mi[q, r, :], ((1,), (1,)))
            gmb[...] += dmixed.astype(F32)
            dmixer = dot(mt[...], dmixed)
            gvec[0:1, :] += jnp.sum(dmixer * s0[q, r, :], axis=0, keepdims=True)
            gvec[5:6, :] += jnp.sum(dmixer, axis=0, keepdims=True)
            d0 = (d1 + scale(0) * dmixer).astype(BF16)
            grad = dot(xs[q, r, :], d0, ((0,), (0,)))
            for t in range(MP):
                ge[t, 0:LANE, :] += grad[t * LANE : (t + 1) * LANE]
                ge[t, LANE:er, :] += grad[MP * LANE + t * rest_rows : MP * LANE + (t + 1) * rest_rows]

    def backward(base, p, carry):
        backward_hidden(base, p)
        backward_rest(base, p)
        return carry

    for n, (lo, hi) in enumerate(waves_of(NP)):
        lax.fori_loop(lo, hi, functools.partial(forward, lo), 0)
        if n == 0:
            gathered(2)
            gathered(3)
        last = class_head()
        if hi < NP:
            lax.fori_loop(lo, hi, functools.partial(backward, lo), 0)

    def arrived(dst, sem, peer):
        remote(dst, dst, sem, sem, peer).wait_recv()

    def columns(t):
        return pl.ds(pl.multiple_of(t * hid, LANE), hid)

    def part(u, n):
        return pl.ds(pl.multiple_of(u * n, 8), n)

    last()
    yacts[y, z] = asum[:, columns(z)]
    yfac[y, z] = fac[z]
    for d, v in enumerate(zpeer):
        go(asum.at[:, columns(v)], yacts.at[y, z], zf_s.at[d, 0], zf_r.at[z, 0], {"mp": v})
        go(fac.at[v], yfac.at[y, z], zf_s.at[d, 1], zf_r.at[z, 1], {"mp": v})
    order = zpeer + [z]
    backward_hidden(lo, lo)
    for i, t in enumerate(order):
        for d, u in enumerate(ypeer):
            ysw[i, d] = gw[part(u, PW), columns(t)].astype(BF16)
            go(ysw.at[i, d], yrw.at[t, d], yw_s.at[i, d], yw_r.at[t, d], {"dp": u})
    backward_rest(lo, lo)
    for i, t in enumerate(order):
        for d, u in enumerate(ypeer):
            yse[i, d] = ge[t, part(u, PE), :].astype(BF16)
            go(yse.at[i, d], yre.at[t, d], ye_s.at[i, d], ye_r.at[t, d], {"dp": u})

    for k in late:
        loads[k].start()

    gvec[8:9, :] += scale(2) * gvec[6:7, :] + scale(0) * gvec[5:6, :]
    row = lax.broadcasted_iota(jnp.int32, (ROWS, 256), 0)
    column = lax.broadcasted_iota(jnp.int32, (ROWS, 256), 1)
    bias_grad = jnp.sum(gmb[...], axis=1, keepdims=True)
    grad = jnp.concatenate([gm[...], jnp.zeros((ROWS, 256 - ROWS), F32)], axis=1)
    grad = jnp.where(column < PATCHES, grad, jnp.where(column == PATCHES, bias_grad, 0.0))
    grad = jnp.where(row < PATCHES, grad, 0.0)
    own = D // MP
    lane = lax.broadcasted_iota(jnp.int32, (16, LANE), 1)
    for t in range(MP):
        n = min(S_VEC, ROWS - t * S_VEC)
        sm[t, 0:n, :] = grad[t * S_VEC : t * S_VEC + n]
        if n < S_VEC:
            sm[t, n:S_VEC, :] = jnp.zeros((S_VEC - n, 256), F32)
        vector = gvec[...]
        if t:
            vector = pltpu.roll(vector, D - t * own, 1)
        sm[t, S_VEC:S_ROWS, 0:LANE] = jnp.where(lane < own, vector[:, 0:LANE], 0.0)
        sm[t, S_VEC:S_ROWS, LANE:] = jnp.zeros((16, LANE), F32)
        sm[t, S_VEC + 10 : S_VEC + 11, 0:LANE] = gvec[10:11, 0:LANE]
        for k in range(hid // LANE):
            at = t * hid + k * LANE
            sm[t, S_VEC + 11 + k : S_VEC + 12 + k, 0:LANE] = csum[:, at : at + LANE]
    zsm[z] = sm[z]
    for d, v in enumerate(zpeer):
        go(sm.at[v], zsm.at[z], zf_s.at[d, 2], zf_r.at[z, 2], {"mp": v})

    for v in zpeer:
        arrived(yacts.at[y, v], zf_r.at[v, 0], {"mp": v})
        arrived(yfac.at[y, v], zf_r.at[v, 1], {"mp": v})
    for d, u in enumerate(ypeer):
        go(yacts.at[y], yacts.at[y], yf_s.at[d, 1], yf_r.at[y, 1], {"dp": u})
        go(yfac.at[y], yfac.at[y], yf_s.at[d, 2], yf_r.at[y, 2], {"dp": u})

    def from_dp(first, received, sems, send, out, out_sems, z_sems, n):
        for i, t in enumerate(order):
            value = first(t)
            for d in range(DP - 1):
                arrived(received.at[t, d], sems.at[t, d], {"dp": ypeer[d]})
                value = value + received[t, d].astype(F32)
            if i < MP - 1:
                send[i] = value.astype(BF16)
                go(send.at[i], out.at[i], out_sems.at[i], z_sems.at[i], {"mp": t})
        return value

    g_w[part(y, PW), :] = from_dp(lambda t: gw[part(y, PW), columns(t)], yrw, yw_r, zsw, zrw, zw_s, zw_r, PW)

    for v in zpeer:
        arrived(zsm.at[v], zf_r.at[v, 2], {"mp": v})
    summed = zsm[0]
    for v in range(1, MP):
        summed = summed + zsm[v]
    ysm[y] = summed
    for d, u in enumerate(ypeer):
        go(ysm.at[y], ysm.at[y], yf_s.at[d, 0], yf_r.at[y, 0], {"dp": u})

    g_e[part(y, PE), :] = from_dp(lambda t: ge[t, part(y, PE), :], yre, ye_r, zse, zre, ze_s, ze_r, PE)

    shared = []

    def from_mp(total, received, sems, n, k):
        value = total[part(y, n), :]
        for i in range(MP - 1):
            arrived(received.at[i], sems.at[i], {"mp": zpeer[i]})
            value = value + received[i].astype(F32)
        total[part(y, n), :] = value
        for d, u in enumerate(ypeer):
            c = remote(total.at[part(y, n), :], total.at[part(y, n), :], ag_s.at[d, k], ag_r.at[y, k], {"dp": u})
            c.start()
            shared.append(c)
        return value

    def squares(v):
        return jnp.sum(jnp.sum(v * v, axis=0, keepdims=True), axis=1, keepdims=True)

    mine = squares(from_mp(g_w, zrw, zw_r, PW, 0))

    for u in ypeer:
        arrived(ysm.at[u], yf_r.at[u, 0], {"dp": u})
    summed = ysm[0]
    for u in range(1, DP):
        summed = summed + ysm[u]
    g_mix[part(z, S_VEC), :] = summed[0:S_VEC]
    for d, v in enumerate(zpeer):
        go(g_mix.at[part(z, S_VEC), :], g_mix.at[part(z, S_VEC), :], nm_s.at[d], nm_r.at[z], {"mp": v})
    vector = summed[S_VEC:S_ROWS, 0:LANE]

    for u in ypeer:
        arrived(yacts.at[u], yf_r.at[u, 1], {"dp": u})
        arrived(yfac.at[u], yf_r.at[u, 2], {"dp": u})
    n = 16 * MP
    grad_shr = jnp.zeros((hid, D), F32)
    grad_cls = jnp.zeros((D, cpad), F32)
    cls_bias = jnp.zeros((1, cpad), F32)
    for u in range(DP):
        whole = yfac[u]
        dout = whole[:, 0:16, :].reshape(n, D)
        pooled = whole[:, 16:32, :].reshape(n, D)
        dlog = whole[:, 32:48, 0:cpad].reshape(n, cpad)
        three = thirds(yacts[u].reshape(n, hid), 0)
        grad_shr = grad_shr + dot(three, jnp.concatenate([dout] * 3, axis=0), ((0,), (0,)))
        grad_cls = grad_cls + dot(pooled, dlog, ((0,), (0,)))
        cls_bias = cls_bias + jnp.sum(dlog.astype(F32), axis=0, keepdims=True)
    g_shr[...] = grad_shr
    g_cls[0:D, :] = grad_cls
    g_cls[D:, :] = jnp.concatenate([cls_bias, jnp.zeros((g_cls.shape[0] - D - 1, cpad), F32)], axis=0)
    once = squares(grad_shr) + squares(grad_cls) + squares(cls_bias) + squares(summed[0:S_VEC])
    once = once + squares(vector[0:10]) + squares(vector[11 : 11 + hid // LANE])

    mine = mine + squares(from_mp(g_e, zre, ze_r, PE, 1))
    nsq[y, z] = jnp.broadcast_to(mine + jnp.where(y == 0, once, 0.0), (8, LANE))
    for k, peer in enumerate(others):
        go(nsq.at[y, z], nsq.at[y, z], nq_s.at[k], nq_r.at[y, z], peer)
    for k in range(4, 21):
        if k != 4:
            loads[k].wait()
    for v in zpeer:
        arrived(g_mix.at[part(v, S_VEC), :], nm_r.at[v], {"mp": v})
    for peer in others:
        arrived(nsq.at[peer["dp"], peer["mp"]], nq_r.at[peer["dp"], peer["mp"]], peer)
    square = jnp.zeros((1, 1), F32)
    for u in range(DP):
        for v in range(MP):
            square = square + nsq[u, v, 0:1, 0:1]
    loss_sum = vector[10:11, 0:1]
    weight_total = vector[10:11, 1:2]
    size = jnp.sqrt(square) / weight_total
    factor = clip_limit / jnp.maximum(size, clip_limit)
    scaled = factor / weight_total
    lane = lax.broadcasted_iota(jnp.int32, (8, LANE), 1)
    info[...] = jnp.where(
        lane == 0, loss_sum, jnp.where(lane == 1, weight_total, jnp.where(lane == 2, size, scaled))
    )

    (_, _, _, _, _, sca_w, shi_w) = held[:7]
    (emb1, mixing1, expa1, shr1, cls1, sca1, shi1) = held[7:14]
    (emb2, mixing2, expa2, shr2, cls2, sca2, shi2) = held[14:21]
    wide = sca_w.shape[1]
    gstep = [g + 1 - 2 * lax.rem(g, 2), lax.rem(g + 2, 4)]
    near, far = {"group": gstep[0]}, {"group": gstep[1]}
    core = lax.rem(g, 2)

    def halves(ref, k):
        n = ref.shape[0] // 2
        return ref.at[pl.ds(pl.multiple_of(k * n, 8), n), :]

    mvs = gp.at[0:2, 0 : hid // 2, 0:D]
    mvc = gp.at[0:2, 0 : C_ROWS // 2, D : D + 256]
    mve = gp.at[0:2, 0 : E_ROWS // 2, D + 256 : 2 * D + 256]

    def put(moved, at, value):
        n = moved.shape[1]
        rows, width = value.shape
        k = min(max(n - at, 0), rows)
        if k:
            moved[0, at : at + k, 0:width] = value[0:k]
        if k < rows:
            moved[1, at + k - n : at + rows - n, 0:width] = value[k:]

    fine = C_VEC - C_ROWS // 2

    def first_step(k, moved, out):
        go(moved.at[1 - core], halves(out, 1 - core), g_s.at[k, 0], g_r.at[k, 0], near)

    def second_step(k, moved, out, pairs):
        arrived(halves(out, core), g_r.at[k, 0], near)
        n = moved.shape[1]
        value = moved[core] + out[part(core, n), :]
        pairs[0, 0:n] = value.astype(BF16)
        if pairs.shape[1] > n:
            value = value[fine : fine + 16]
            pairs[0, n:] = (value - rounded(value)).astype(BF16)
        go(pairs.at[0], pairs.at[1], g_s.at[k, 1], g_r.at[k, 1], far)

    def third_step(k, pairs, out):
        arrived(pairs.at[1], g_r.at[k, 1], far)
        n = out.shape[0] // 2
        total = pairs[0].astype(F32) + pairs[1].astype(F32)
        out[part(core, n), :] = total[0:n]
        if pairs.shape[1] > n:
            out[pl.ds(pl.multiple_of(core * n + fine, 8), 16), :] = total[fine : fine + 16] + total[n:]
        go(halves(out, core), halves(out, core), g_s.at[k, 2], g_r.at[k, 2], near)

    put(mvs, 0, adamw(shr[...], g_shr[...] * scaled, shr1[...], shr2[...], matrix_rate))
    first_step(0, mvs, sum_s)
    mvc[...] = jnp.zeros(mvc.shape, F32)
    put(mvc, C_CLS, adamw(cls[...], g_cls[0 : D + 1, 0:ncls] * scaled, cls1[...], cls2[...], head_rate))
    put(
        mvc, C_MIX,
        adamw(mixing[...], g_mix[0:PATCHES, 0 : PATCHES + 1] * scaled, mixing1[...], mixing2[...], matrix_rate),
    )
    g_vec[...] = vector
    for k, (w, one, two) in enumerate(((sca_w, sca1, sca2), (shi_w, shi1, shi2))):
        value = adamw(w[...], g_vec[5 * k : 5 * k + 5, 0:wide] * scaled, one[...], two[...], vector_rate)
        put(mvc, C_VEC + 8 * k, value)
    first_step(1, mvc, sum_c)
    second_step(0, mvs, sum_s, h2s)
    for u in ypeer:
        arrived(g_w.at[part(u, PW), :], ag_r.at[u, 0], {"dp": u})
        arrived(g_e.at[part(u, PE), :], ag_r.at[u, 1], {"dp": u})
    bias = jnp.concatenate([g_vec[11 + k : 12 + k, :] for k in range(hid // LANE)], axis=1)
    last_row = slice(D, D + 1)
    mve[...] = jnp.zeros(mve.shape, F32)
    put(mve, E_EXP, adamw(expa[0:D, :], g_w[0:D, :] * scaled, expa1[0:D, :], expa2[0:D, :], matrix_rate))
    put(mve, E_EXP + D, adamw(expa[last_row, :], bias * scaled, expa1[last_row, :], expa2[last_row, :], matrix_rate))
    put(mve, E_EMB, adamw(emb[...], g_e[0:er, :] * scaled, emb1[...], emb2[...], matrix_rate))
    first_step(2, mve, sum_e)
    second_step(1, mvc, sum_c, h2c)
    second_step(2, mve, sum_e, h2e)
    third_step(0, h2s, sum_s)
    third_step(1, h2c, sum_c)
    third_step(2, h2e, sum_e)
    for k, out in enumerate((sum_s, sum_c, sum_e)):
        arrived(halves(out, 1 - core), g_r.at[k, 2], near)

    def drain(p, carry):
        for d in range(MP - 1):
            send(p, d).wait_send()
        return carry

    lax.fori_loop(max(NP - SLOTS, 0), NP, drain, 0)
    for c in started + shared:
        c.wait_send()


def local_step(G, DP, MP, shapes, labels, partner, sca, shi, class_weight, patches, states):
    NI = patches.shape[0] // MP
    NP = NI // 2
    PR = 2 * ROWS
    er, hid, ncls = shapes[0][0], shapes[2][1], shapes[4][1]
    hid_all = hid * MP
    pd = er * MP
    cpad = -(-ncls // LANE) * LANE
    wave = max(hi - lo for lo, hi in waves_of(NP))
    pair = 2 if DP % 2 == 0 else 1
    dp1 = max(DP - 1, 1)
    PW, PE = part_rows(D, DP), part_rows(er, DP)
    dma = pltpu.SemaphoreType.DMA
    vm = pl.BlockSpec(memory_space=VMEM)
    smem = pl.BlockSpec(memory_space=SMEM)
    hbm = pl.BlockSpec(memory_space=pl.ANY)
    s = jax.ShapeDtypeStruct
    return pl.pallas_call(
        functools.partial(step_kernel, G, DP, MP, NI, ncls),
        out_shape=(
            s((DP * PW, D), F32),
            s((DP * PE, D), F32),
            s((MP * S_VEC, 256), F32),
            s((hid, D), F32),
            s((392, cpad), F32),
            s((16, LANE), F32),
            s((hid, D), F32),
            s((C_ROWS, 256), F32),
            s((E_ROWS, D), F32),
            s((8, LANE), F32),
        ),
        in_specs=[smem, smem, vm, vm, vm] + [hbm] * 22,
        out_specs=(vm,) * 10,
        scratch_shapes=[VMEM(shape, F32) for shape in shapes + 2 * (shapes[1:3] + shapes[4:])]
        + [
            VMEM(patches.shape, F32),
            VMEM((MP - 1, SLOTS, 3 * MAIN + 16, LANE), BF16),
            VMEM((MP, NP, 3 * MAIN + 16, LANE), BF16),
            VMEM((MP, er, D), BF16),
            VMEM((D, hid_all), BF16),
            VMEM((hid_all, D), BF16),
            VMEM((D, cpad * MP), BF16),
            VMEM((MP, 16, hid), F32),
            VMEM((wave, PR, pd), BF16),
            VMEM((wave, PR, hid_all), F32),
            VMEM((wave, PR, D), F32),
            VMEM((wave, PR, D), F32),
            VMEM((wave, PR, D), F32),
            VMEM((wave, PR, D), BF16),
            VMEM((wave, PR, D), BF16),
            VMEM((pd, D), BF16),
            VMEM((ROWS, ROWS), BF16),
            VMEM((ROWS, ROWS), BF16),
            VMEM((ROWS, PATCHES), BF16),
            VMEM((ROWS, 1), F32),
            VMEM((16, D), F32),
            VMEM((1, hid_all), F32),
            VMEM((1, cpad * MP), F32),
            VMEM((16, hid_all), F32),
            VMEM((16, D), F32),
            VMEM((16, LANE), jnp.int32),
            VMEM((16, LANE), jnp.int32),
            VMEM((16, hid_all), F32),
            VMEM((16, D), F32),
            VMEM((PR, hid_all), BF16),
            VMEM((1, hid_all), F32),
            VMEM((DP * PW, hid_all), F32),
            VMEM((MP, DP * PE, D), F32),
            VMEM((ROWS, ROWS), F32),
            VMEM((ROWS, D), F32),
            VMEM((16, D), F32),
            VMEM((MP, S_ROWS, 256), F32),
            VMEM((MP, 48, D), BF16),
            VMEM((MP, S_ROWS, 256), F32),
            VMEM((DP, S_ROWS, 256), F32),
            VMEM((DP, MP, 16, hid), F32),
            VMEM((DP, MP, 48, D), BF16),
            VMEM((MP, dp1, PW, hid), BF16),
            VMEM((MP, dp1, PW, hid), BF16),
            VMEM((MP - 1, PW, hid), BF16),
            VMEM((MP - 1, PW, hid), BF16),
            VMEM((MP, dp1, PE, D), BF16),
            VMEM((MP, dp1, PE, D), BF16),
            VMEM((MP - 1, PE, D), BF16),
            VMEM((MP - 1, PE, D), BF16),
            VMEM((DP, MP, 8, LANE), F32),
            VMEM((2, hid // 2, D), BF16),
            VMEM((2, C_ROWS // 2 + 16, 256), BF16),
            VMEM((2, E_ROWS // 2, D), BF16),
            dma((22,)),
            dma((MP - 1, SLOTS)),
            dma((MP, NP)),
            dma((MP - 1, 4)),
            dma((MP, 4)),
            dma((MP - 1, G * pair - 1 or 1, 4)),
            dma((MP, G * pair, 4)),
            dma((MP - 1,)),
            dma((MP,)),
            dma((MP - 1, 3)),
            dma((MP, 3)),
            dma((dp1, 3)),
            dma((DP, 3)),
            dma((MP, dp1)),
            dma((MP, dp1)),
            dma((MP - 1,)),
            dma((MP - 1,)),
            dma((MP, dp1)),
            dma((MP, dp1)),
            dma((MP - 1,)),
            dma((MP - 1,)),
            dma((dp1, 2)),
            dma((DP, 2)),
            dma((MP - 1,)),
            dma((MP,)),
            dma((DP * MP - 1,)),
            dma((DP, MP)),
            dma((3, 3)),
            dma((3, 3)),
        ],
        compiler_params=pltpu.CompilerParams(
            collective_id=0, has_side_effects=True, vmem_limit_bytes=63 << 20
        ),
    )(labels, partner, sca, shi, class_weight, patches, *states)


def finish_kernel(groups, *refs):
    (info, *grads_in), refs = refs[:10], refs[10:]
    states, refs = refs[:28], refs[28:]
    (losses, norm), refs = refs[:2], refs[2:]
    outs, refs = refs[:28], refs[28:]
    grads_held, refs = refs[:9], refs[9:]
    held, refs = refs[:28], refs[28:]
    new, (load, load_grad, save) = refs[:28], refs[28:]
    first = [pltpu.make_async_copy(a, b, load_grad.at[k]) for k, (a, b) in enumerate(zip(grads_in, grads_held, strict=True))]
    loads = [pltpu.make_async_copy(flat(a), b, load.at[k]) for k, (a, b) in enumerate(zip(states, held, strict=True))]
    saves = [pltpu.make_async_copy(a, flat(b), save.at[k]) for k, (a, b) in enumerate(zip(new, outs, strict=True))]
    for c in first:
        c.start()
    for k in (3, 2, 0, 4, 1, 5, 6):
        for j in range(4):
            loads[7 * j + k].start()
    losses[...] = info[0:1, 0:2]
    norm[...] = info[0:1, 2:3]
    scaled = info[0:1, 3:4]
    g_w, g_e, g_mix, g_shr, g_cls, g_vec, sum_s, sum_c, sum_e = grads_held
    for c in first:
        c.wait()
    wide = held[5].shape[1]
    ncls = held[4].shape[1]
    er = held[0].shape[0]
    all_rows = slice(None)

    bias = jnp.concatenate([g_vec[11 + k : 12 + k, :] for k in range(D // LANE)], axis=1)
    work = (
        (3, all_rows, lambda: g_shr[...], lambda: sum_s[...]),
        (2, slice(0, D), lambda: g_w[0:D, :], lambda: sum_e[E_EXP : E_EXP + D, :]),
        (2, slice(D, D + 1), lambda: bias, lambda: sum_e[E_EXP + D : E_EXP + D + 1, :]),
        (0, all_rows, lambda: g_e[0:er, :], lambda: sum_e[E_EMB : E_EMB + er, :]),
        (4, all_rows, lambda: g_cls[0 : D + 1, 0:ncls], lambda: sum_c[C_CLS : C_CLS + D + 1, 0:ncls]),
        (1, all_rows, lambda: g_mix[0:PATCHES, 0 : PATCHES + 1], lambda: sum_c[C_MIX : C_MIX + PATCHES, 0 : PATCHES + 1]),
        (5, all_rows, lambda: g_vec[0:5, 0:wide], lambda: sum_c[C_VEC : C_VEC + 5, 0:wide]),
        (6, all_rows, lambda: g_vec[5:10, 0:wide], lambda: sum_c[C_VEC + 8 : C_VEC + 13, 0:wide]),
    )
    for n, (k, r, gradient, total) in enumerate(work):
        if n == 0 or work[n - 1][0] != k:
            for j in range(4):
                loads[7 * j + k].wait()
        weight, one, two, outer = (held[7 * j + k] for j in range(4))
        update, mean, square, velocity = (new[7 * j + k] for j in range(4))
        grad = gradient() * scaled
        mean[r, :] = beta_one * one[r, :] + (1.0 - beta_one) * grad
        square[r, :] = beta_two * two[r, :] + (1.0 - beta_two) * grad * grad
        average = total() * (1.0 / groups)
        moving = outer_momentum * outer[r, :] + average
        velocity[r, :] = moving
        update[r, :] = weight[r, :] - outer_rate * (average + outer_momentum * moving)
        if n + 1 == len(work) or work[n + 1][0] != k:
            for j in range(4):
                saves[7 * j + k].start()
    for c in saves:
        c.wait()


def finish(G, info, grads, shapes, states, out_shapes):
    dma = pltpu.SemaphoreType.DMA
    vm = pl.BlockSpec(memory_space=VMEM)
    hbm = pl.BlockSpec(memory_space=pl.ANY)
    return pl.pallas_call(
        functools.partial(finish_kernel, G),
        out_shape=tuple(jax.ShapeDtypeStruct(shape, F32) for shape in ((1, 2), (1, 1), *out_shapes)),
        in_specs=[vm] + [hbm] * 37,
        out_specs=(vm,) * 2 + (hbm,) * 28,
        scratch_shapes=[VMEM(a.shape, F32) for a in grads]
        + [VMEM(shape, F32) for shape in shapes] * 8
        + [dma((28,)), dma((9,)), dma((28,))],
        compiler_params=pltpu.CompilerParams(vmem_limit_bytes=62 << 20),
    )(info, *grads, *states)


def thin(a):
    return jnp.swapaxes(a, 0, 1)


def per_device(
    G, DP, MP,
    patches, labels, partner, class_weight,
    embedding, mixing, expand, shrink, classifier, scales, shifts, *state,
):
    weights = (embedding, thin(mixing), thin(expand), shrink[0], classifier, scales, shifts)

    def moments(a):
        return (a[0][0], thin(a[1][0]), thin(a[2][0]), a[3][0, 0], thin(a[4]), thin(a[5]), thin(a[6]))

    firsts, seconds = moments(state[0:7]), moments(state[7:14])
    o = state[14:21]
    outers = (o[0], thin(o[1]), thin(o[2]), o[3][0], o[4], o[5], o[6])
    shapes = tuple((a.shape[0], a.shape[-1]) for a in weights)
    *grads, info = local_step(
        G, DP, MP, shapes, labels[0], partner[0], scales, shifts, class_weight.reshape(1, -1),
        jnp.swapaxes(patches[0], 1, 2), (*weights, *firsts, *seconds),
    )
    out_shapes = tuple(a.shape for a in (*weights, *firsts, *seconds, *outers))
    losses, norm, *done = finish(G, info, grads, shapes, (*weights, *firsts, *seconds, *outers), out_shapes)
    updates, means, squares, velocities = (list(done[7 * k : 7 * k + 7]) for k in range(4))

    def whole(a):
        return (a[0], thin(a[1]), thin(a[2]), a[3][None], a[4], a[5], a[6])

    def by_group(a):
        return (a[0][None], thin(a[1])[None], thin(a[2])[None], a[3][None, None], thin(a[4]), thin(a[5]), thin(a[6]))

    return (
        losses, norm[0],
        *whole(updates), *by_group(means), *by_group(squares), *whole(velocities),
    )


WEIGHT_SPECS = (
    P("mp", None),
    P(),
    P(None, None, "mp"),
    P(None, "mp", None),
    P(None, "mp"),
    P(None, "mp"),
    P(None, "mp"),
)
STATE_SPECS = (
    P("group", "mp", None),
    P("group", None, None, None),
    P("group", None, None, "mp"),
    P("group", None, "mp", None),
    P("group", None, "mp"),
    P("group", None, "mp"),
    P("group", None, "mp"),
)


def solution(mesh):
    G, DP, MP = mesh.shape["group"], mesh.shape["dp"], mesh.shape["mp"]
    return jax.shard_map(
        functools.partial(per_device, G, DP, MP),
        mesh=mesh,
        in_specs=(
            P("group", "dp", None, "mp"),
            P("group", "dp"),
            P("group", "dp"),
            P(),
            *WEIGHT_SPECS,
            *STATE_SPECS,
            *STATE_SPECS,
            *WEIGHT_SPECS,
        ),
        out_specs=(
            P("group", None),
            P("group"),
            *WEIGHT_SPECS,
            *STATE_SPECS,
            *STATE_SPECS,
            *WEIGHT_SPECS,
        ),
        check_vma=False,
    )
```

time: 215 us -> 181 us (0.84)
  Pallas kernels: 214 us -> 179 us
    pallas_call x1 -> x0, Pallas kernels: 78.5 us -> none  [gradient_sums(): pl.pallas_call(functools.partial(sum_kernel, G, DP, MP), out_shape=(s((DP...]
    pallas_call x1, Pallas kernels: 126 us -> 171 us  [local_step(): pl.pallas_call(functools.partial(step_kernel, G, DP, MP, NI, ncls), out_s...]
where the time goes in v4:
time: 181 us; the launch traced here: 180 us
  Pallas kernels  179 us (99%)
    pallas_call x1, Pallas kernels, local_step(): pl.pallas_call(functools.partial(step_kernel, G, DP, MP, NI, ncls), out_s...  171 us
    pallas_call x1, Pallas kernels, finish(): pl.pallas_call(functools.partial(finish_kernel, G), out_shape=tuple((jax....  8.75 us

profile of v4, /device:TPU:0, one launch (start us, length us, event | category | flops | bytes accessed | tf_op | source)
XLA Modules:
  0.0 180.3 jit_solution(3098490696286384254)
XLA Ops:
  0.7 170.7 %shard_map.535 = (f32[384,384]{1,0:T(8,128)}, f32[192,384]{1,0:T(8,128)}, f32[224,256]{1,0:T(8,128)}, f32[384,384]{1,0:T(8,128)}, f32[392,256]{1,0:T(8,128)}, /*...) custom-call(s32[48]{0:T(128)} %bitcast.94, ...), custom_call_target="tpu_custom_call" | custom-call | tf_op jit(solution)/shard_map/pallas_call | solution.py:740
  171.4 8.8 %shard_map.536 = (f32[1,2]{1,0:T(1,128)}, f32[1,1]{1,0:T(1,128)}, f32[192,384]{1,0:T(8,128)}, f32[196,1,197]{2,1,0:T(1,128)}, f32[385,1,384]{2,1,0:T(1,128)}, /*...) custom-call(f32[8,128]{1,0:T(8,128)} %get-tuple-element.70.refs_0_, ...), custom_call_target="tpu_custom_call" | custom-call | tf_op jit(solution)/shard_map/pallas_call | solution.py:910

commit v5 on v4

--- a/solution.py
+++ b/solution.py
@@ -35,9 +35,9 @@
 GELU_A = 0.7978845608028654
 GELU_B = GELU_A * 0.044715
 
-S_VEC, S_ROWS = 56, 72
+MIX, MIX16 = 56, 64
 C_CLS, C_MIX, C_VEC, C_ROWS = 0, 392, 592, 608
-E_EXP, E_EMB, E_ROWS = 0, 392, 608
+E_EXP, E_EMB, E_ROWS = 0, 392, 640
 
 
 def dot(a, b, dims=((1,), (0,)), precision=None):
@@ -73,13 +73,11 @@
 
 
 CHUNK = 256
-AHEAD = 2
-SLOTS = AHEAD + 1
+SLOTS = 3
 
 
 def waves_of(pairs):
-    cuts = list(range(0, pairs - 1, 2)) + [pairs - 1, pairs]
-    return list(zip(cuts[:-1], cuts[1:], strict=True))
+    return [(lo, min(lo + 2, pairs)) for lo in range(0, pairs, 2)]
 
 
 def part_rows(rows, DP):
@@ -101,18 +99,19 @@
 def step_kernel(G, DP, MP, NI, ncls, *refs):
     (labels, partner, sca, shi, class_weight, patches), refs = refs[:6], refs[6:]
     states, refs = refs[:21], refs[21:]
-    (g_w, g_e, g_mix, g_shr, g_cls, g_vec, sum_s, sum_c, sum_e, info), refs = refs[:10], refs[10:]
+    (*results, info), refs = refs[:10], refs[10:]
+    (g_w, g_e, g_mix, g_shr, g_cls, g_vec, sum_s, sum_c, sum_e), refs = refs[:9], refs[9:]
     held, refs = list(refs[:17]), refs[17:]
     (
         pv, stage, rows, e_all, w1, w2, wc, small,
-        xs, gp, s0, s1, mx, mi, fi, ep, mm, mt, eye, mbias, vec, b1, cw, asum, s1sum, la, lb,
-        dact, ds2, dh, csum, gw, ge, gm, gmb, gvec,
-        sm, fac, zsm, ysm, yacts, yfac,
+        xs, gp, s0, s1, mx, mi, fi, ep, mm, mt, eye, mbias, vec, b1, cb, cw, asum, s1sum, la, lb,
+        dact, ds2, dh, fit, csum, gw, ge, gm, gmb, gvec,
+        gmix, sm, fac, zsm, zvec, ysm, yvec, yacts, yfac, agw, age,
         ysw, yrw, zsw, zrw, yse, yre, zse, zre, nsq,
         h2s, h2c, h2e,
-        load, rs_send, rs_recv, wz_send, wz_recv, wg_send, wg_recv, sm_send, sm_recv,
+        load, rs_send, rs_recv, wz_send, wz_recv, wp_send, wp_recv, wc_send, wc_recv, sm_send, sm_recv,
         zf_s, zf_r, yf_s, yf_r, yw_s, yw_r, zw_s, zw_r, ye_s, ye_r, ze_s, ze_r, ag_s, ag_r,
-        nm_s, nm_r, nq_s, nq_r, g_s, g_r,
+        nm_s, nm_r, nq_s, nq_r, g_s, g_r, out_sem,
     ) = refs
     late = {7: mx.at[0, 0 : held[0].shape[0], :], 14: mx.at[1, 0 : held[0].shape[0], :]}
     late |= {10: s1.at[0, 0:D, :], 17: s1.at[1, 0:D, :]}
@@ -130,41 +129,41 @@
     er = emb.shape[0]
     NCH = hid_all // CHUNK
     PW, PE = g_w.shape[0] // DP, g_e.shape[0] // DP
-    pair = 2 if DP % 2 == 0 else 1
+
+    stores = []
+
+    def store(k, value):
+        c = pltpu.make_async_copy(value, results[k], out_sem.at[k])
+        c.start()
+        stores.append(c)
 
     loads = [pltpu.make_async_copy(flat(a), b, load.at[k]) for k, (a, b) in enumerate(zip(states, held, strict=True))]
     load_patches = pltpu.make_async_copy(patches, pv, load.at[21])
     loads[0].start()
     loads[2].start()
     load_patches.start()
-    for k in range(21):
-        if k not in (0, 2, *late):
-            loads[k].start()
 
     zpeer = [lax.rem(z + d, MP) for d in range(1, MP)]
-    half = lax.rem(y, pair)
-    plane, plane_far = [], []
-    for e in range(pair):
-        for d in range(G):
-            if d or e:
-                j = lax.rem(g + d, G)
-                h = half if e == 0 else 1 - half
-                plane_far.append(d > 0)
-                plane.append((j, y if e == 0 else y + 1 - 2 * half, j * pair + h, e))
-    place = g * pair + half
-    parts = G * pair
     ypeer = [lax.rem(y + d, DP) for d in range(1, DP)]
     others = [{"mp": lax.rem(z + c, MP), "dp": lax.rem(y + d, DP)} for d in range(DP) for c in range(MP) if c or d]
-    greet(others + [{"group": j, "dp": u} for (j, u, _, _), far in zip(plane, plane_far, strict=True) if far])
-
-    def pieces(t, j):
-        ee, hh, dd = er // G, hid // parts, D // parts
-        return (
-            e_all.at[t, pl.ds(pl.multiple_of(j // pair * ee, 16), ee), :],
-            w1.at[pl.ds(pl.multiple_of(j * dd, 16), dd), pl.ds(pl.multiple_of(t * hid, LANE), hid)],
-            w2.at[pl.ds(pl.multiple_of(t * hid + j * hh, 16), hh), :],
-            wc.at[pl.ds(pl.multiple_of(j * dd, 16), dd), pl.ds(pl.multiple_of(t * cpad, LANE), cpad)],
-        )
+    core, beside = lax.rem(g, 2), y + 1 - 2 * lax.rem(y, 2)
+    near, far = {"group": g + 1 - 2 * core}, {"group": lax.rem(g + 2, G)}
+    plane = [far, {"dp": beside}, {**far, "dp": beside}]
+    greet(others + [near, far, plane[2]])
+
+    def pieces(t, k, x, h, n=1):
+        if k == 0:
+            size = er // 4 * (1 if n == 1 else 2)
+            at = core * (er // 2) + x * (er // 4)
+            return e_all.at[t, pl.ds(pl.multiple_of(at, 16), size), :]
+        size = D // 8 * n
+        at = core * (D // 2) + (x * 2 + h) * (D // 8)
+        if k == 2:
+            return w2.at[pl.ds(pl.multiple_of(t * hid + at, 16), size), :]
+        ref, width = (w1, hid) if k == 1 else (wc, cpad)
+        return ref.at[pl.ds(pl.multiple_of(at, 16), size), pl.ds(pl.multiple_of(t * width, LANE), width)]
+
+    here = (g // 2, lax.rem(y, 2))
 
     started = []
 
@@ -174,25 +173,38 @@
         started.append(c)
 
     def spread(k):
-        part = pieces(z, place)[k]
+        part = pieces(z, k, *here)
         for d, t in enumerate(zpeer):
             go(part, part, wz_send.at[d, k], wz_recv.at[z, k], {"mp": t})
 
     def pass_on(k):
-        for d in range(1, MP):
-            t = lax.rem(z + MP - d, MP)
-            part = pieces(t, place)[k]
-            remote(part, part, wz_send.at[d - 1, k], wz_recv.at[t, k], {"mp": t}).wait_recv()
-            for e, (j, u, _, other) in enumerate(plane):
-                if k or not other:
-                    go(part, part, wg_send.at[d - 1, e, k], wg_recv.at[t, place, k], {"group": j, "dp": u})
+        for d, t in enumerate(zpeer):
+            part = pieces(t, k, *here)
+            remote(part, part, wz_send.at[d, k], wz_recv.at[t, k], {"mp": t}).wait_recv()
+            for e, peer in enumerate(plane[: 1 if k == 0 else 3]):
+                go(part, part, wp_send.at[d, e, k], wp_recv.at[t, e, k], peer)
+
+    def share_out(k):
+        there = ((1 - here[0], here[1]), (here[0], 1 - here[1]), (1 - here[0], 1 - here[1]))
+        for d, t in enumerate(zpeer):
+            for e, peer in enumerate(plane[: 1 if k == 0 else 3]):
+                part = pieces(t, k, *there[e])
+                remote(part, part, wp_send.at[d, e, k], wp_recv.at[t, e, k], peer).wait_recv()
+            part = pieces(t, k, 0, 0, 4)
+            go(part, part, wc_send.at[d, k], wc_recv.at[t, k], near)
 
     def gathered(k):
         for t in zpeer:
-            for j, u, at, other in plane:
-                if k or not other:
-                    part = pieces(t, at)[k]
-                    remote(part, part, wg_send.at[0, 0, k], wg_recv.at[t, at, k], {"group": j, "dp": u}).wait_recv()
+            if k == 0:
+                part = e_all.at[t, pl.ds(pl.multiple_of((1 - core) * (er // 2), 16), er // 2), :]
+            elif k == 2:
+                part = w2.at[pl.ds(pl.multiple_of(t * hid + (1 - core) * (D // 2), 16), D // 2), :]
+            else:
+                ref, width = (w1, hid) if k == 1 else (wc, cpad)
+                part = ref.at[
+                    pl.ds(pl.multiple_of((1 - core) * (D // 2), 16), D // 2), pl.ds(pl.multiple_of(t * width, LANE), width)
+                ]
+            remote(part, part, wc_send.at[0, k], wc_recv.at[t, k], near).wait_recv()
 
     loads[0].wait()
     e_all[z] = emb[...].astype(BF16)
@@ -235,32 +247,46 @@
         slot = lax.rem(p, SLOTS)
         return remote(stage.at[d, slot], rows.at[z, p], rs_send.at[d, slot], rs_recv.at[z, p], {"mp": zpeer[d]})
 
-    def issue(p):
+    def prepare(p):
         for d in range(MP - 1):
             blend_pair(zpeer[d], p, stage, (d, lax.rem(p, SLOTS)))
+
+    def start(p):
+        for d in range(MP - 1):
             send(p, d).start()
 
-    load_patches.wait()
-    issue(0)
-
+    for k in (3, 4, 1):
+        loads[k].start()
+    small[z] = jnp.zeros(small.shape[1:], F32)
+    small[z, 0:5, 0 : D // MP] = sca[...]
+    small[z, 5:10, 0 : D // MP] = shi[...]
+    for k in range(hid // LANE):
+        small[z, 10 + k : 11 + k, :] = rounded(expa[D : D + 1, k * LANE : (k + 1) * LANE])
     loads[3].wait()
     w2[pl.ds(pl.multiple_of(z * hid, 16), hid), :] = shr[...].astype(BF16)
+    spread(2)
     loads[4].wait()
     head = jnp.concatenate([cls[0:D, :], jnp.zeros((D, cpad - ncls), F32)], axis=1)
     wc[:, pl.ds(pl.multiple_of(z * cpad, LANE), cpad)] = head.astype(BF16)
-    spread(2)
     spread(3)
-    small[z] = jnp.zeros(small.shape[1:], F32)
-    small[z, 0:5, 0 : D // MP] = sca[...]
-    small[z, 5:10, 0 : D // MP] = shi[...]
-    small[z, 10:11, :] = rounded(expa[D : D + 1, :])
-    small[z, 11:12, 0:ncls] = rounded(cls[D : D + 1, :])
+    for k in range(cpad // LANE):
+        n = min(LANE, ncls - k * LANE)
+        small[z, 13 + k : 14 + k, 0:n] = rounded(cls[D : D + 1, k * LANE : k * LANE + n])
     for d, t in enumerate(zpeer):
         go(small.at[z], small.at[z], sm_send.at[d], sm_recv.at[z], {"mp": t})
-    for p in range(1, min(AHEAD, NP)):
-        issue(p)
+    load_patches.wait()
+    prepare(0)
+    start(0)
     pass_on(0)
     pass_on(1)
+    if NP > 1:
+        prepare(1)
+        start(1)
+    pass_on(2)
+    pass_on(3)
+    for k in range(5, 21):
+        if k not in late:
+            loads[k].start()
 
     loads[1].wait()
     wide = jnp.concatenate([mixing[...], jnp.zeros((PATCHES, 256 - PATCHES - 1), F32)], axis=1)
@@ -276,6 +302,7 @@
     asum[...] = jnp.zeros_like(asum)
     s1sum[...] = jnp.zeros_like(s1sum)
     csum[...] = jnp.zeros_like(csum)
+    fit[D:, :] = jnp.ones((16, PR), BF16)
     gw[...] = jnp.zeros_like(gw)
     ge[...] = jnp.zeros_like(ge)
     gm[...] = jnp.zeros_like(gm)
@@ -289,13 +316,19 @@
         la[i : i + 1, :] = jnp.full((1, LANE), own, jnp.int32)
         lb[i : i + 1, :] = jnp.full((1, LANE), mate, jnp.int32)
 
+    share_out(0)
+    share_out(1)
+
     for t in zpeer:
         remote(small.at[t], small.at[t], sm_send.at[0], sm_recv.at[t], {"mp": t}).wait_recv()
     full = jnp.zeros((16, D), F32)
     for t in range(MP):
-        block = small[t]
+        block = jnp.concatenate([small[t], jnp.zeros((16, D - LANE), F32)], axis=1)
         full = full + (pltpu.roll(block, t * (D // MP), 1) if t else block)
-        b1[:, t * hid : (t + 1) * hid] = small[t, 10:11, :]
+        for k in range(hid // LANE):
+            b1[:, t * hid + k * LANE : t * hid + (k + 1) * LANE] = small[t, 10 + k : 11 + k, :]
+        for k in range(cpad // LANE):
+            cb[:, t * cpad + k * LANE : t * cpad + (k + 1) * LANE] = small[t, 13 + k : 14 + k, :]
     vec[...] = full
     gathered(0)
     rest_rows = er - LANE
@@ -303,8 +336,8 @@
         ep[t * LANE : (t + 1) * LANE, :] = e_all[t, 0:LANE, :]
         ep[MP * LANE + t * rest_rows : MP * LANE + (t + 1) * rest_rows, :] = e_all[t, LANE:er, :]
     gathered(1)
-    pass_on(2)
-    pass_on(3)
+    share_out(2)
+    share_out(3)
 
     def scale(k):
         return vec[k : k + 1, :]
@@ -313,14 +346,15 @@
         return vec[5 + k : 6 + k, :]
 
     def forward(base, p, carry):
-        @pl.when(p + AHEAD < NP)
+        @pl.when(p + 2 < NP)
         def _():
-            @pl.when(p + AHEAD >= SLOTS)
+            @pl.when(p + 2 >= SLOTS)
             def _():
                 for d in range(MP - 1):
-                    send(p + AHEAD - SLOTS, d).wait_send()
-
-            issue(p + AHEAD)
+                    send(p + 2 - SLOTS, d).wait_send()
+
+            prepare(p + 2)
+            start(p + 2)
 
         q = p - base
         blend_pair(z, p, rows, (z, p))
@@ -364,6 +398,7 @@
             return carry
 
         lax.fori_loop(0, NCH, chunk, 0)
+
         return carry
 
     def class_head():
@@ -371,12 +406,11 @@
         outsum = three[0:16] + three[16:32] + three[32:48] + PATCHES * shift(2)
         stream2 = s1sum[...] + scale(3) * outsum
         pooled = (scale(4) * (stream2 * (1.0 / PATCHES)) + shift(4)).astype(BF16)
-        bias = jnp.concatenate([small[t, 11:12, 0:cpad] for t in range(MP)], axis=1)
         lane = lax.broadcasted_iota(jnp.int32, (16, cpad * MP), 1)
         inside = lax.rem(lane, cpad)
         valid = inside < ncls
         class_id = (lane // cpad) * ncls + inside
-        logits = jnp.where(valid, dot(pooled, wc[...]) + bias, -1e30)
+        logits = jnp.where(valid, dot(pooled, wc[...]) + cb[...], -1e30)
         hot_a = jnp.where(valid & (class_id == la[:, 0:1]), 1.0, 0.0)
         hot_b = jnp.where(valid & (class_id == lb[:, 0:1]), 1.0, 0.0)
         weight_a = mix_share * jnp.sum(hot_a * cw[...], axis=1, keepdims=True)
@@ -415,17 +449,26 @@
 
         return last
 
+    def turn_input(q):
+        fit[0:D, :] = jnp.transpose(fi[q])
+
+    def hidden_gradient(q, p, cols):
+        for b in range(2):
+            r = slice(b * ROWS, (b + 1) * ROWS)
+            dh[r, cols] = (gp[q, r, cols] * dact[pl.ds(2 * p + b, 1), cols]).astype(BF16)
+
+    def backward_columns(q, p, cols):
+        hidden_gradient(q, p, cols)
+        grad = dot(fit[...], dh[:, cols])
+        gw[0:D, cols] += grad[0:D]
+        csum[0:1, cols] += grad[D : D + 1]
+
     def backward_hidden(base, p):
         q = p - base
+        turn_input(q)
 
         def chunk(c, carry):
-            cols = pl.ds(pl.multiple_of(c * CHUNK, CHUNK), CHUNK)
-            for b in range(2):
-                r = slice(b * ROWS, (b + 1) * ROWS)
-                dh[r, cols] = (gp[q, r, cols] * dact[pl.ds(2 * p + b, 1), cols]).astype(BF16)
-            value = dh[:, cols]
-            csum[0:1, cols] += jnp.sum(value.astype(F32), axis=0, keepdims=True)
-            gw[0:D, cols] += dot(fi[q], value, ((0,), (0,)))
+            backward_columns(q, p, pl.ds(pl.multiple_of(c * CHUNK, CHUNK), CHUNK))
             return carry
 
         lax.fori_loop(0, NCH, chunk, 0)
@@ -478,15 +521,22 @@
     yacts[y, z] = asum[:, columns(z)]
     yfac[y, z] = fac[z]
     for d, v in enumerate(zpeer):
-        go(asum.at[:, columns(v)], yacts.at[y, z], zf_s.at[d, 0], zf_r.at[z, 0], {"mp": v})
-        go(fac.at[v], yfac.at[y, z], zf_s.at[d, 1], zf_r.at[z, 1], {"mp": v})
+        go(asum.at[:, columns(v)], yacts.at[y, z], zf_s.at[d, 2], zf_r.at[z, 2], {"mp": v})
+        go(fac.at[v], yfac.at[y, z], zf_s.at[d, 3], zf_r.at[z, 3], {"mp": v})
     order = zpeer + [z]
-    backward_hidden(lo, lo)
+    for p in range(lo, hi - 1):
+        backward_hidden(lo, p)
+    turn_input(hi - 1 - lo)
     for i, t in enumerate(order):
+        backward_columns(hi - 1 - lo, hi - 1, columns(t))
         for d, u in enumerate(ypeer):
             ysw[i, d] = gw[part(u, PW), columns(t)].astype(BF16)
             go(ysw.at[i, d], yrw.at[t, d], yw_s.at[i, d], yw_r.at[t, d], {"dp": u})
-    backward_rest(lo, lo)
+    backward_rest(lo, hi - 1)
+    for p in range(lo, hi - 1):
+        for t in range(MP):
+            hidden_gradient(p - lo, p, columns(t))
+        backward_rest(lo, p)
     for i, t in enumerate(order):
         for d, u in enumerate(ypeer):
             yse[i, d] = ge[t, part(u, PE), :].astype(BF16)
@@ -505,29 +555,28 @@
     own = D // MP
     lane = lax.broadcasted_iota(jnp.int32, (16, LANE), 1)
     for t in range(MP):
-        n = min(S_VEC, ROWS - t * S_VEC)
-        sm[t, 0:n, :] = grad[t * S_VEC : t * S_VEC + n]
-        if n < S_VEC:
-            sm[t, n:S_VEC, :] = jnp.zeros((S_VEC - n, 256), F32)
+        n = min(MIX, ROWS - t * MIX)
+        gmix[t, 0:n, :] = grad[t * MIX : t * MIX + n]
+        gmix[t, n:, :] = jnp.zeros((MIX16 - n, 256), F32)
+        sm[t] = gmix[t].astype(BF16)
         vector = gvec[...]
         if t:
             vector = pltpu.roll(vector, D - t * own, 1)
-        sm[t, S_VEC:S_ROWS, 0:LANE] = jnp.where(lane < own, vector[:, 0:LANE], 0.0)
-        sm[t, S_VEC:S_ROWS, LANE:] = jnp.zeros((16, LANE), F32)
-        sm[t, S_VEC + 10 : S_VEC + 11, 0:LANE] = gvec[10:11, 0:LANE]
+        zvec[z, t] = jnp.where(lane < own, vector[:, 0:LANE], 0.0)
+        zvec[z, t, 10:11, :] = gvec[10:11, 0:LANE]
         for k in range(hid // LANE):
             at = t * hid + k * LANE
-            sm[t, S_VEC + 11 + k : S_VEC + 12 + k, 0:LANE] = csum[:, at : at + LANE]
-    zsm[z] = sm[z]
+            zvec[z, t, 11 + k : 12 + k, :] = csum[:, at : at + LANE]
     for d, v in enumerate(zpeer):
-        go(sm.at[v], zsm.at[z], zf_s.at[d, 2], zf_r.at[z, 2], {"mp": v})
+        go(sm.at[v], zsm.at[z], zf_s.at[d, 0], zf_r.at[z, 0], {"mp": v})
+        go(zvec.at[z, v], zvec.at[z, v], zf_s.at[d, 1], zf_r.at[z, 1], {"mp": v})
 
     for v in zpeer:
-        arrived(yacts.at[y, v], zf_r.at[v, 0], {"mp": v})
-        arrived(yfac.at[y, v], zf_r.at[v, 1], {"mp": v})
+        arrived(yacts.at[y, v], zf_r.at[v, 2], {"mp": v})
+        arrived(yfac.at[y, v], zf_r.at[v, 3], {"mp": v})
     for d, u in enumerate(ypeer):
-        go(yacts.at[y], yacts.at[y], yf_s.at[d, 1], yf_r.at[y, 1], {"dp": u})
-        go(yfac.at[y], yfac.at[y], yf_s.at[d, 2], yf_r.at[y, 2], {"dp": u})
+        go(yacts.at[y], yacts.at[y], yf_s.at[d, 2], yf_r.at[y, 2], {"dp": u})
+        go(yfac.at[y], yfac.at[y], yf_s.at[d, 3], yf_r.at[y, 3], {"dp": u})
 
     def from_dp(first, received, sems, send, out, out_sems, z_sems, n):
         for i, t in enumerate(order):
@@ -540,51 +589,50 @@
                 go(send.at[i], out.at[i], out_sems.at[i], z_sems.at[i], {"mp": t})
         return value
 
-    g_w[part(y, PW), :] = from_dp(lambda t: gw[part(y, PW), columns(t)], yrw, yw_r, zsw, zrw, zw_s, zw_r, PW)
-
+    own_w = from_dp(lambda t: gw[part(y, PW), columns(t)], yrw, yw_r, zsw, zrw, zw_s, zw_r, PW)
+
+    mixed = gmix[z, 0:MIX, :]
     for v in zpeer:
-        arrived(zsm.at[v], zf_r.at[v, 2], {"mp": v})
-    summed = zsm[0]
+        arrived(zsm.at[v], zf_r.at[v, 0], {"mp": v})
+        arrived(zvec.at[v, z], zf_r.at[v, 1], {"mp": v})
+        mixed = mixed + zsm[v, 0:MIX, :].astype(F32)
+    vector = zvec[0, z]
     for v in range(1, MP):
-        summed = summed + zsm[v]
-    ysm[y] = summed
+        vector = vector + zvec[v, z]
+    ysm[y] = mixed
+    yvec[y] = vector
     for d, u in enumerate(ypeer):
         go(ysm.at[y], ysm.at[y], yf_s.at[d, 0], yf_r.at[y, 0], {"dp": u})
-
-    g_e[part(y, PE), :] = from_dp(lambda t: ge[t, part(y, PE), :], yre, ye_r, zse, zre, ze_s, ze_r, PE)
-
-    shared = []
-
-    def from_mp(total, received, sems, n, k):
-        value = total[part(y, n), :]
+        go(yvec.at[y], yvec.at[y], yf_s.at[d, 1], yf_r.at[y, 1], {"dp": u})
+
+    own_e = from_dp(lambda t: ge[t, part(y, PE), :], yre, ye_r, zse, zre, ze_s, ze_r, PE)
+
+    def from_mp(own_sum, received, sems, gathered, k):
+        value = own_sum
         for i in range(MP - 1):
             arrived(received.at[i], sems.at[i], {"mp": zpeer[i]})
             value = value + received[i].astype(F32)
-        total[part(y, n), :] = value
+        gathered[y] = value.astype(BF16)
         for d, u in enumerate(ypeer):
-            c = remote(total.at[part(y, n), :], total.at[part(y, n), :], ag_s.at[d, k], ag_r.at[y, k], {"dp": u})
-            c.start()
-            shared.append(c)
-        return value
+            go(gathered.at[y], gathered.at[y], ag_s.at[d, k], ag_r.at[y, k], {"dp": u})
+        return rounded(value)
 
     def squares(v):
         return jnp.sum(jnp.sum(v * v, axis=0, keepdims=True), axis=1, keepdims=True)
 
-    mine = squares(from_mp(g_w, zrw, zw_r, PW, 0))
+    mine = squares(from_mp(own_w, zrw, zw_r, agw, 0))
 
     for u in ypeer:
         arrived(ysm.at[u], yf_r.at[u, 0], {"dp": u})
-    summed = ysm[0]
+        arrived(yvec.at[u], yf_r.at[u, 1], {"dp": u})
+    mixed, vector = ysm[0], yvec[0]
     for u in range(1, DP):
-        summed = summed + ysm[u]
-    g_mix[part(z, S_VEC), :] = summed[0:S_VEC]
-    for d, v in enumerate(zpeer):
-        go(g_mix.at[part(z, S_VEC), :], g_mix.at[part(z, S_VEC), :], nm_s.at[d], nm_r.at[z], {"mp": v})
-    vector = summed[S_VEC:S_ROWS, 0:LANE]
+        mixed, vector = mixed + ysm[u], vector + yvec[u]
+    g_mix[part(z, MIX), :] = mixed
 
     for u in ypeer:
-        arrived(yacts.at[u], yf_r.at[u, 1], {"dp": u})
-        arrived(yfac.at[u], yf_r.at[u, 2], {"dp": u})
+        arrived(yacts.at[u], yf_r.at[u, 2], {"dp": u})
+        arrived(yfac.at[u], yf_r.at[u, 3], {"dp": u})
     n = 16 * MP
     grad_shr = jnp.zeros((hid, D), F32)
     grad_cls = jnp.zeros((D, cpad), F32)
@@ -601,18 +649,22 @@
     g_shr[...] = grad_shr
     g_cls[0:D, :] = grad_cls
     g_cls[D:, :] = jnp.concatenate([cls_bias, jnp.zeros((g_cls.shape[0] - D - 1, cpad), F32)], axis=0)
-    once = squares(grad_shr) + squares(grad_cls) + squares(cls_bias) + squares(summed[0:S_VEC])
+    once = squares(grad_shr) + squares(grad_cls) + squares(cls_bias) + squares(mixed)
     once = once + squares(vector[0:10]) + squares(vector[11 : 11 + hid // LANE])
 
-    mine = mine + squares(from_mp(g_e, zre, ze_r, PE, 1))
+    mine = mine + squares(from_mp(own_e, zre, ze_r, age, 1))
     nsq[y, z] = jnp.broadcast_to(mine + jnp.where(y == 0, once, 0.0), (8, LANE))
     for k, peer in enumerate(others):
         go(nsq.at[y, z], nsq.at[y, z], nq_s.at[k], nq_r.at[y, z], peer)
+    for d, v in enumerate(zpeer):
+        go(g_mix.at[part(z, MIX), :], g_mix.at[part(z, MIX), :], nm_s.at[d], nm_r.at[z], {"mp": v})
+    store(3, g_shr)
+    store(4, g_cls)
+    g_vec[...] = vector
+    store(5, g_vec)
     for k in range(4, 21):
         if k != 4:
             loads[k].wait()
-    for v in zpeer:
-        arrived(g_mix.at[part(v, S_VEC), :], nm_r.at[v], {"mp": v})
     for peer in others:
         arrived(nsq.at[peer["dp"], peer["mp"]], nq_r.at[peer["dp"], peer["mp"]], peer)
     square = jnp.zeros((1, 1), F32)
@@ -633,10 +685,6 @@
     (emb1, mixing1, expa1, shr1, cls1, sca1, shi1) = held[7:14]
     (emb2, mixing2, expa2, shr2, cls2, sca2, shi2) = held[14:21]
     wide = sca_w.shape[1]
-    gstep = [g + 1 - 2 * lax.rem(g, 2), lax.rem(g + 2, 4)]
-    near, far = {"group": gstep[0]}, {"group": gstep[1]}
-    core = lax.rem(g, 2)
-
     def halves(ref, k):
         n = ref.shape[0] // 2
         return ref.at[pl.ds(pl.multiple_of(k * n, 8), n), :]
@@ -659,6 +707,12 @@
     def first_step(k, moved, out):
         go(moved.at[1 - core], halves(out, 1 - core), g_s.at[k, 0], g_r.at[k, 0], near)
 
+    side = lax.rem(y, 2)
+
+    def some(ref, k, which):
+        n = ref.shape[1] // 2
+        return ref.at[k, pl.ds(pl.multiple_of(which * n, 16), n), :]
+
     def second_step(k, moved, out, pairs):
         arrived(halves(out, core), g_r.at[k, 0], near)
         n = moved.shape[1]
@@ -667,34 +721,31 @@
         if pairs.shape[1] > n:
             value = value[fine : fine + 16]
             pairs[0, n:] = (value - rounded(value)).astype(BF16)
-        go(pairs.at[0], pairs.at[1], g_s.at[k, 1], g_r.at[k, 1], far)
+        go(some(pairs, 0, side), some(pairs, 1, side), g_s.at[k, 1], g_r.at[k, 1], far)
+
+    def hand_on(k, pairs):
+        arrived(some(pairs, 1, side), g_r.at[k, 1], far)
+        go(some(pairs, 1, side), some(pairs, 1, side), g_s.at[k, 2], g_r.at[k, 2], {"dp": beside})
 
     def third_step(k, pairs, out):
-        arrived(pairs.at[1], g_r.at[k, 1], far)
+        arrived(some(pairs, 1, 1 - side), g_r.at[k, 2], {"dp": beside})
         n = out.shape[0] // 2
         total = pairs[0].astype(F32) + pairs[1].astype(F32)
         out[part(core, n), :] = total[0:n]
         if pairs.shape[1] > n:
             out[pl.ds(pl.multiple_of(core * n + fine, 8), 16), :] = total[fine : fine + 16] + total[n:]
-        go(halves(out, core), halves(out, core), g_s.at[k, 2], g_r.at[k, 2], near)
+        go(halves(out, core), halves(out, core), g_s.at[k, 3], g_r.at[k, 3], near)
 
     put(mvs, 0, adamw(shr[...], g_shr[...] * scaled, shr1[...], shr2[...], matrix_rate))
     first_step(0, mvs, sum_s)
-    mvc[...] = jnp.zeros(mvc.shape, F32)
-    put(mvc, C_CLS, adamw(cls[...], g_cls[0 : D + 1, 0:ncls] * scaled, cls1[...], cls2[...], head_rate))
-    put(
-        mvc, C_MIX,
-        adamw(mixing[...], g_mix[0:PATCHES, 0 : PATCHES + 1] * scaled, mixing1[...], mixing2[...], matrix_rate),
-    )
-    g_vec[...] = vector
-    for k, (w, one, two) in enumerate(((sca_w, sca1, sca2), (shi_w, shi1, shi2))):
-        value = adamw(w[...], g_vec[5 * k : 5 * k + 5, 0:wide] * scaled, one[...], two[...], vector_rate)
-        put(mvc, C_VEC + 8 * k, value)
-    first_step(1, mvc, sum_c)
-    second_step(0, mvs, sum_s, h2s)
     for u in ypeer:
-        arrived(g_w.at[part(u, PW), :], ag_r.at[u, 0], {"dp": u})
-        arrived(g_e.at[part(u, PE), :], ag_r.at[u, 1], {"dp": u})
+        arrived(agw.at[u], ag_r.at[u, 0], {"dp": u})
+        arrived(age.at[u], ag_r.at[u, 1], {"dp": u})
+    for u in range(DP):
+        g_w[u * PW : (u + 1) * PW, :] = agw[u].astype(F32)
+        g_e[u * PE : (u + 1) * PE, :] = age[u].astype(F32)
+    store(0, g_w)
+    store(1, g_e)
     bias = jnp.concatenate([g_vec[11 + k : 12 + k, :] for k in range(hid // LANE)], axis=1)
     last_row = slice(D, D + 1)
     mve[...] = jnp.zeros(mve.shape, F32)
@@ -702,13 +753,34 @@
     put(mve, E_EXP + D, adamw(expa[last_row, :], bias * scaled, expa1[last_row, :], expa2[last_row, :], matrix_rate))
     put(mve, E_EMB, adamw(emb[...], g_e[0:er, :] * scaled, emb1[...], emb2[...], matrix_rate))
     first_step(2, mve, sum_e)
+    second_step(0, mvs, sum_s, h2s)
+    for v in zpeer:
+        arrived(g_mix.at[part(v, MIX), :], nm_r.at[v], {"mp": v})
+    store(2, g_mix)
+    mvc[...] = jnp.zeros(mvc.shape, F32)
+    put(mvc, C_CLS, adamw(cls[...], g_cls[0 : D + 1, 0:ncls] * scaled, cls1[...], cls2[...], head_rate))
+    put(
+        mvc, C_MIX,
+        adamw(mixing[...], g_mix[0:PATCHES, 0 : PATCHES + 1] * scaled, mixing1[...], mixing2[...], matrix_rate),
+    )
+    for k, (w, one, two) in enumerate(((sca_w, sca1, sca2), (shi_w, shi1, shi2))):
+        value = adamw(w[...], g_vec[5 * k : 5 * k + 5, 0:wide] * scaled, one[...], two[...], vector_rate)
+        put(mvc, C_VEC + 8 * k, value)
+    first_step(1, mvc, sum_c)
+    second_step(2, mve, sum_e, h2e)
+    hand_on(0, h2s)
     second_step(1, mvc, sum_c, h2c)
-    second_step(2, mve, sum_e, h2e)
+    hand_on(2, h2e)
     third_step(0, h2s, sum_s)
+    hand_on(1, h2c)
+    third_step(2, h2e, sum_e)
+    arrived(halves(sum_s, 1 - core), g_r.at[0, 3], near)
+    store(6, sum_s)
     third_step(1, h2c, sum_c)
-    third_step(2, h2e, sum_e)
-    for k, out in enumerate((sum_s, sum_c, sum_e)):
-        arrived(halves(out, 1 - core), g_r.at[k, 2], near)
+    arrived(halves(sum_e, 1 - core), g_r.at[2, 3], near)
+    store(8, sum_e)
+    arrived(halves(sum_c, 1 - core), g_r.at[1, 3], near)
+    store(7, sum_c)
 
     def drain(p, carry):
         for d in range(MP - 1):
@@ -716,8 +788,10 @@
         return carry
 
     lax.fori_loop(max(NP - SLOTS, 0), NP, drain, 0)
-    for c in started + shared:
+    for c in started:
         c.wait_send()
+    for c in stores:
+        c.wait()
 
 
 def local_step(G, DP, MP, shapes, labels, partner, sca, shi, class_weight, patches, states):
@@ -729,7 +803,6 @@
     pd = er * MP
     cpad = -(-ncls // LANE) * LANE
     wave = max(hi - lo for lo, hi in waves_of(NP))
-    pair = 2 if DP % 2 == 0 else 1
     dp1 = max(DP - 1, 1)
     PW, PE = part_rows(D, DP), part_rows(er, DP)
     dma = pltpu.SemaphoreType.DMA
@@ -737,23 +810,17 @@
     smem = pl.BlockSpec(memory_space=SMEM)
     hbm = pl.BlockSpec(memory_space=pl.ANY)
     s = jax.ShapeDtypeStruct
+    results = (
+        (DP * PW, D), (DP * PE, D), (MP * MIX, 256), (hid, D), (392, cpad), (16, LANE),
+        (hid, D), (C_ROWS, 256), (E_ROWS, D),
+    )
     return pl.pallas_call(
         functools.partial(step_kernel, G, DP, MP, NI, ncls),
-        out_shape=(
-            s((DP * PW, D), F32),
-            s((DP * PE, D), F32),
-            s((MP * S_VEC, 256), F32),
-            s((hid, D), F32),
-            s((392, cpad), F32),
-            s((16, LANE), F32),
-            s((hid, D), F32),
-            s((C_ROWS, 256), F32),
-            s((E_ROWS, D), F32),
-            s((8, LANE), F32),
-        ),
+        out_shape=(*(s(shape, F32) for shape in results), s((8, LANE), F32)),
         in_specs=[smem, smem, vm, vm, vm] + [hbm] * 22,
-        out_specs=(vm,) * 10,
-        scratch_shapes=[VMEM(shape, F32) for shape in shapes + 2 * (shapes[1:3] + shapes[4:])]
+        out_specs=(hbm,) * 9 + (vm,),
+        scratch_shapes=[VMEM(shape, F32) for shape in results]
+        + [VMEM(shape, F32) for shape in shapes + 2 * (shapes[1:3] + shapes[4:])]
         + [
             VMEM(patches.shape, F32),
             VMEM((MP - 1, SLOTS, 3 * MAIN + 16, LANE), BF16),
@@ -762,7 +829,7 @@
             VMEM((D, hid_all), BF16),
             VMEM((hid_all, D), BF16),
             VMEM((D, cpad * MP), BF16),
-            VMEM((MP, 16, hid), F32),
+            VMEM((MP, 16, LANE), F32),
             VMEM((wave, PR, pd), BF16),
             VMEM((wave, PR, hid_all), F32),
             VMEM((wave, PR, D), F32),
@@ -778,6 +845,7 @@
             VMEM((16, D), F32),
             VMEM((1, hid_all), F32),
             VMEM((1, cpad * MP), F32),
+            VMEM((1, cpad * MP), F32),
             VMEM((16, hid_all), F32),
             VMEM((16, D), F32),
             VMEM((16, LANE), jnp.int32),
@@ -785,18 +853,24 @@
             VMEM((16, hid_all), F32),
             VMEM((16, D), F32),
             VMEM((PR, hid_all), BF16),
+            VMEM((D + 16, PR), BF16),
             VMEM((1, hid_all), F32),
             VMEM((DP * PW, hid_all), F32),
             VMEM((MP, DP * PE, D), F32),
             VMEM((ROWS, ROWS), F32),
             VMEM((ROWS, D), F32),
             VMEM((16, D), F32),
-            VMEM((MP, S_ROWS, 256), F32),
+            VMEM((MP, MIX16, 256), F32),
+            VMEM((MP, MIX16, 256), BF16),
             VMEM((MP, 48, D), BF16),
-            VMEM((MP, S_ROWS, 256), F32),
-            VMEM((DP, S_ROWS, 256), F32),
+            VMEM((MP, MIX16, 256), BF16),
+            VMEM((MP, MP, 16, LANE), F32),
+            VMEM((DP, MIX, 256), F32),
+            VMEM((DP, 16, LANE), F32),
             VMEM((DP, MP, 16, hid), F32),
             VMEM((DP, MP, 48, D), BF16),
+            VMEM((DP, PW, hid), BF16),
+            VMEM((DP, PE, D), BF16),
             VMEM((MP, dp1, PW, hid), BF16),
             VMEM((MP, dp1, PW, hid), BF16),
             VMEM((MP - 1, PW, hid), BF16),
@@ -814,14 +888,16 @@
             dma((MP, NP)),
             dma((MP - 1, 4)),
             dma((MP, 4)),
-            dma((MP - 1, G * pair - 1 or 1, 4)),
-            dma((MP, G * pair, 4)),
+            dma((MP - 1, 3, 4)),
+            dma((MP, 3, 4)),
+            dma((MP - 1, 4)),
+            dma((MP, 4)),
             dma((MP - 1,)),
             dma((MP,)),
-            dma((MP - 1, 3)),
-            dma((MP, 3)),
-            dma((dp1, 3)),
-            dma((DP, 3)),
+            dma((MP - 1, 4)),
+            dma((MP, 4)),
+            dma((dp1, 4)),
+            dma((DP, 4)),
             dma((MP, dp1)),
             dma((MP, dp1)),
             dma((MP - 1,)),
@@ -836,8 +912,9 @@
             dma((MP,)),
             dma((DP * MP - 1,)),
             dma((DP, MP)),
-            dma((3, 3)),
-            dma((3, 3)),
+            dma((3, 4)),
+            dma((3, 4)),
+            dma((9,)),
         ],
         compiler_params=pltpu.CompilerParams(
             collective_id=0, has_side_effects=True, vmem_limit_bytes=63 << 20

time: 181 us -> 172 us (0.950)
  Pallas kernels: 179 us -> 170 us
    pallas_call x1, Pallas kernels: 171 us -> 162 us  [local_step(): pl.pallas_call(functools.partial(step_kernel, G, DP, MP, NI, ncls), out_s...]
where the time goes in v5:
time: 172 us; the launch traced here: 171 us
  Pallas kernels  170 us (99%)
    pallas_call x1, Pallas kernels, local_step(): pl.pallas_call(functools.partial(step_kernel, G, DP, MP, NI, ncls), out_s...  162 us
    pallas_call x1, Pallas kernels, finish(): pl.pallas_call(functools.partial(finish_kernel, G), out_shape=tuple((jax....  8.76 us

profile of v5, /device:TPU:0, one launch (start us, length us, event | category | flops | bytes accessed | tf_op | source)
XLA Modules:
  0.0 171.3 jit_solution(7211182174209427615)
XLA Ops:
  0.7 161.7 %shard_map.535 = (f32[384,384]{1,0:T(8,128)}, f32[192,384]{1,0:T(8,128)}, f32[224,256]{1,0:T(8,128)}, f32[384,384]{1,0:T(8,128)}, f32[392,256]{1,0:T(8,128)}, /*...) custom-call(s32[48]{0:T(128)} %bitcast.94, ...), custom_call_target="tpu_custom_call" | custom-call | tf_op jit(solution)/shard_map/pallas_call | solution.py:817
  162.4 8.8 %shard_map.536 = (f32[1,2]{1,0:T(1,128)}, f32[1,1]{1,0:T(1,128)}, f32[192,384]{1,0:T(8,128)}, f32[196,1,197]{2,1,0:T(1,128)}, f32[385,1,384]{2,1,0:T(1,128)}, /*...) custom-call(f32[8,128]{1,0:T(8,128)} %get-tuple-element.70.refs_0_, ...), custom_call_target="tpu_custom_call" | custom-call | tf_op jit(solution)/shard_map/pallas_call | solution.py:987

commit v6 on v5

--- a/solution.py
+++ b/solution.py
@@ -302,7 +302,7 @@
     asum[...] = jnp.zeros_like(asum)
     s1sum[...] = jnp.zeros_like(s1sum)
     csum[...] = jnp.zeros_like(csum)
-    fit[D:, :] = jnp.ones((16, PR), BF16)
+    fit[:, D:, :] = jnp.ones((fit.shape[0], 16, PR), BF16)
     gw[...] = jnp.zeros_like(gw)
     ge[...] = jnp.zeros_like(ge)
     gm[...] = jnp.zeros_like(gm)
@@ -450,7 +450,7 @@
         return last
 
     def turn_input(q):
-        fit[0:D, :] = jnp.transpose(fi[q])
+        fit[q, 0:D, :] = jnp.transpose(fi[q])
 
     def hidden_gradient(q, p, cols):
         for b in range(2):
@@ -459,7 +459,7 @@
 
     def backward_columns(q, p, cols):
         hidden_gradient(q, p, cols)
-        grad = dot(fit[...], dh[:, cols])
+        grad = dot(fit[q], dh[:, cols])
         gw[0:D, cols] += grad[0:D]
         csum[0:1, cols] += grad[D : D + 1]
 
@@ -524,11 +524,11 @@
         go(asum.at[:, columns(v)], yacts.at[y, z], zf_s.at[d, 2], zf_r.at[z, 2], {"mp": v})
         go(fac.at[v], yfac.at[y, z], zf_s.at[d, 3], zf_r.at[z, 3], {"mp": v})
     order = zpeer + [z]
-    for p in range(lo, hi - 1):
-        backward_hidden(lo, p)
-    turn_input(hi - 1 - lo)
+    for p in range(lo, hi):
+        turn_input(p - lo)
     for i, t in enumerate(order):
-        backward_columns(hi - 1 - lo, hi - 1, columns(t))
+        for p in range(lo, hi):
+            backward_columns(p - lo, p, columns(t))
         for d, u in enumerate(ypeer):
             ysw[i, d] = gw[part(u, PW), columns(t)].astype(BF16)
             go(ysw.at[i, d], yrw.at[t, d], yw_s.at[i, d], yw_r.at[t, d], {"dp": u})
@@ -707,6 +707,7 @@
     def first_step(k, moved, out):
         go(moved.at[1 - core], halves(out, 1 - core), g_s.at[k, 0], g_r.at[k, 0], near)
 
+    split = (True, False, True)
     side = lax.rem(y, 2)
 
     def some(ref, k, which):
@@ -721,14 +722,22 @@
         if pairs.shape[1] > n:
             value = value[fine : fine + 16]
             pairs[0, n:] = (value - rounded(value)).astype(BF16)
-        go(some(pairs, 0, side), some(pairs, 1, side), g_s.at[k, 1], g_r.at[k, 1], far)
+        if split[k]:
+            go(some(pairs, 0, side), some(pairs, 1, side), g_s.at[k, 1], g_r.at[k, 1], far)
+        else:
+            go(pairs.at[0], pairs.at[1], g_s.at[k, 1], g_r.at[k, 1], far)
 
     def hand_on(k, pairs):
+        if not split[k]:
+            return
         arrived(some(pairs, 1, side), g_r.at[k, 1], far)
         go(some(pairs, 1, side), some(pairs, 1, side), g_s.at[k, 2], g_r.at[k, 2], {"dp": beside})
 
     def third_step(k, pairs, out):
-        arrived(some(pairs, 1, 1 - side), g_r.at[k, 2], {"dp": beside})
+        if split[k]:
+            arrived(some(pairs, 1, 1 - side), g_r.at[k, 2], {"dp": beside})
+        else:
+            arrived(pairs.at[1], g_r.at[k, 1], far)
         n = out.shape[0] // 2
         total = pairs[0].astype(F32) + pairs[1].astype(F32)
         out[part(core, n), :] = total[0:n]
@@ -853,7 +862,7 @@
             VMEM((16, hid_all), F32),
             VMEM((16, D), F32),
             VMEM((PR, hid_all), BF16),
-            VMEM((D + 16, PR), BF16),
+            VMEM((wave, D + 16, PR), BF16),
             VMEM((1, hid_all), F32),
             VMEM((DP * PW, hid_all), F32),
             VMEM((MP, DP * PE, D), F32),

time: 172 us -> 169 us (0.983)
  Pallas kernels: 170 us -> 167 us
    pallas_call x1, Pallas kernels: 162 us -> 158 us  [local_step(): pl.pallas_call(functools.partial(step_kernel, G, DP, MP, NI, ncls), out_s...]
where the time goes in v6:
time: 169 us; the launch traced here: 167 us
  Pallas kernels  167 us (99%)
    pallas_call x1, Pallas kernels, local_step(): pl.pallas_call(functools.partial(step_kernel, G, DP, MP, NI, ncls), out_s...  158 us
    pallas_call x1, Pallas kernels, finish(): pl.pallas_call(functools.partial(finish_kernel, G), out_shape=tuple((jax....  8.76 us

profile of v6, /device:TPU:0, one launch (start us, length us, event | category | flops | bytes accessed | tf_op | source)
XLA Modules:
  0.0 167.4 jit_solution(8346676685106612774)
XLA Ops:
  0.7 157.8 %shard_map.535 = (f32[384,384]{1,0:T(8,128)}, f32[192,384]{1,0:T(8,128)}, f32[224,256]{1,0:T(8,128)}, f32[384,384]{1,0:T(8,128)}, f32[392,256]{1,0:T(8,128)}, /*...) custom-call(s32[48]{0:T(128)} %bitcast.94, ...), custom_call_target="tpu_custom_call" | custom-call | tf_op jit(solution)/shard_map/pallas_call | solution.py:826
  158.5 8.8 %shard_map.536 = (f32[1,2]{1,0:T(1,128)}, f32[1,1]{1,0:T(1,128)}, f32[192,384]{1,0:T(8,128)}, f32[196,1,197]{2,1,0:T(1,128)}, f32[385,1,384]{2,1,0:T(1,128)}, /*...) custom-call(f32[8,128]{1,0:T(8,128)} %get-tuple-element.70.refs_0_, ...), custom_call_target="tpu_custom_call" | custom-call | tf_op jit(solution)/shard_map/pallas_call | solution.py:996

commit v7 on v6

--- a/solution.py
+++ b/solution.py
@@ -252,7 +252,7 @@
             blend_pair(zpeer[d], p, stage, (d, lax.rem(p, SLOTS)))
 
     def start(p):
-        for d in range(MP - 1):
+        for d in reversed(range(MP - 1)):
             send(p, d).start()
 
     for k in (3, 4, 1):
@@ -523,7 +523,7 @@
     for d, v in enumerate(zpeer):
         go(asum.at[:, columns(v)], yacts.at[y, z], zf_s.at[d, 2], zf_r.at[z, 2], {"mp": v})
         go(fac.at[v], yfac.at[y, z], zf_s.at[d, 3], zf_r.at[z, 3], {"mp": v})
-    order = zpeer + [z]
+    order = zpeer[::-1] + [z]
     for p in range(lo, hi):
         turn_input(p - lo)
     for i, t in enumerate(order):
@@ -610,7 +610,7 @@
     def from_mp(own_sum, received, sems, gathered, k):
         value = own_sum
         for i in range(MP - 1):
-            arrived(received.at[i], sems.at[i], {"mp": zpeer[i]})
+            arrived(received.at[i], sems.at[i], {"mp": order[i]})
             value = value + received[i].astype(F32)
         gathered[y] = value.astype(BF16)
         for d, u in enumerate(ypeer):

time: 169 us -> 170 us (level)
  Pallas kernels: 167 us -> 169 us
    pallas_call x1, Pallas kernels: 158 us -> 160 us  [local_step(): pl.pallas_call(functools.partial(step_kernel, G, DP, MP, NI, ncls), out_s...]
where the time goes in v7:
time: 170 us
  Pallas kernels  169 us (99%)
    pallas_call x1, Pallas kernels, local_step(): pl.pallas_call(functools.partial(step_kernel, G, DP, MP, NI, ncls), out_s...  160 us
    pallas_call x1, Pallas kernels, finish(): pl.pallas_call(functools.partial(finish_kernel, G), out_shape=tuple((jax....  8.76 us

profile of v7, /device:TPU:0, one launch (start us, length us, event | category | flops | bytes accessed | tf_op | source)
XLA Modules:
  0.0 169.6 jit_solution(7253521193806219313)
XLA Ops:
  0.7 160.0 %shard_map.535 = (f32[384,384]{1,0:T(8,128)}, f32[192,384]{1,0:T(8,128)}, f32[224,256]{1,0:T(8,128)}, f32[384,384]{1,0:T(8,128)}, f32[392,256]{1,0:T(8,128)}, /*...) custom-call(s32[48]{0:T(128)} %bitcast.94, ...), custom_call_target="tpu_custom_call" | custom-call | tf_op jit(solution)/shard_map/pallas_call | solution.py:826
  160.7 8.8 %shard_map.536 = (f32[1,2]{1,0:T(1,128)}, f32[1,1]{1,0:T(1,128)}, f32[192,384]{1,0:T(8,128)}, f32[196,1,197]{2,1,0:T(1,128)}, f32[385,1,384]{2,1,0:T(1,128)}, /*...) custom-call(f32[8,128]{1,0:T(8,128)} %get-tuple-element.70.refs_0_, ...), custom_call_target="tpu_custom_call" | custom-call | tf_op jit(solution)/shard_map/pallas_call | solution.py:996

commit v8 on v6

--- a/solution.py
+++ b/solution.py
@@ -252,7 +252,7 @@
             blend_pair(zpeer[d], p, stage, (d, lax.rem(p, SLOTS)))
 
     def start(p):
-        for d in range(MP - 1):
+        for d in reversed(range(MP - 1)):
             send(p, d).start()
 
     for k in (3, 4, 1):

time: 169 us -> 168 us (level)
  no operation moved by 1% of the time
where the time goes in v8:
time: 168 us; the launch traced here: 167 us
  Pallas kernels  166 us (99%)
    pallas_call x1, Pallas kernels, local_step(): pl.pallas_call(functools.partial(step_kernel, G, DP, MP, NI, ncls), out_s...  157 us
    pallas_call x1, Pallas kernels, finish(): pl.pallas_call(functools.partial(finish_kernel, G), out_shape=tuple((jax....  8.76 us

profile of v8, /device:TPU:0, one launch (start us, length us, event | category | flops | bytes accessed | tf_op | source)
XLA Modules:
  0.0 167.1 jit_solution(5069765572253938718)
XLA Ops:
  0.7 157.5 %shard_map.535 = (f32[384,384]{1,0:T(8,128)}, f32[192,384]{1,0:T(8,128)}, f32[224,256]{1,0:T(8,128)}, f32[384,384]{1,0:T(8,128)}, f32[392,256]{1,0:T(8,128)}, /*...) custom-call(s32[48]{0:T(128)} %bitcast.94, ...), custom_call_target="tpu_custom_call" | custom-call | tf_op jit(solution)/shard_map/pallas_call | solution.py:826
  158.1 8.8 %shard_map.536 = (f32[1,2]{1,0:T(1,128)}, f32[1,1]{1,0:T(1,128)}, f32[192,384]{1,0:T(8,128)}, f32[196,1,197]{2,1,0:T(1,128)}, f32[385,1,384]{2,1,0:T(1,128)}, /*...) custom-call(f32[8,128]{1,0:T(8,128)} %get-tuple-element.70.refs_0_, ...), custom_call_target="tpu_custom_call" | custom-call | tf_op jit(solution)/shard_map/pallas_call | solution.py:996
